TPU v7x, 32 devices: a whole 2x2x4 slice. The times are simulated.
32 devices in a mesh: groups: 2 (over y), users: 4 (over z), mp: 2 (over x), helpers: 2 (over core).
Axes of the slice: x: 2, y: 2, z: 4, core: 2. Of those that a mesh axis runs over, the one named last changes fastest.
Arguments:
- candidates: bfloat16 [32, 128, 1024], P(('groups', 'users', 'helpers')), parts along dimension 0, may hold values from -6 to 6
- block_user: int32 [32], P(('groups', 'users', 'helpers')), parts along dimension 0, may hold values from 0 to 31, as said below
- block_count: int32 [32], P(('groups', 'users', 'helpers')), parts along dimension 0, may hold values from 16 to 32, as said below
- own_map: int32 [64], P('groups'), parts along dimension 0, may hold values from 0 to 31, as said below
- history_key_cache: bfloat16 [64, 512, 1024], P(('groups', 'users'), None, 'mp'), parts along dimension 0, may hold values from -6 to 6
- cache_values: bfloat16 [64, 512, 1024], P(('groups', 'users'), None, 'mp'), parts along dimension 0, may hold values from -64 to 64
- w_query_unit: bfloat16 [2, 1024, 1024], P(None, None, 'mp'), may hold values from -0.1875 to 0.1875
- time_bias: float32 [8, 512], P('mp'), may hold values from -5 to 5
- output_weight: bfloat16 [1024, 1024], P('mp'), may hold values from -0.1875 to 0.1875
- w_score: float32 [1024], P('mp'), may hold values from -0.1875 to 0.1875
Outputs:
- scores: float32 [32, 128], P(('groups', 'users', 'helpers')), parts along dimension 0
There are 2 independent parts, one for each index of `groups`. A program takes and returns all parts, laid end to end along the dimension named above; an argument that names none is the same for every part. Nothing has to cross between parts.
Inputs may be any that keep to these rules, and one draw needn't show every extreme that they name: own_map is a permutation of the users; user u's history is row own_map[u] of the caches. `block_user`: the 2 blocks of one device belong to users whose cache rows, divided by 8, are all different; in every draw one such quotient is that of a block on every device. `block_count`: on every device some block has exactly 32 live candidates.
All inputs are finite; a program needn't handle non-finite values.
Results may differ from a plain program's by a relative error of at most 0.003.
Values may be sent and summed in bfloat16 or wider, within the bound.
No kernel may reach another device: no remote copies, remote signals or barrier semaphores. Data moves between devices by JAX's collectives and lax.ppermute only.
A program may use at most 128 MiB of HBM per device.

v0:
```python
import jax
import jax.numpy as jnp
from jax import lax
from jax.sharding import PartitionSpec as P

EPSILON = 1e-05


def local(
    candidates,
    block_user,
    block_count,
    own_map,
    history_key_cache,
    cache_values,
    w_query_unit,
    time_bias,
    output_weight,
    w_score,
):
    owners = lax.axis_size("users")
    model_index = lax.axis_index("mp")
    blocks, block_rows, model_width = candidates.shape
    users_here = history_key_cache.shape[0]
    local_width = history_key_cache.shape[2]
    heads_here = time_bias.shape[0]
    head_size = local_width // heads_here
    logit_scale = head_size ** (-0.5)
    column_start = model_index * local_width
    w_columns = lax.all_to_all(output_weight, "mp", split_axis=1, concat_axis=0, tiled=True)
    user_range = jnp.arange(own_map.shape[0], dtype=jnp.int32)
    storage = jnp.sum(
        jnp.where(block_user[:, None] == user_range[None, :], own_map[None, :], 0), axis=1
    )
    owner_index = storage // users_here
    local_row = storage % users_here
    selection = (owner_index[None, :] == jnp.arange(owners, dtype=jnp.int32)[:, None]).astype(
        jnp.float32
    )
    outgoing = jnp.einsum(
        "ob,brd->ord",
        selection.astype(jnp.bfloat16),
        candidates,
        preferred_element_type=jnp.float32,
    ).astype(jnp.bfloat16)
    positions = jnp.arange(block_rows, dtype=jnp.int32)
    row_marks = jnp.where(
        positions[None, :] < block_count[:, None], (local_row + 1)[:, None], 0
    ).astype(jnp.float32)
    row_tags = jnp.dot(selection, row_marks, precision=lax.Precision.HIGHEST).astype(jnp.bfloat16)
    position_rows = lax.all_to_all(outgoing, "users", split_axis=0, concat_axis=0, tiled=True)
    tags_in = lax.all_to_all(row_tags, "users", split_axis=0, concat_axis=0, tiled=True)
    item_count = position_rows.shape[1]
    projected = jnp.einsum(
        "snd,kdc->ksnc", position_rows, w_query_unit, preferred_element_type=jnp.float32
    )
    query_bf = jax.nn.silu(projected[0]).astype(jnp.bfloat16)
    unit_gate = jax.nn.silu(projected[1])
    tag_values = tags_in.astype(jnp.float32)
    live_rows = tag_values > 0.5
    slot_user = jnp.clip(jnp.max(tag_values, axis=1) - 1.0, 0.0, users_here - 1.0).astype(jnp.int32)

    def attend(slot_item):
        query_slot, user_slot = slot_item
        key_rows = lax.dynamic_index_in_dim(
            history_key_cache, user_slot, 0, keepdims=False
        ).reshape(-1, heads_here, head_size)
        value_rows = lax.dynamic_index_in_dim(cache_values, user_slot, 0, keepdims=False).reshape(
            -1, heads_here, head_size
        )
        query_heads = query_slot.reshape(item_count, heads_here, head_size)
        logits = (
            jnp.einsum("nhd,lhd->hnl", query_heads, key_rows, preferred_element_type=jnp.float32)
            * logit_scale
            + time_bias[:, None, :]
        )
        weights = jax.nn.silu(logits).astype(jnp.bfloat16)
        mixture = jnp.einsum(
            "hnl,lhd->nhd", weights, value_rows, preferred_element_type=jnp.float32
        )
        return mixture.reshape(item_count, local_width)

    mixture = lax.map(attend, (query_bf, slot_user), batch_size=8)
    totals = lax.psum((jnp.sum(mixture, axis=2), jnp.sum(mixture * mixture, axis=2)), "mp")
    row_mean = totals[0] / model_width
    spread = totals[1] / model_width - row_mean * row_mean
    normed = (mixture - row_mean[..., None]) * lax.rsqrt(spread[..., None] + EPSILON)
    gate_applied_rows = (normed * unit_gate).astype(jnp.bfloat16)
    empty = jnp.zeros((owners, item_count, local_width), jnp.float32)
    shard_piece = lax.all_gather(gate_applied_rows, "mp", axis=2, tiled=True)
    weight_rows = lax.slice_in_dim(w_columns, 0, shard_piece.shape[2], axis=0)
    out_part = empty + jnp.einsum(
        "dfh,hk->dfk", shard_piece, weight_rows, preferred_element_type=jnp.float32
    )
    features = lax.dynamic_slice_in_dim(position_rows, column_start, local_width, 2).astype(
        jnp.float32
    )
    partial_value = jnp.sum(jax.nn.silu(features + out_part) * w_score, axis=2)
    summed_scores = lax.psum(partial_value, "mp")
    summed_scores = jnp.where(live_rows, summed_scores, jnp.zeros_like(summed_scores))
    returned = lax.all_to_all(summed_scores, "users", split_axis=0, concat_axis=0, tiled=True)
    my_scores = jnp.dot(selection.T, returned, precision=lax.Precision.HIGHEST)
    return jnp.pad(my_scores, ((0, 0), (0, block_rows - block_rows)))


def solution(mesh):
    return jax.shard_map(
        local,
        mesh=mesh,
        in_specs=(
            P(("groups", "users", "helpers"), None, None),
            P(("groups", "users", "helpers")),
            P(("groups", "users", "helpers")),
            P("groups"),
            P(("groups", "users"), None, "mp"),
            P(("groups", "users"), None, "mp"),
            P(None, None, "mp"),
            P("mp", None),
            P("mp", None),
            P("mp"),
        ),
        out_specs=P(("groups", "users", "helpers"), None),
        check_vma=False,
    )
```

profile of v0, /device:TPU:0, one launch (start us, length us, event | category | flops | bytes accessed | tf_op | source)
XLA Modules:
  0.0 121.8 jit_solution(206468200354092284)
XLA Ops:
  6.5 0.0 copy-start
  6.5 1.0 fusion.18
  7.6 0.9 fusion.10
  8.5 0.6 copy.46
  9.1 6.3 %all-to-all-start = ((bf16[4,1,128]{2,1,0:T(2,128)(2,1)}), bf16[4,1,128]{2,1,0:T(2,128)(2,1)S(1)}, u32[]{:S(2)}, u32[]{:S(2)}) async-start(bf16[4,1,128]{2,1,0:T(2,128)(2,1)} %copy.46), calls=%async_computation | async-start | bytes 4096 | tf_op jit(solution)/shard_map/all_to_all | solution.py:52
  15.4 2.0 %convolution_convert_fusion = bf16[4,128,1024]{2,0,1:T(4,128)(2,1)S(1)} fusion(bf16[2,128,1024]{2,1,0:T(8,128)(2,1)} %param.10, s32[2]{0:T(128)S(1)} %get-tuple-element.12), kind=kOutput, calls=%fused_computation.8 | convolution fusion | flops 2621464 | bytes 1572872 | tf_op jit(solution)/shard_map/ob,brd->ord/dot_general | solution.py:40
  17.4 1.3 %copy.49 = bf16[4,128,1024]{2,1,0:T(8,128)(2,1)} copy(bf16[4,128,1024]{2,0,1:T(4,128)(2,1)S(1)} %convolution_convert_fusion) | data formatting | bytes 2097152 | tf_op jit(solution)/shard_map/convert_element_type | solution.py:45
  18.7 2.1 %all-to-all-done = bf16[4,1,128]{2,1,0:T(2,128)(2,1)S(1)} async-done(((bf16[4,1,128]{2,1,0:T(2,128)(2,1)}), bf16[4,1,128]{2,1,0:T(2,128)(2,1)S(1)}, u32[]{:S(2)}, u32[]{:S(2)}) %all-to-all-start) | async-done | bytes 1056 | tf_op jit(solution)/shard_map/all_to_all | solution.py:52
  20.8 3.5 %all-to-all-start.1 = ((bf16[4,128,1024]{2,1,0:T(8,128)(2,1)}), bf16[4,128,1024]{2,1,0:T(8,128)(2,1)S(1)}, u32[]{:S(2)}, u32[]{:S(2)}) async-start(bf16[4,128,1024]{2,1,0:T(8,128)(2,1)} %copy.49), calls=%async_computation.1 | async-start | bytes 2097152 | tf_op jit(solution)/shard_map/all_to_all | solution.py:51
  24.3 0.0 all-gather.2.cloned.1.call-start
  24.4 0.1 reduce_max.14
  24.5 4.2 %gather_fusion = bf16[4,512,512]{2,1,0:T(8,128)(2,1)} fusion(bf16[8,512,512]{2,1,0:T(8,128)(2,1)} %param.15, s32[4]{0:T(128)S(1)} %fusion.28), kind=kCustom, calls=%fused_computation | custom fusion | bytes 4194352 | tf_op jit(solution)/shard_map/vmap(jit(dynamic_index_in_dim))/gather | solution.py:68
  28.7 4.2 %copy.60 = bf16[4,512,512]{1,2,0:T(8,128)(2,1)} copy(bf16[4,512,512]{2,1,0:T(8,128)(2,1)} %gather_fusion) | data formatting | bytes 4194304 | tf_op jit(solution)/shard_map/vmap()/reshape | solution.py:68
  32.9 4.2 %gather_fusion.1 = bf16[4,512,512]{2,1,0:T(8,128)(2,1)} fusion(bf16[8,512,512]{2,1,0:T(8,128)(2,1)} %param.14, s32[4]{0:T(128)S(1)} %fusion.28), kind=kCustom, calls=%fused_computation.1 | custom fusion | bytes 4194352 | tf_op jit(solution)/shard_map/vmap(jit(dynamic_index_in_dim))/gather | solution.py:65
  37.1 11.9 %all-to-all-done.1 = bf16[4,128,1024]{2,1,0:T(8,128)(2,1)S(1)} async-done(((bf16[4,128,1024]{2,1,0:T(8,128)(2,1)}), bf16[4,128,1024]{2,1,0:T(8,128)(2,1)S(1)}, u32[]{:S(2)}, u32[]{:S(2)}) %all-to-all-start.1) | async-done | bytes 1048608 | tf_op jit(solution)/shard_map/all_to_all | solution.py:51
  49.0 0.0 copy-start.2
  49.0 1.0 copy-done.2
  50.0 0.0 copy-done
  50.0 1.2 %fusion.4 = f32[2,4,128,512]{3,2,0,1:T(8,128)S(1)} fusion(bf16[2,1024,512]{2,1,0:T(8,128)(2,1)S(1)} %copy-done, bf16[4,128,1024]{2,1,0:T(8,128)(2,1)S(1)} %all-to-all-done.1), kind=kOutput, calls=%fused_computation.7 | convolution fusion | flops 1073741824 | bytes 5242880 | tf_op jit(solution)/shard_map/snd,kdc->ksnc/dot_general | solution.py:54
  51.3 0.0 copy-start.1
  51.3 1.3 %copy-done.1 = f32[2,4,128,512]{3,2,0,1:T(8,128)} copy-done((f32[2,4,128,512]{3,2,0,1:T(8,128)}, f32[2,4,128,512]{3,2,0,1:T(8,128)S(1)}, u32[]{:S(2)}) %copy-start.1) | copy-done | bytes 2097176
  52.6 0.0 copy-start.4
  52.6 0.1 slice.14
  52.7 1.3 %squeeze.9 = f32[4,128,4,128]{3,2,1,0:T(4,128)} reshape(f32[1,4,128,512]{3,2,0,1:T(8,128)S(1)} %slice.14) | data formatting | bytes 2097152 | tf_op jit(solution)/shard_map/squeeze | solution.py:57
  54.0 0.0 copy-done.4
  54.0 5.9 %bitcast_reduce_fusion = (f32[4,128]{1,0:T(4,128)S(1)}, f32[4,128]{1,0:T(4,128)S(1)}, f32[4,4,128,128]{3,2,1,0:T(8,128)}) fusion(bf16[4,512,4,128]{1,3,2,0:T(8,128)(2,1)} %bitcast.70, f32[4,512]{1,0:T(4,128)S(1)} %copy-done.4, f32[4,128,4,128]{3,2,1,0:T(4,128)} %squeeze.9, bf16[4,512,512]{2,1,0:T(8,128)(2,1)} %gather_fusion.1), kind=kOutput, calls=%fused_computation.16 | convolution fusion | flops 546307072 | bytes 6303744 | tf_op jit(solution)/shard_map/vmap(hnl,lhd->nhd)/dot_general | solution.py:78
  59.9 1.6 %copy.61 = f32[4,128,512]{2,1,0:T(8,128)S(1)} copy(f32[4,128,512]{1,2,0:T(8,128)} %bitcast.72) | data formatting | bytes 2097152 | tf_op jit(solution)/shard_map/vmap()/reshape | solution.py:81
  61.5 4.9 %all-reduce.1 = (f32[4,128]{1,0:T(4,128)S(1)}, f32[4,128]{1,0:T(4,128)S(1)}) all-reduce(f32[4,128]{1,0:T(4,128)S(1)} %get-tuple-element.6, f32[4,128]{1,0:T(4,128)S(1)} %get-tuple-element.5), channel_id=1, replica_groups=mesh['groups'=2,'users'=4,'mp'=2,'helpers'=2] {'mp'}, use_global_device_ids=true, to_apply=%region_5.6 | all-reduce | flops 1024 | bytes 8192 | tf_op jit(solution)/shard_map/psum | solution.py:84
  66.4 2.4 %multiply_convert_fusion.1 = bf16[4,128,512]{2,1,0:T(8,128)(2,1)} fusion(f32[2,4,128,512]{3,2,0,1:T(8,128)} %copy-done.1, f32[4,128,512]{2,1,0:T(8,128)S(1)} %copy.61, f32[4,128]{1,0:T(4,128)S(1)} %get-tuple-element.10, f32[4,128]{1,0:T(4,128)S(1)} %get-tuple-element.9), kind=kLoop, calls=%fused_computation.20 | loop fusion | flops 2097152 | bytes 2625536 | tf_op jit(solution)/shard_map/convert_element_type | solution.py:88
  68.8 0.0 all-gather.2.cloned.1.call-update
  68.8 0.0 copy-start.3
  68.8 0.0 copy-start.5
  68.8 2.4 %copy.82 = bf16[64,2,8,512]{3,2,0,1:T(8,128)(2,1)} copy(bf16[64,2,8,512]{3,2,1,0:T(8,128)(2,1)} %bitcast.71) | data formatting | bytes 2097152 | tf_op jit(solution)/shard_map/all_to_all | solution.py:30
  71.2 4.5 %all-to-all-start.2 = ((bf16[512,2,512]{2,0,1:T(8,128)(2,1)}), bf16[512,2,512]{2,0,1:T(8,128)(2,1)}, u32[]{:S(2)}, u32[]{:S(2)}) async-start(bf16[512,2,512]{2,0,1:T(8,128)(2,1)} %bitcast.69), calls=%async_computation.2 | async-start | bytes 2097152 | tf_op jit(solution)/shard_map/all_to_all | solution.py:30
  75.7 23.2 %all-to-all-done.2 = bf16[512,2,512]{2,0,1:T(8,128)(2,1)} async-done(((bf16[512,2,512]{2,0,1:T(8,128)(2,1)}), bf16[512,2,512]{2,0,1:T(8,128)(2,1)}, u32[]{:S(2)}, u32[]{:S(2)}) %all-to-all-start.2) | async-done | bytes 1048608 | tf_op jit(solution)/shard_map/all_to_all | solution.py:30
  98.9 0.0 all-gather.2.cloned.1.call-done
  98.9 0.0 copy-done.3
  98.9 0.0 copy-done.5
  98.9 2.5 %multiply_reduce_fusion = f32[4,128]{1,0:T(4,128)S(1)} fusion(bf16[4,128,1024]{2,1,0:T(8,128)(2,1)} %all-gather.2.cloned.1.call-done, bf16[1024,512,1]{1,0,2:T(8,128)(2,1)} %bitcast.15, f32[512]{0:T(512)S(1)} %copy-done.5, bf16[4,128,1024]{2,1,0:T(8,128)(2,1)S(1)} %copy-done.3, s32[]{:T(128)S(6)} %select_n.51), kind=kOutput, calls=%fused_computation.19 | convolution fusion | flops 538967552 | bytes 2625540 | tf_op jit(solution)/shard_map/dfh,hk->dfk/dot_general | solution.py:92
  101.4 4.9 %psum.23 = f32[4,128]{1,0:T(4,128)S(1)} all-reduce(f32[4,128]{1,0:T(4,128)S(1)} %multiply_reduce_fusion), channel_id=1, replica_groups=mesh['groups'=2,'users'=4,'mp'=2,'helpers'=2] {'mp'}, use_global_device_ids=true, to_apply=%region_7.8 | all-reduce | flops 512 | bytes 4096 | tf_op jit(solution)/shard_map/psum | solution.py:99
  106.4 7.9 %all_to_all.45 = f32[4,1,128]{2,1,0:T(1,128)S(1)} all-to-all(f32[4,1,128]{2,1,0:T(1,128)S(1)} %bitcast.73), channel_id=1, replica_groups=mesh['groups'=2,'users'=4,'mp'=2,'helpers'=2] {'users'}, dimensions={0} | all-to-all | bytes 4096 | tf_op jit(solution)/shard_map/all_to_all | solution.py:101
  114.2 0.8 fusion.22
  (4 shorter events, 0.0 us)
Async XLA Ops:
  6.5 43.5 %copy-start = (bf16[2,1024,512]{2,1,0:T(8,128)(2,1)S(1)}, bf16[2,1024,512]{2,1,0:T(8,128)(2,1)}, u32[]{:S(2)}) copy-start(bf16[2,1024,512]{2,1,0:T(8,128)(2,1)} %param.16) | copy-start | bytes 6291460
  9.1 11.7 %all-to-all-start = ((bf16[4,1,128]{2,1,0:T(2,128)(2,1)}), bf16[4,1,128]{2,1,0:T(2,128)(2,1)S(1)}, u32[]{:S(2)}, u32[]{:S(2)}) async-start(bf16[4,1,128]{2,1,0:T(2,128)(2,1)} %copy.46), calls=%async_computation | async-start | bytes 4096 | tf_op jit(solution)/shard_map/all_to_all | solution.py:52
  20.8 28.2 %all-to-all-start.1 = ((bf16[4,128,1024]{2,1,0:T(8,128)(2,1)}), bf16[4,128,1024]{2,1,0:T(8,128)(2,1)S(1)}, u32[]{:S(2)}, u32[]{:S(2)}) async-start(bf16[4,128,1024]{2,1,0:T(8,128)(2,1)} %copy.49), calls=%async_computation.1 | async-start | bytes 2097152 | tf_op jit(solution)/shard_map/all_to_all | solution.py:51
  24.3 74.6 %all-gather.2.cloned.1.call-start = ((), (), s32[]{:S(2)}) async-start(), calls=%async_computation.4 | async-start | bytes 1572864 | tf_op jit(solution)/shard_map/all_gather | solution.py:90
  49.0 1.0 copy-start.2
  51.3 1.4 %copy-start.1 = (f32[2,4,128,512]{3,2,0,1:T(8,128)}, f32[2,4,128,512]{3,2,0,1:T(8,128)S(1)}, u32[]{:S(2)}) copy-start(f32[2,4,128,512]{3,2,0,1:T(8,128)S(1)} %fusion.4) | copy-start | bytes 6291460
  52.6 1.4 %copy-start.4 = (f32[4,512]{1,0:T(4,128)S(1)}, f32[4,512]{1,0:T(4,128)}, u32[]{:S(2)}) copy-start(f32[4,512]{1,0:T(4,128)} %param.17) | copy-start | bytes 24580
  68.8 30.1 %copy-start.3 = (bf16[4,128,1024]{2,1,0:T(8,128)(2,1)S(1)}, bf16[4,128,1024]{2,1,0:T(8,128)(2,1)}, u32[]{:S(2)}) copy-start(bf16[4,128,1024]{2,1,0:T(8,128)(2,1)} %copy-done.2) | copy-start | bytes 3145732
  68.8 30.1 %copy-start.5 = (f32[512]{0:T(512)S(1)}, f32[512]{0:T(512)}, u32[]{:S(2)}) copy-start(f32[512]{0:T(512)} %param.19) | copy-start | bytes 6148
  71.2 27.7 %all-to-all-start.2 = ((bf16[512,2,512]{2,0,1:T(8,128)(2,1)}), bf16[512,2,512]{2,0,1:T(8,128)(2,1)}, u32[]{:S(2)}, u32[]{:S(2)}) async-start(bf16[512,2,512]{2,0,1:T(8,128)(2,1)} %bitcast.69), calls=%async_computation.2 | async-start | bytes 2097152 | tf_op jit(solution)/shard_map/all_to_all | solution.py:30
Sparse Core Ops, SparseCore 0:
  68.9 29.6 all-gather.1
where the time goes:
time: 123 us; the launch traced here: 122 us
  waiting for transfers between devices  37.2 us (30%)
  local copies, waits for them, and re-layouts  22.2 us (18%)
  blocking collectives  17.8 us (14%)
  starting transfers between devices  14.3 us (12%)
  between operations  13.5 us (11%)
  matrix products  13.3 us (11%)
  other arithmetic  3.54 us (3%)
    all_to_all x1, waiting for transfers between devices, local(): lax.all_to_all(output_weight, 'mp', split_axis=1, concat_axis=0, tiled=True)  23.2 us
    all_to_all x1, waiting for transfers between devices, local(): lax.all_to_all(outgoing, 'users', split_axis=0, concat_axis=0, tiled=True)  11.9 us
    all_to_all x1, blocking collectives, local(): lax.all_to_all(summed_scores, 'users', split_axis=0, concat_axis=0, tiled...  7.87 us
    all_to_all x1, starting transfers between devices, local(): lax.all_to_all(row_tags, 'users', split_axis=0, concat_axis=0, tiled=True)  6.32 us
    dot_general x1, matrix products, attend(): jnp.einsum('hnl,lhd->nhd', weights, value_rows, preferred_element_type=jn...  5.89 us
    psum x1, blocking collectives, local(): lax.psum((jnp.sum(mixture, axis=2), jnp.sum(mixture * mixture, axis=2)),...  4.94 us
    psum x1, blocking collectives, local(): summed_scores = lax.psum(partial_value, 'mp')  4.94 us
    all_to_all x1, starting transfers between devices, local(): lax.all_to_all(output_weight, 'mp', split_axis=1, concat_axis=0, tiled=True)  4.46 us
  transfers between devices with their start and end apart: 4, of which 3 were waited for; matrix products, arithmetic and copies ran while one was open for 15% of the time, Pallas kernels for 0%

commit v1 on v0

v1 whole, which is shorter than its diff:
```python
import functools

import jax
import jax.numpy as jnp
from jax import lax
from jax.experimental import pallas as pl
from jax.experimental.pallas import tpu as pltpu
from jax.sharding import PartitionSpec as P

EPSILON = 1e-05
MOST = 32
LANES = 128
F32 = jnp.float32
BF16 = jnp.bfloat16
VMEM = pl.BlockSpec(memory_space=pltpu.VMEM)
SMEM = pl.BlockSpec(memory_space=pltpu.SMEM)
ANY = pl.BlockSpec(memory_space=pl.ANY)


def silu(v):
    return v / (1.0 + jnp.exp(-v))


def split3(v):
    high = v.astype(BF16).astype(F32)
    rest = v - high
    middle = rest.astype(BF16).astype(F32)
    return high, middle, rest - middle


def in_lanes(columns, rows):
    lane = lax.broadcasted_iota(jnp.int32, (rows, LANES), 1)
    tail = jnp.zeros((rows, LANES), F32)
    for position, column in enumerate(columns):
        tail = jnp.where(lane == position, column, tail)
    return tail


def joined(tail, first):
    return tail[:, first : first + 1] + tail[:, first + 1 : first + 2] + tail[:, first + 2 : first + 3]


def placed(block_user, own_map, block, users_here):
    storage = own_map[block_user[block]]
    return storage // users_here, storage % users_here


def query_kernel(owners, users_here, block_user, own_map, me, candidates, weights, *rest):
    slots = rest[:owners]
    x, w, x_sems, w_sem = rest[owners:]
    blocks = candidates.shape[0]
    width = w.shape[1]
    w_copy = pltpu.make_async_copy(weights.at[0], w, w_sem)
    w_copy.start()
    x_copies = [
        pltpu.make_async_copy(
            candidates.at[b, pl.ds(0, MOST)], x.at[pl.ds(b * MOST, MOST)], x_sems.at[b]
        )
        for b in range(blocks)
    ]
    for copy in x_copies:
        copy.start()
    for copy in x_copies:
        copy.wait()
    w_copy.wait()
    query = silu(jnp.dot(x[...], w[...], preferred_element_type=F32)).astype(BF16)
    homes = [placed(block_user, own_map, b, users_here) for b in range(blocks)]
    for s in range(owners):
        slot = jnp.zeros((MOST, width), BF16)
        tag = jnp.zeros((MOST, LANES), F32)
        for b, (owner, row) in enumerate(homes):
            here = (owner ^ me[0]) == s
            slot = jnp.where(here, query[b * MOST : (b + 1) * MOST], slot)
            tag = jnp.where(here, row.astype(F32), tag)
        slots[s][:, :width] = slot
        slots[s][:, width:] = tag.astype(BF16)


def attend_kernel(owners, bias, keys, values, *rest):
    slots, outs = rest[:owners], rest[owners:]
    users_here, _, width = keys.shape
    heads = bias.shape[0]
    size = width // heads
    scale = size ** (-0.5)
    for s in range(owners):
        tag = jnp.max(slots[s][:, width:].astype(F32))
        row = jnp.clip(tag.astype(jnp.int32), 0, users_here - 1)
        parts = []
        for h in range(heads):
            cut = slice(h * size, (h + 1) * size)
            logits = lax.dot_general(
                slots[s][:, cut],
                keys[row, :, cut],
                (((1,), (1,)), ((), ())),
                preferred_element_type=F32,
            )
            weight = silu(logits * scale + bias[h : h + 1, :]).astype(BF16)
            parts.append(jnp.dot(weight, values[row, :, cut], preferred_element_type=F32))
        mixture = jnp.concatenate(parts, axis=1)
        mean = jnp.mean(mixture, axis=1, keepdims=True)
        outs[s][:, :width] = (mixture - mean).astype(BF16)
        outs[s][:, width:] = in_lanes(split3(mean), MOST).astype(BF16)


def gate_kernel(candidates, weights, out_weight, w_score, gate_out, base_out, x, w, x_sems, w_sem):
    blocks = candidates.shape[0]
    rows = blocks * MOST
    width = w.shape[1]
    w_copy = pltpu.make_async_copy(weights.at[1], w, w_sem)
    w_copy.start()
    x_copies = [
        pltpu.make_async_copy(
            candidates.at[b, pl.ds(0, MOST)], x.at[pl.ds(b * MOST, MOST)], x_sems.at[b]
        )
        for b in range(blocks)
    ]
    for copy in x_copies:
        copy.start()
    for copy in x_copies:
        copy.wait()
    w_copy.wait()
    gate = silu(jnp.dot(x[...], w[...], preferred_element_type=F32))
    gate_out[...] = gate
    base_out[:rows, :] = jnp.dot(gate.astype(BF16), out_weight[...], preferred_element_type=F32)
    base_out[rows:, :] = jnp.zeros((base_out.shape[0] - rows, base_out.shape[1]), F32)
    base_out[rows : rows + 1, :width] = w_score[...]


def product_kernel(owners, users_here, block_user, own_map, me, gate, out_weight, *rest):
    slots = rest[:owners]
    full, sent = rest[owners:]
    width = gate.shape[1]
    model = out_weight.shape[1]
    blocks = gate.shape[0] // MOST
    centred, tails = [], []
    for b in range(blocks):
        owner, _ = placed(block_user, own_map, b, users_here)
        picked = slots[0][...]
        for s in range(1, owners):
            picked = jnp.where((owner ^ me[0]) == s, slots[s][...], picked)
        picked = picked.astype(F32)
        centred.append(picked[:, :width])
        tails.append(picked[:, width:])
    centred = jnp.concatenate(centred, axis=0)
    mean = joined(jnp.concatenate(tails, axis=0), 0)
    squares = jnp.sum(centred * centred, axis=1, keepdims=True)
    product = jnp.dot(
        (centred * gate[...]).astype(BF16), out_weight[...], preferred_element_type=F32
    )
    tail = in_lanes(split3(mean) + split3(squares), centred.shape[0])
    full[:, :model] = product
    full[:, model:] = tail
    sent[:, :model] = product.astype(BF16)
    sent[:, model:] = tail.astype(BF16)


def score_kernel(parts, block_count, me, candidates, *rest):
    bases, products, out = rest[:parts], rest[parts : 2 * parts], rest[2 * parts]
    x, sems = rest[2 * parts + 1 :]
    blocks, block_rows, model = candidates.shape
    rows = blocks * MOST
    width = model // parts
    copies = [
        pltpu.make_async_copy(
            candidates.at[b, pl.ds(0, MOST)], x.at[pl.ds(b * MOST, MOST)], sems.at[b]
        )
        for b in range(blocks)
    ]
    for copy in copies:
        copy.start()
    for copy in copies:
        copy.wait()
    tails = [p[:, model:].astype(F32) for p in products]
    means = [joined(t, 0) for t in tails]
    squares = sum(joined(t, 3) for t in tails)
    mean = sum(means) / parts
    spread = squares / model + sum((m - mean) * (m - mean) for m in means) / parts
    scale = lax.rsqrt(spread + EPSILON)
    total = sum(p[:, :model].astype(F32) for p in products)
    for m, base in zip(means, bases):
        total = total + (m - mean) * base[:rows, :]
    terms = silu(x[...].astype(F32) + total * scale)
    score = jnp.zeros((rows, 1), F32)
    for c in range(parts):
        vector = jnp.zeros((1, width), F32)
        for s in range(parts):
            vector = jnp.where((me[0] ^ s) == c, bases[s][rows : rows + 1, :width], vector)
        score = score + jnp.sum(
            terms[:, c * width : (c + 1) * width] * vector, axis=1, keepdims=True
        )
    place = lax.broadcasted_iota(jnp.int32, (MOST, block_rows), 0)
    lane = lax.broadcasted_iota(jnp.int32, (MOST, block_rows), 1)
    for b in range(blocks):
        keep = (place == lane) & (lane < block_count[b])
        spread_out = jnp.where(keep, score[b * MOST : (b + 1) * MOST], 0.0)
        out[b : b + 1, :] = jnp.sum(spread_out, axis=0, keepdims=True)


def exchange(arrays, axis):
    size = lax.axis_size(axis)
    return [arrays[0]] + [
        lax.ppermute(arrays[s], axis, [(k, k ^ s) for k in range(size)]) for s in range(1, size)
    ]


def local(
    candidates,
    block_user,
    block_count,
    own_map,
    history_key_cache,
    cache_values,
    w_query_unit,
    time_bias,
    output_weight,
    w_score,
):
    owners = lax.axis_size("users")
    parts = lax.axis_size("mp")
    user_index = lax.axis_index("users").astype(jnp.int32).reshape(1)
    model_index = lax.axis_index("mp").astype(jnp.int32).reshape(1)
    blocks, block_rows, model = candidates.shape
    users_here, _, width = history_key_cache.shape
    rows = blocks * MOST
    shape = jax.ShapeDtypeStruct

    def call(kernel, out_shape, in_specs, scratch=()):
        many = isinstance(out_shape, list)
        return pl.pallas_call(
            kernel,
            out_shape=out_shape,
            in_specs=in_specs,
            out_specs=[VMEM] * len(out_shape) if many else VMEM,
            scratch_shapes=list(scratch),
            compiler_params=pltpu.CompilerParams(vmem_limit_bytes=40 * 1024 * 1024),
        )

    loads = [
        pltpu.VMEM((rows, model), BF16),
        pltpu.VMEM((model, width), BF16),
        pltpu.SemaphoreType.DMA((blocks,)),
        pltpu.SemaphoreType.DMA,
    ]
    slots = call(
        functools.partial(query_kernel, owners, users_here),
        [shape((MOST, width + LANES), BF16)] * owners,
        [SMEM, SMEM, SMEM, ANY, ANY],
        loads,
    )(block_user, own_map, user_index, candidates, w_query_unit)
    slots = exchange(slots, "users")
    gate, base = call(
        gate_kernel,
        [shape((rows, width), F32), shape((rows + 8, model), F32)],
        [ANY, ANY, VMEM, VMEM],
        loads,
    )(candidates, w_query_unit, output_weight, w_score.reshape(1, width))
    bases = exchange([base] * parts, "mp")
    mixtures = call(
        functools.partial(attend_kernel, owners),
        [shape((MOST, width + LANES), BF16)] * owners,
        [VMEM] * (3 + owners),
    )(time_bias, history_key_cache, cache_values, *slots)
    mixtures = exchange(mixtures, "users")
    product, sent = call(
        functools.partial(product_kernel, owners, users_here),
        [shape((rows, model + LANES), F32), shape((rows, model + LANES), BF16)],
        [SMEM, SMEM, SMEM] + [VMEM] * (2 + owners),
    )(block_user, own_map, user_index, gate, output_weight, *mixtures)
    products = [product] + exchange([sent] * parts, "mp")[1:]
    return call(
        functools.partial(score_kernel, parts),
        shape((blocks, block_rows), F32),
        [SMEM, SMEM, ANY] + [VMEM] * (2 * parts),
        [pltpu.VMEM((rows, model), BF16), pltpu.SemaphoreType.DMA((blocks,))],
    )(block_count, model_index, candidates, *bases, *products)


def solution(mesh):
    return jax.shard_map(
        local,
        mesh=mesh,
        in_specs=(
            P(("groups", "users", "helpers"), None, None),
            P(("groups", "users", "helpers")),
            P(("groups", "users", "helpers")),
            P("groups"),
            P(("groups", "users"), None, "mp"),
            P(("groups", "users"), None, "mp"),
            P(None, None, "mp"),
            P("mp", None),
            P("mp", None),
            P("mp"),
        ),
        out_specs=P(("groups", "users", "helpers"), None),
        check_vma=False,
    )
```

time: 123 us -> 44.6 us (0.36)
  waiting for transfers between devices: 37.2 us -> 12.5 us
  blocking collectives: 17.8 us -> 0 us
  between operations: 13.5 us -> 0.07 us
  matrix products: 13.3 us -> 0 us
  local copies, waits for them, and re-layouts: 22.2 us -> 11.3 us
  Pallas kernels: 0 us -> 7.72 us
  other arithmetic: 3.54 us -> 0 us
  starting transfers between devices: 14.3 us -> 12.7 us
    all_to_all x3 -> x0, waiting for transfers between devices: 37.2 us -> none  [the longest x1 23.2 us: local(): lax.all_to_all(output_weight, 'mp', split_axis=1, concat_axis=0, tiled=True)]
    all_to_all x3 -> x0, starting transfers between devices: 14.3 us -> none  [the longest x1 6.32 us: local(): lax.all_to_all(row_tags, 'users', split_axis=0, concat_axis=0, tiled=True)]
    dot_general x6 -> x0, matrix products: 13.3 us -> none  [the longest x1 5.89 us: attend(): jnp.einsum('hnl,lhd->nhd', weights, value_rows, preferred_element_type=jn...]
    ppermute x0 -> x8, starting transfers between devices: none -> 12.7 us  [exchange(): lax.ppermute(arrays[s], axis, [(k, k ^ s) for k in range(size)])]
    ppermute x0 -> x8, waiting for transfers between devices: none -> 12.5 us  [exchange(): lax.ppermute(arrays[s], axis, [(k, k ^ s) for k in range(size)])]
    psum x2 -> x0, blocking collectives: 9.88 us -> none  [the longest x1 4.94 us: local(): lax.psum((jnp.sum(mixture, axis=2), jnp.sum(mixture * mixture, axis=2)),...]
    unnamed x12 -> x32, local copies, waits for them, and re-layouts: 2.37 us -> 11.3 us
    gather x2 -> x0, local copies, waits for them, and re-layouts: 8.42 us -> none  [the longest x1 4.22 us: attend(): lax.dynamic_index_in_dim(cache_values, user_slot, 0, keepdims=False)]
  transfers between devices with their start and end apart: 4 -> 8, of which waited for: 3 -> 5; matrix products, arithmetic and copies ran while one was open for 15% -> 0% of each run, Pallas kernels for 0% -> 12%
where the time goes in v1:
time: 44.6 us; the launch traced here: 44.2 us
  starting transfers between devices  12.7 us (28%)
  waiting for transfers between devices  12.5 us (28%)
  local copies, waits for them, and re-layouts  11.3 us (25%)
  Pallas kernels  7.72 us (17%)
    ppermute x8, starting transfers between devices, exchange(): lax.ppermute(arrays[s], axis, [(k, k ^ s) for k in range(size)])  12.7 us
    ppermute x8, waiting for transfers between devices, exchange(): lax.ppermute(arrays[s], axis, [(k, k ^ s) for k in range(size)])  12.5 us
    unnamed x32, local copies, waits for them, and re-layouts  11.3 us
    pallas_call x1, Pallas kernels, local(): call(functools.partial(attend_kernel, owners), [shape((MOST, width + LANE...  3.13 us
    pallas_call x1, Pallas kernels, local(): call(functools.partial(score_kernel, parts), shape((blocks, block_rows),...  1.71 us
    pallas_call x1, Pallas kernels, local(): call(functools.partial(query_kernel, owners, users_here), [shape((MOST, w...  1.15 us
  transfers between devices with their start and end apart: 8, of which 5 were waited for; matrix products, arithmetic and copies ran while one was open for 0% of the time, Pallas kernels for 12%

profile of v1, /device:TPU:0, one launch (start us, length us, event | category | flops | bytes accessed | tf_op | source)
XLA Modules:
  0.0 44.2 jit_solution(784289733072116345)
XLA Ops:
  0.0 0.0 copy-start
  0.0 1.6 %copy-done = bf16[2,1024,512]{2,1,0:T(8,128)(2,1)S(1)} copy-done((bf16[2,1024,512]{2,1,0:T(8,128)(2,1)S(1)}, bf16[2,1024,512]{2,1,0:T(8,128)(2,1)}, u32[]{:S(2)}) %copy-start) | copy-done | bytes 2097176
  1.6 0.0 copy-start.2
  1.6 1.0 %copy-done.2 = bf16[2,128,1024]{2,1,0:T(8,128)(2,1)S(1)} copy-done((bf16[2,128,1024]{2,1,0:T(8,128)(2,1)S(1)}, bf16[2,128,1024]{2,1,0:T(8,128)(2,1)}, u32[]{:S(2)}) %copy-start.2) | copy-done | bytes 524312
  2.6 0.0 copy-start.7
  2.6 1.2 %copy-done.7 = bf16[512,1024]{1,0:T(8,128)(2,1)S(1)} copy-done((bf16[512,1024]{1,0:T(8,128)(2,1)S(1)}, bf16[512,1024]{1,0:T(8,128)(2,1)}, u32[]{:S(2)}) %copy-start.7) | copy-done | bytes 1048600
  3.9 0.0 copy-start.10
  3.9 0.7 %copy-done.10 = f32[512]{0:T(512)S(1)} copy-done((f32[512]{0:T(512)S(1)}, f32[512]{0:T(512)}, u32[]{:S(2)}) %copy-start.10) | copy-done | bytes 2072
  4.5 0.0 copy-start.1
  4.5 0.0 copy-start.9
  4.5 0.8 %shard_map.100 = (f32[64,512]{1,0:T(8,128)S(1)}, f32[72,1024]{1,0:T(8,128)S(1)}) custom-call(bf16[2,128,1024]{2,1,0:T(8,128)(2,1)S(1)} %copy-done.2, bf16[2,1024,512]{2,1,0:T(8,128)(2,1)S(1)} %copy-done, bf16[512,1024]{1,0:T(8,128)(2,1)S(1)} %copy-done.7, f32[1,512]{1,0:T(1,128)S(1)} %bitcast.3), custom_call_target="tpu_custom_call" | custom-call | tf_op jit(solution)/shard_map/pallas_call | solution.py:251
  5.4 3.0 %collective-permute-start = (f32[72,1024]{1,0:T(8,128)S(1)}, f32[72,1024]{1,0:T(8,128)S(1)}, u32[]{:S(2)}, u32[]{:S(2)}) collective-permute-start(f32[72,1024]{1,0:T(8,128)S(1)} %get-tuple-element.17.rest_0_), channel_id=1, source_target_pairs={{0,2},{2,0},{1,3},{3,1},{4,6},{6,4},{5,7},{7,5},{8,10},{10,8},{9,1... | collective-permute-start | bytes 884744 | tf_op jit(solution)/shard_map/ppermute | solution.py:202
  8.4 0.0 copy-done.1
  8.4 0.0 copy-start.3
  8.4 1.0 %copy-done.3 = bf16[2,128,1024]{2,1,0:T(8,128)(2,1)S(1)} copy-done((bf16[2,128,1024]{2,1,0:T(8,128)(2,1)S(1)}, bf16[2,128,1024]{2,1,0:T(8,128)(2,1)}, u32[]{:S(2)}) %copy-start.3) | copy-done | bytes 524312
  9.4 0.0 copy-start.11
  9.4 0.7 %copy-done.11 = s32[2]{0:T(128)S(1)} copy-done((s32[2]{0:T(128)S(1)}, s32[2]{0:T(128)}, u32[]{:S(2)}) %copy-start.11) | copy-done | bytes 32
  10.1 0.0 copy-start.13
  10.1 0.7 %copy-done.13 = s32[32]{0:T(128)S(1)} copy-done((s32[32]{0:T(128)S(1)}, s32[32]{0:T(128)}, u32[]{:S(2)}) %copy-start.13) | copy-done | bytes 152
  10.8 1.2 %shard_map.101 = (bf16[32,640]{1,0:T(8,128)(2,1)S(1)}, bf16[32,640]{1,0:T(8,128)(2,1)S(1)}, bf16[32,640]{1,0:T(8,128)(2,1)S(1)}, bf16[32,640]{1,0:T(8,128)(2,1)S(1)}) custom-call(s32[2]{0:T(128)S(1)} %copy-done.11, s32[32]{0:T(128)S(1)} %copy-done.13, s32[1]{0:T(128)} %bitcast.2.me, bf16[2,128,1024]{2,1,0:T(8,128)(2,1)S(1)} %copy-done.3, ...), custom_call_target="tpu_custom_call" | custom-call | tf_op jit(solution)/shard_map/pallas_call | solution.py:244
  11.9 1.6 %collective-permute-start.1 = (bf16[32,640]{1,0:T(8,128)(2,1)S(1)}, bf16[32,640]{1,0:T(8,128)(2,1)S(1)}, u32[]{:S(2)}, u32[]{:S(2)}) collective-permute-start(bf16[32,640]{1,0:T(8,128)(2,1)S(1)} %get-tuple-element.20), channel_id=1, source_target_pairs={{0,4},{4,0},{8,12},{12,8},{1,5},{5,1},{9,13},{13,9},{2,6},{6,2},{1... | collective-permute-start | bytes 122888 | tf_op jit(solution)/shard_map/ppermute | solution.py:202
  13.6 2.6 %collective-permute-start.2 = (bf16[32,640]{1,0:T(8,128)(2,1)S(1)}, bf16[32,640]{1,0:T(8,128)(2,1)S(1)}, u32[]{:S(2)}, u32[]{:S(2)}) collective-permute-start(bf16[32,640]{1,0:T(8,128)(2,1)S(1)} %get-tuple-element.21), channel_id=1, source_target_pairs={{0,8},{4,12},{8,0},{12,4},{1,9},{5,13},{9,1},{13,5},{2,10},{6,14},... | collective-permute-start | bytes 122888 | tf_op jit(solution)/shard_map/ppermute | solution.py:202
  16.1 0.2 collective-permute-start.3
  16.4 0.0 collective-permute-done.1.rest_1_
  16.4 2.6 %collective-permute-done.2.rest_2_ = bf16[32,640]{1,0:T(8,128)(2,1)S(1)} collective-permute-done((bf16[32,640]{1,0:T(8,128)(2,1)S(1)}, bf16[32,640]{1,0:T(8,128)(2,1)S(1)}, u32[]{:S(2)}, u32[]{:S(2)}) %collective-permute-start.2) | collective-permute-done | bytes 40992 | tf_op jit(solution)/shard_map/ppermute | solution.py:202
  18.9 3.0 %collective-permute-done.3.rest_3_ = bf16[32,640]{1,0:T(8,128)(2,1)S(1)} collective-permute-done((bf16[32,640]{1,0:T(8,128)(2,1)S(1)}, bf16[32,640]{1,0:T(8,128)(2,1)S(1)}, u32[]{:S(2)}, u32[]{:S(2)}) %collective-permute-start.3) | collective-permute-done | bytes 40992 | tf_op jit(solution)/shard_map/ppermute | solution.py:202
  21.9 0.0 copy-done.9
  21.9 0.0 copy-start.5
  22.0 2.2 %copy-done.5 = bf16[8,512,512]{2,1,0:T(8,128)(2,1)S(1)} copy-done((bf16[8,512,512]{2,1,0:T(8,128)(2,1)S(1)}, bf16[8,512,512]{2,1,0:T(8,128)(2,1)}, u32[]{:S(2)}) %copy-start.5) | copy-done | bytes 4194328
  24.1 2.2 %copy-done.6 = bf16[8,512,512]{2,1,0:T(8,128)(2,1)S(1)} copy-done((bf16[8,512,512]{2,1,0:T(8,128)(2,1)S(1)}, bf16[8,512,512]{2,1,0:T(8,128)(2,1)}, u32[]{:S(2)}) %copy-start.6) | copy-done | bytes 4194328
  26.3 0.0 copy-start.15
  26.3 3.1 %shard_map.102 = (bf16[32,640]{1,0:T(8,128)(2,1)S(1)}, bf16[32,640]{1,0:T(8,128)(2,1)S(1)}, bf16[32,640]{1,0:T(8,128)(2,1)S(1)}, bf16[32,640]{1,0:T(8,128)(2,1)S(1)}) custom-call(f32[4,512]{1,0:T(4,128)S(1)} %copy-done.9, bf16[8,512,512]{2,1,0:T(8,128)(2,1)S(1)} %copy-done.5, bf16[8,512,512]{2,1,0:T(8,128)(2,1)S(1)} %copy-done.6, ...), custom_call_target="tpu_custom_call" | custom-call | tf_op jit(solution)/shard_map/pallas_call | solution.py:258
  29.5 0.1 collective-permute-start.4
  29.6 1.0 %collective-permute-start.5 = (bf16[32,640]{1,0:T(8,128)(2,1)S(1)}, bf16[32,640]{1,0:T(8,128)(2,1)S(1)}, u32[]{:S(2)}, u32[]{:S(2)}) collective-permute-start(bf16[32,640]{1,0:T(8,128)(2,1)S(1)} %get-tuple-element.25), channel_id=1, source_target_pairs={{0,8},{4,12},{8,0},{12,4},{1,9},{5,13},{9,1},{13,5},{2,10},{6,14},... | collective-permute-start | bytes 122888 | tf_op jit(solution)/shard_map/ppermute | solution.py:202
  30.6 3.3 %collective-permute-start.6 = (bf16[32,640]{1,0:T(8,128)(2,1)S(1)}, bf16[32,640]{1,0:T(8,128)(2,1)S(1)}, u32[]{:S(2)}, u32[]{:S(2)}) collective-permute-start(bf16[32,640]{1,0:T(8,128)(2,1)S(1)} %get-tuple-element.26), channel_id=1, source_target_pairs={{0,12},{4,8},{8,4},{12,0},{1,13},{5,9},{9,5},{13,1},{2,14},{6,10},... | collective-permute-start | bytes 122888 | tf_op jit(solution)/shard_map/ppermute | solution.py:202
  33.9 0.0 collective-permute-done.4.rest_1_
  33.9 0.6 %collective-permute-done.5.rest_2_ = bf16[32,640]{1,0:T(8,128)(2,1)S(1)} collective-permute-done((bf16[32,640]{1,0:T(8,128)(2,1)S(1)}, bf16[32,640]{1,0:T(8,128)(2,1)S(1)}, u32[]{:S(2)}, u32[]{:S(2)}) %collective-permute-start.5) | collective-permute-done | bytes 40992 | tf_op jit(solution)/shard_map/ppermute | solution.py:202
  34.5 1.9 %collective-permute-done.6.rest_3_ = bf16[32,640]{1,0:T(8,128)(2,1)S(1)} collective-permute-done((bf16[32,640]{1,0:T(8,128)(2,1)S(1)}, bf16[32,640]{1,0:T(8,128)(2,1)S(1)}, u32[]{:S(2)}, u32[]{:S(2)}) %collective-permute-start.6) | collective-permute-done | bytes 40992 | tf_op jit(solution)/shard_map/ppermute | solution.py:202
  36.4 0.0 copy-done.8
  36.4 0.0 copy-done.12
  36.4 0.0 copy-done.14
  36.4 0.9 %shard_map.103 = (f32[64,1152]{1,0:T(8,128)S(1)}, bf16[64,1152]{1,0:T(8,128)(2,1)S(1)}) custom-call(s32[2]{0:T(128)S(1)} %copy-done.12, s32[32]{0:T(128)S(1)} %copy-done.14, s32[1]{0:T(128)} %bitcast.2.me, f32[64,512]{1,0:T(8,128)S(1)} %get-tuple-element.18.gate, bf16[512,1024]{1,0:T(8,128)(2,1)S(1)} %copy-done.8, ...), custom_call_target="tpu_custom_call" | custom-call | tf_op jit(solution)/shard_map/pallas_call | solution.py:264
  37.3 0.8 %collective-permute-start.7 = (bf16[64,1152]{1,0:T(8,128)(2,1)S(1)}, bf16[64,1152]{1,0:T(8,128)(2,1)S(1)}, u32[]{:S(2)}, u32[]{:S(2)}) collective-permute-start(bf16[64,1152]{1,0:T(8,128)(2,1)S(1)} %get-tuple-element.28), channel_id=1, source_target_pairs={{0,2},{2,0},{1,3},{3,1},{4,6},{6,4},{5,7},{7,5},{8,10},{10,8},{9,1... | collective-permute-start | bytes 442376 | tf_op jit(solution)/shard_map/ppermute | solution.py:202
  38.1 4.4 %collective-permute-done.7.rest_3_ = bf16[64,1152]{1,0:T(8,128)(2,1)S(1)} collective-permute-done((bf16[64,1152]{1,0:T(8,128)(2,1)S(1)}, bf16[64,1152]{1,0:T(8,128)(2,1)S(1)}, u32[]{:S(2)}, u32[]{:S(2)}) %collective-permute-start.7) | collective-permute-done | bytes 147488 | tf_op jit(solution)/shard_map/ppermute | solution.py:202
  42.5 0.0 collective-permute-done.rest_1_
  42.5 0.0 copy-done.4
  42.5 0.0 copy-done.15
  42.5 1.7 %shard_map.104 = f32[2,128]{1,0:T(2,128)} custom-call(s32[2]{0:T(128)S(1)} %copy-done.15, s32[1]{0:T(128)} %bitcast.me, bf16[2,128,1024]{2,1,0:T(8,128)(2,1)S(1)} %copy-done.4, f32[72,1024]{1,0:T(8,128)S(1)} %get-tuple-element.17.rest_0_, f32[72,1024]{1,0:T(8,128)S(1)} %collective-permute-done.rest_1_, f32[64,1152]{1,0:T(8,128)S(1)} %get-tuple-element.27.rest_2_, ...), custom_call_target="tpu_custom_call" | custom-call | tf_op jit(solution)/shard_map/pallas_call | solution.py:270
  (5 shorter events, 0.0 us)
Async XLA Ops:
  0.0 1.6 %copy-start = (bf16[2,1024,512]{2,1,0:T(8,128)(2,1)S(1)}, bf16[2,1024,512]{2,1,0:T(8,128)(2,1)}, u32[]{:S(2)}) copy-start(bf16[2,1024,512]{2,1,0:T(8,128)(2,1)} %weights.3) | copy-start | bytes 6291460
  1.6 1.0 %copy-start.2 = (bf16[2,128,1024]{2,1,0:T(8,128)(2,1)S(1)}, bf16[2,128,1024]{2,1,0:T(8,128)(2,1)}, u32[]{:S(2)}) copy-start(bf16[2,128,1024]{2,1,0:T(8,128)(2,1)} %candidates.5) | copy-start | bytes 1572868
  2.6 1.2 %copy-start.7 = (bf16[512,1024]{1,0:T(8,128)(2,1)S(1)}, bf16[512,1024]{1,0:T(8,128)(2,1)}, u32[]{:S(2)}) copy-start(bf16[512,1024]{1,0:T(8,128)(2,1)} %out_weight.3) | copy-start | bytes 3145732
  3.9 0.7 %copy-start.10 = (f32[512]{0:T(512)S(1)}, f32[512]{0:T(512)}, u32[]{:S(2)}) copy-start(f32[512]{0:T(512)} %param.19) | copy-start | bytes 6148
  4.5 3.9 %copy-start.1 = (bf16[2,1024,512]{2,1,0:T(8,128)(2,1)S(1)}, bf16[2,1024,512]{2,1,0:T(8,128)(2,1)}, u32[]{:S(2)}) copy-start(bf16[2,1024,512]{2,1,0:T(8,128)(2,1)} %weights.3) | copy-start | bytes 6291460
  4.5 17.4 %copy-start.9 = (f32[4,512]{1,0:T(4,128)S(1)}, f32[4,512]{1,0:T(4,128)}, u32[]{:S(2)}) copy-start(f32[4,512]{1,0:T(4,128)} %bias.1) | copy-start | bytes 24580
  5.4 37.1 %collective-permute-start = (f32[72,1024]{1,0:T(8,128)S(1)}, f32[72,1024]{1,0:T(8,128)S(1)}, u32[]{:S(2)}, u32[]{:S(2)}) collective-permute-start(f32[72,1024]{1,0:T(8,128)S(1)} %get-tuple-element.17.rest_0_), channel_id=1, source_target_pairs={{0,2},{2,0},{1,3},{3,1},{4,6},{6,4},{5,7},{7,5},{8,10},{10,8},{9,1... | collective-permute-start | bytes 884744 | tf_op jit(solution)/shard_map/ppermute | solution.py:202
  8.4 1.0 %copy-start.3 = (bf16[2,128,1024]{2,1,0:T(8,128)(2,1)S(1)}, bf16[2,128,1024]{2,1,0:T(8,128)(2,1)}, u32[]{:S(2)}) copy-start(bf16[2,128,1024]{2,1,0:T(8,128)(2,1)} %candidates.5) | copy-start | bytes 1572868
  9.4 0.7 %copy-start.11 = (s32[2]{0:T(128)S(1)}, s32[2]{0:T(128)}, u32[]{:S(2)}) copy-start(s32[2]{0:T(128)} %block_user.3) | copy-start | bytes 28
  10.1 0.7 %copy-start.13 = (s32[32]{0:T(128)S(1)}, s32[32]{0:T(128)}, u32[]{:S(2)}) copy-start(s32[32]{0:T(128)} %own_map.3) | copy-start | bytes 388
  11.9 4.5 %collective-permute-start.1 = (bf16[32,640]{1,0:T(8,128)(2,1)S(1)}, bf16[32,640]{1,0:T(8,128)(2,1)S(1)}, u32[]{:S(2)}, u32[]{:S(2)}) collective-permute-start(bf16[32,640]{1,0:T(8,128)(2,1)S(1)} %get-tuple-element.20), channel_id=1, source_target_pairs={{0,4},{4,0},{8,12},{12,8},{1,5},{5,1},{9,13},{13,9},{2,6},{6,2},{1... | collective-permute-start | bytes 122888 | tf_op jit(solution)/shard_map/ppermute | solution.py:202
  13.6 5.4 %collective-permute-start.2 = (bf16[32,640]{1,0:T(8,128)(2,1)S(1)}, bf16[32,640]{1,0:T(8,128)(2,1)S(1)}, u32[]{:S(2)}, u32[]{:S(2)}) collective-permute-start(bf16[32,640]{1,0:T(8,128)(2,1)S(1)} %get-tuple-element.21), channel_id=1, source_target_pairs={{0,8},{4,12},{8,0},{12,4},{1,9},{5,13},{9,1},{13,5},{2,10},{6,14},... | collective-permute-start | bytes 122888 | tf_op jit(solution)/shard_map/ppermute | solution.py:202
  16.1 5.8 %collective-permute-start.3 = (bf16[32,640]{1,0:T(8,128)(2,1)S(1)}, bf16[32,640]{1,0:T(8,128)(2,1)S(1)}, u32[]{:S(2)}, u32[]{:S(2)}) collective-permute-start(bf16[32,640]{1,0:T(8,128)(2,1)S(1)} %get-tuple-element.22), channel_id=1, source_target_pairs={{0,12},{4,8},{8,4},{12,0},{1,13},{5,9},{9,5},{13,1},{2,14},{6,10},... | collective-permute-start | bytes 122888 | tf_op jit(solution)/shard_map/ppermute | solution.py:202
  21.9 2.2 %copy-start.5 = (bf16[8,512,512]{2,1,0:T(8,128)(2,1)S(1)}, bf16[8,512,512]{2,1,0:T(8,128)(2,1)}, u32[]{:S(2)}) copy-start(bf16[8,512,512]{2,1,0:T(8,128)(2,1)} %keys.1) | copy-start | bytes 12582916
  24.1 2.2 %copy-start.6 = (bf16[8,512,512]{2,1,0:T(8,128)(2,1)S(1)}, bf16[8,512,512]{2,1,0:T(8,128)(2,1)}, u32[]{:S(2)}) copy-start(bf16[8,512,512]{2,1,0:T(8,128)(2,1)} %values.1) | copy-start | bytes 12582916
  26.3 10.1 %copy-start.8 = (bf16[512,1024]{1,0:T(8,128)(2,1)S(1)}, bf16[512,1024]{1,0:T(8,128)(2,1)}, u32[]{:S(2)}) copy-start(bf16[512,1024]{1,0:T(8,128)(2,1)} %out_weight.3) | copy-start | bytes 3145732
  26.3 10.1 %copy-start.12 = (s32[2]{0:T(128)S(1)}, s32[2]{0:T(128)}, u32[]{:S(2)}) copy-start(s32[2]{0:T(128)} %block_user.3) | copy-start | bytes 28
  26.3 10.1 %copy-start.14 = (s32[32]{0:T(128)S(1)}, s32[32]{0:T(128)}, u32[]{:S(2)}) copy-start(s32[32]{0:T(128)} %own_map.3) | copy-start | bytes 388
  26.3 16.2 %copy-start.4 = (bf16[2,128,1024]{2,1,0:T(8,128)(2,1)S(1)}, bf16[2,128,1024]{2,1,0:T(8,128)(2,1)}, u32[]{:S(2)}) copy-start(bf16[2,128,1024]{2,1,0:T(8,128)(2,1)} %candidates.5) | copy-start | bytes 1572868
  26.3 16.2 %copy-start.15 = (s32[2]{0:T(128)S(1)}, s32[2]{0:T(128)}, u32[]{:S(2)}) copy-start(s32[2]{0:T(128)} %block_count.1) | copy-start | bytes 28
  29.5 4.5 %collective-permute-start.4 = (bf16[32,640]{1,0:T(8,128)(2,1)S(1)}, bf16[32,640]{1,0:T(8,128)(2,1)S(1)}, u32[]{:S(2)}, u32[]{:S(2)}) collective-permute-start(bf16[32,640]{1,0:T(8,128)(2,1)S(1)} %get-tuple-element.24), channel_id=1, source_target_pairs={{0,4},{4,0},{8,12},{12,8},{1,5},{5,1},{9,13},{13,9},{2,6},{6,2},{1... | collective-permute-start | bytes 122888 | tf_op jit(solution)/shard_map/ppermute | solution.py:202
  29.6 5.0 %collective-permute-start.5 = (bf16[32,640]{1,0:T(8,128)(2,1)S(1)}, bf16[32,640]{1,0:T(8,128)(2,1)S(1)}, u32[]{:S(2)}, u32[]{:S(2)}) collective-permute-start(bf16[32,640]{1,0:T(8,128)(2,1)S(1)} %get-tuple-element.25), channel_id=1, source_target_pairs={{0,8},{4,12},{8,0},{12,4},{1,9},{5,13},{9,1},{13,5},{2,10},{6,14},... | collective-permute-start | bytes 122888 | tf_op jit(solution)/shard_map/ppermute | solution.py:202
  30.6 5.8 %collective-permute-start.6 = (bf16[32,640]{1,0:T(8,128)(2,1)S(1)}, bf16[32,640]{1,0:T(8,128)(2,1)S(1)}, u32[]{:S(2)}, u32[]{:S(2)}) collective-permute-start(bf16[32,640]{1,0:T(8,128)(2,1)S(1)} %get-tuple-element.26), channel_id=1, source_target_pairs={{0,12},{4,8},{8,4},{12,0},{1,13},{5,9},{9,5},{13,1},{2,14},{6,10},... | collective-permute-start | bytes 122888 | tf_op jit(solution)/shard_map/ppermute | solution.py:202
  37.3 5.2 %collective-permute-start.7 = (bf16[64,1152]{1,0:T(8,128)(2,1)S(1)}, bf16[64,1152]{1,0:T(8,128)(2,1)S(1)}, u32[]{:S(2)}, u32[]{:S(2)}) collective-permute-start(bf16[64,1152]{1,0:T(8,128)(2,1)S(1)} %get-tuple-element.28), channel_id=1, source_target_pairs={{0,2},{2,0},{1,3},{3,1},{4,6},{6,4},{5,7},{7,5},{8,10},{10,8},{9,1... | collective-permute-start | bytes 442376 | tf_op jit(solution)/shard_map/ppermute | solution.py:202

commit v2 on v1

v2 whole, which is shorter than its diff:
```python
import functools

import jax
import jax.numpy as jnp
from jax import lax
from jax.experimental import pallas as pl
from jax.experimental.pallas import tpu as pltpu
from jax.sharding import PartitionSpec as P

EPSILON = 1e-05
MOST = 32
LANES = 128
F32 = jnp.float32
BF16 = jnp.bfloat16
VMEM = pl.BlockSpec(memory_space=pltpu.VMEM)
SMEM = pl.BlockSpec(memory_space=pltpu.SMEM)
HBM = pl.BlockSpec(memory_space=pltpu.HBM)


def silu(v):
    return v / (1.0 + jnp.exp(-v))


def split3(v):
    high = v.astype(BF16).astype(F32)
    rest = v - high
    middle = rest.astype(BF16).astype(F32)
    return high, middle, rest - middle


def in_lanes(columns, rows):
    lane = lax.broadcasted_iota(jnp.int32, (rows, LANES), 1)
    tail = jnp.zeros((rows, LANES), F32)
    for position, column in enumerate(columns):
        tail = jnp.where(lane == position, column, tail)
    return tail


def joined(tail, first):
    return tail[:, first : first + 1] + tail[:, first + 1 : first + 2] + tail[:, first + 2 : first + 3]


def placed(block_user, own_map, block, users_here):
    storage = own_map[block_user[block]]
    return storage // users_here, storage % users_here


def query_kernel(
    owners, users_here, user_source, map_source, count_source, me, candidates, weights, *rest
):
    slots, (x, place, counts) = rest[:owners], rest[owners : owners + 3]
    w, block_user, own_map, x_sems, sems = rest[owners + 3 :]
    blocks = candidates.shape[0]
    width = w.shape[1]
    w_copy = pltpu.make_async_copy(weights.at[0], w, sems.at[0])
    x_copies = [
        pltpu.make_async_copy(
            candidates.at[b, pl.ds(0, MOST)], x.at[pl.ds(b * MOST, MOST)], x_sems.at[b]
        )
        for b in range(blocks)
    ]
    small = [
        pltpu.make_async_copy(user_source, block_user, sems.at[1]),
        pltpu.make_async_copy(map_source, own_map, sems.at[2]),
        pltpu.make_async_copy(count_source, counts, sems.at[3]),
    ]
    for copy in small + x_copies + [w_copy]:
        copy.start()
    for copy in small:
        copy.wait()
    homes = [placed(block_user, own_map, b, users_here) for b in range(blocks)]
    for b, (owner, _) in enumerate(homes):
        place[b] = owner ^ me[0]
    for copy in x_copies + [w_copy]:
        copy.wait()
    query = silu(jnp.dot(x[...], w[...], preferred_element_type=F32)).astype(BF16)
    for s in range(owners):
        slot = jnp.zeros((MOST, width), BF16)
        tag = jnp.zeros((MOST, LANES), F32)
        for b, (owner, row) in enumerate(homes):
            here = (owner ^ me[0]) == s
            slot = jnp.where(here, query[b * MOST : (b + 1) * MOST], slot)
            tag = jnp.where(here, row.astype(F32), tag)
        slots[s][:, :width] = slot
        slots[s][:, width:] = tag.astype(BF16)


def attend_kernel(owners, _, bias, keys, values, *rest):
    slots, outs = rest[:owners], rest[owners : 2 * owners]
    v, v_sems = rest[2 * owners :]
    users_here, _, width = keys.shape
    heads = bias.shape[0]
    size = width // heads
    scale = size ** (-0.5)
    rows, copies = [], []
    for s in range(owners):
        tag = jnp.max(slots[s][:, width:].astype(F32))
        row = jnp.clip(tag.astype(jnp.int32), 0, users_here - 1)
        copy = pltpu.make_async_copy(values.at[row], v.at[s], v_sems.at[s])
        copy.start()
        rows.append(row)
        copies.append(copy)
    for s in range(owners):
        weights = []
        for h in range(heads):
            cut = slice(h * size, (h + 1) * size)
            logits = lax.dot_general(
                slots[s][:, cut],
                keys[rows[s], :, cut],
                (((1,), (1,)), ((), ())),
                preferred_element_type=F32,
            )
            weights.append(silu(logits * scale + bias[h : h + 1, :]).astype(BF16))
        copies[s].wait()
        parts = [
            jnp.dot(w, v[s, :, h * size : (h + 1) * size], preferred_element_type=F32)
            for h, w in enumerate(weights)
        ]
        mixture = jnp.concatenate(parts, axis=1)
        mean = jnp.mean(mixture, axis=1, keepdims=True)
        outs[s][:, :width] = (mixture - mean).astype(BF16)
        outs[s][:, width:] = in_lanes(split3(mean), MOST).astype(BF16)


def gate_kernel(_, x, weights, out_source, score_source, gate_out, base_out, out_w, w, vector, sems):
    rows = x.shape[0]
    width = w.shape[1]
    copies = [
        pltpu.make_async_copy(weights.at[1], w, sems.at[0]),
        pltpu.make_async_copy(out_source, out_w, sems.at[1]),
        pltpu.make_async_copy(score_source, vector, sems.at[2]),
    ]
    for copy in copies:
        copy.start()
    for copy in copies:
        copy.wait()
    gate = silu(jnp.dot(x[...], w[...], preferred_element_type=F32))
    gate_out[...] = gate
    base = jnp.dot(gate.astype(BF16), out_w[...], preferred_element_type=F32)
    base_out[:rows, :] = base.astype(BF16)
    line = lax.broadcasted_iota(jnp.int32, (16, width), 0)
    block = jnp.zeros((16, width), F32)
    for position, piece in enumerate(split3(vector[...])):
        block = jnp.where(line == position, piece, block)
    base_out[rows:, :] = jnp.zeros((16, base_out.shape[1]), BF16)
    base_out[rows:, :width] = block.astype(BF16)


def product_kernel(owners, place, gate, out_weight, *rest):
    slots = rest[:owners]
    full, sent = rest[owners:]
    width = gate.shape[1]
    model = out_weight.shape[1]
    blocks = gate.shape[0] // MOST
    centred, tails = [], []
    for b in range(blocks):
        picked = slots[0][...]
        for s in range(1, owners):
            picked = jnp.where(place[b] == s, slots[s][...], picked)
        picked = picked.astype(F32)
        centred.append(picked[:, :width])
        tails.append(picked[:, width:])
    centred = jnp.concatenate(centred, axis=0)
    mean = joined(jnp.concatenate(tails, axis=0), 0)
    squares = jnp.sum(centred * centred, axis=1, keepdims=True)
    product = jnp.dot(
        (centred * gate[...]).astype(BF16), out_weight[...], preferred_element_type=F32
    )
    tail = in_lanes(split3(mean) + split3(squares), centred.shape[0])
    full[:, :model] = product
    full[:, model:] = tail
    sent[:, :model] = product.astype(BF16)
    sent[:, model:] = tail.astype(BF16)


def score_kernel(parts, block_count, me, x, *rest):
    bases, products, out = rest[:parts], rest[parts : 2 * parts], rest[2 * parts]
    blocks, block_rows = out.shape
    rows, model = x.shape
    width = model // parts
    tails = [p[:, model:].astype(F32) for p in products]
    means = [joined(t, 0) for t in tails]
    squares = sum(joined(t, 3) for t in tails)
    mean = sum(means) / parts
    spread = squares / model + sum((m - mean) * (m - mean) for m in means) / parts
    scale = lax.rsqrt(spread + EPSILON)
    total = sum(p[:, :model].astype(F32) for p in products)
    for m, base in zip(means, bases):
        total = total + (m - mean) * base[:rows, :].astype(F32)
    terms = silu(x[...].astype(F32) + total * scale)
    score = jnp.zeros((rows, 1), F32)
    for c in range(parts):
        vector = jnp.zeros((1, width), F32)
        for s in range(parts):
            pieces = bases[s][rows:, :width].astype(F32)
            whole = pieces[0:1] + pieces[1:2] + pieces[2:3]
            vector = jnp.where((me[0] ^ s) == c, whole, vector)
        score = score + jnp.sum(
            terms[:, c * width : (c + 1) * width] * vector, axis=1, keepdims=True
        )
    place = lax.broadcasted_iota(jnp.int32, (MOST, block_rows), 0)
    lane = lax.broadcasted_iota(jnp.int32, (MOST, block_rows), 1)
    for b in range(blocks):
        keep = (place == lane) & (lane < block_count[b])
        spread_out = jnp.where(keep, score[b * MOST : (b + 1) * MOST], 0.0)
        out[b : b + 1, :] = jnp.sum(spread_out, axis=0, keepdims=True)


def exchange(arrays, axis):
    size = lax.axis_size(axis)
    return [arrays[0]] + [
        lax.ppermute(arrays[s], axis, [(k, k ^ s) for k in range(size)]) for s in range(1, size)
    ]


def local(
    candidates,
    block_user,
    block_count,
    own_map,
    history_key_cache,
    cache_values,
    w_query_unit,
    time_bias,
    output_weight,
    w_score,
):
    owners = lax.axis_size("users")
    parts = lax.axis_size("mp")
    user_index = lax.axis_index("users").astype(jnp.int32).reshape(1)
    model_index = lax.axis_index("mp").astype(jnp.int32).reshape(1)
    blocks, block_rows, model = candidates.shape
    users_here, _, width = history_key_cache.shape
    rows = blocks * MOST
    shape = jax.ShapeDtypeStruct

    def call(kernel, out_shape, in_specs, out_specs, scratch=()):
        return pl.pallas_call(
            kernel,
            out_shape=out_shape,
            in_specs=in_specs,
            out_specs=out_specs,
            scratch_shapes=list(scratch),
            compiler_params=pltpu.CompilerParams(vmem_limit_bytes=8 * 1024 * 1024),
        )

    block_user, own_map, block_count, candidates, w_query_unit, output_weight, score_row, value_cache = (
        pltpu.with_memory_space_constraint(a, pltpu.HBM)
        for a in (
            block_user, own_map, block_count, candidates, w_query_unit, output_weight, w_score.reshape(1, width), cache_values,
        )
    )
    slot = shape((MOST, width + LANES), BF16)
    numbers = shape((blocks,), jnp.int32)
    *slots, x, place, counts = call(
        functools.partial(query_kernel, owners, users_here),
        [slot] * owners + [shape((rows, model), BF16), numbers, numbers],
        [HBM, HBM, HBM, SMEM, HBM, HBM],
        [VMEM] * (owners + 1) + [SMEM, SMEM],
        [
            pltpu.VMEM((model, width), BF16),
            pltpu.SMEM(block_user.shape, jnp.int32),
            pltpu.SMEM(own_map.shape, jnp.int32),
            pltpu.SemaphoreType.DMA((blocks,)),
            pltpu.SemaphoreType.DMA((4,)),
        ],
    )(block_user, own_map, block_count, user_index, candidates, w_query_unit)
    slots = exchange(slots, "users")
    gate, base, out_w = call(
        gate_kernel,
        [
            shape((rows, width), F32),
            shape((rows + 16, model), BF16),
            shape(output_weight.shape, BF16),
        ],
        [VMEM, VMEM, HBM, HBM, HBM],
        [VMEM] * 3,
        [
            pltpu.VMEM((model, width), BF16),
            pltpu.VMEM((1, width), F32),
            pltpu.SemaphoreType.DMA((3,)),
        ],
    )(slots[1], x, w_query_unit, output_weight, score_row)
    bases = exchange([base] * parts, "mp")
    mixtures = call(
        functools.partial(attend_kernel, owners),
        [slot] * owners,
        [VMEM, VMEM, VMEM, HBM] + [VMEM] * owners,
        [VMEM] * owners,
        [
            pltpu.VMEM((owners, *history_key_cache.shape[1:]), BF16),
            pltpu.SemaphoreType.DMA((owners,)),
        ],
    )(gate, time_bias, history_key_cache, value_cache, *slots)
    mixtures = exchange(mixtures, "users")
    product, sent = call(
        functools.partial(product_kernel, owners),
        [shape((rows, model + LANES), F32), shape((rows, model + LANES), BF16)],
        [SMEM] + [VMEM] * (2 + owners),
        [VMEM] * 2,
    )(place, gate, out_w, *mixtures)
    products = [product] + exchange([sent] * parts, "mp")[1:]
    return call(
        functools.partial(score_kernel, parts),
        shape((blocks, block_rows), F32),
        [SMEM, SMEM] + [VMEM] * (1 + 2 * parts),
        VMEM,
    )(counts, model_index, x, *bases, *products)


def solution(mesh):
    return jax.shard_map(
        local,
        mesh=mesh,
        in_specs=(
            P(("groups", "users", "helpers"), None, None),
            P(("groups", "users", "helpers")),
            P(("groups", "users", "helpers")),
            P("groups"),
            P(("groups", "users"), None, "mp"),
            P(("groups", "users"), None, "mp"),
            P(None, None, "mp"),
            P("mp", None),
            P("mp", None),
            P("mp"),
        ),
        out_specs=P(("groups", "users", "helpers"), None),
        check_vma=False,
    )
```

time: 44.6 us -> 31.2 us (0.70)
  local copies, waits for them, and re-layouts: 11.3 us -> 0.01 us
  waiting for transfers between devices: 12.5 us -> 8.32 us
  Pallas kernels: 7.72 us -> 9.5 us
  starting transfers between devices: 12.7 us -> 13.2 us
    unnamed x32 -> x4, local copies, waits for them, and re-layouts: 11.3 us -> 0.01 us
    ppermute x8, waiting for transfers between devices: 12.5 us -> 8.32 us  [exchange(): lax.ppermute(arrays[s], axis, [(k, k ^ s) for k in range(size)])]
    pallas_call x4, Pallas kernels: 6.01 us -> 7.97 us  [the longest x1 2.72 us: local(): call(functools.partial(attend_kernel, owners), [slot] * owners, [VMEM, VM...]
    ppermute x8, starting transfers between devices: 12.7 us -> 13.2 us  [exchange(): lax.ppermute(arrays[s], axis, [(k, k ^ s) for k in range(size)])]
  transfers between devices with their start and end apart: 8 -> 8, of which waited for: 5 -> 5; matrix products, arithmetic and copies ran while one was open for 0% -> 0% of each run, Pallas kernels for 12% -> 10%
where the time goes in v2:
time: 31.2 us; the launch traced here: 31 us
  starting transfers between devices  13.2 us (42%)
  Pallas kernels  9.5 us (30%)
  waiting for transfers between devices  8.32 us (27%)
    ppermute x8, starting transfers between devices, exchange(): lax.ppermute(arrays[s], axis, [(k, k ^ s) for k in range(size)])  13.2 us
    ppermute x8, waiting for transfers between devices, exchange(): lax.ppermute(arrays[s], axis, [(k, k ^ s) for k in range(size)])  8.32 us
    pallas_call x1, Pallas kernels, local(): call(functools.partial(attend_kernel, owners), [slot] * owners, [VMEM, VM...  2.72 us
    pallas_call x1, Pallas kernels, local(): call(functools.partial(query_kernel, owners, users_here), [slot] * owners...  2.22 us
    pallas_call x1, Pallas kernels, local(): call(gate_kernel, [shape((rows, width), F32), shape((rows + 16, model), B...  2.15 us
    pallas_call x1, Pallas kernels, local(): call(functools.partial(score_kernel, parts), shape((blocks, block_rows),...  1.53 us
    pallas_call x1, Pallas kernels, local(): call(functools.partial(product_kernel, owners), [shape((rows, model + LAN...  0.88 us
  transfers between devices with their start and end apart: 8, of which 5 were waited for; matrix products, arithmetic and copies ran while one was open for 0% of the time, Pallas kernels for 10%

profile of v2, /device:TPU:0, one launch (start us, length us, event | category | flops | bytes accessed | tf_op | source)
XLA Modules:
  0.0 31.0 jit_solution(15652281604691909631)
XLA Ops:
  0.0 0.0 copy-start.1
  0.0 0.0 copy-start
  0.0 2.2 %shard_map.100 = (bf16[32,640]{1,0:T(8,128)(2,1)S(1)}, bf16[32,640]{1,0:T(8,128)(2,1)S(1)}, bf16[32,640]{1,0:T(8,128)(2,1)S(1)}, bf16[32,640]{1,0:T(8,128)(2,1)S...) custom-call(s32[2]{0:T(128)} %user_source.1, s32[32]{0:T(128)} %map_source.1, s32[2]{0:T(128)} %count_source.1, ...), custom_call_target="tpu_custom_call" | custom-call | tf_op jit(solution)/shard_map/pallas_call | solution.py:255
  2.2 3.1 %collective-permute-start = (bf16[32,640]{1,0:T(8,128)(2,1)S(1)}, bf16[32,640]{1,0:T(8,128)(2,1)S(1)}, u32[]{:S(2)}, u32[]{:S(2)}) collective-permute-start(bf16[32,640]{1,0:T(8,128)(2,1)S(1)} %get-tuple-element.23), channel_id=1, source_target_pairs={{0,4},{4,0},{8,12},{12,8},{1,5},{5,1},{9,13},{13,9},{2,6},{6,2},{1... | collective-permute-start | bytes 122888 | tf_op jit(solution)/shard_map/ppermute | solution.py:212
  5.3 2.6 %collective-permute-start.2 = (bf16[32,640]{1,0:T(8,128)(2,1)S(1)}, bf16[32,640]{1,0:T(8,128)(2,1)S(1)}, u32[]{:S(2)}, u32[]{:S(2)}) collective-permute-start(bf16[32,640]{1,0:T(8,128)(2,1)S(1)} %get-tuple-element.29), channel_id=1, source_target_pairs={{0,8},{4,12},{8,0},{12,4},{1,9},{5,13},{9,1},{13,5},{2,10},{6,14},... | collective-permute-start | bytes 122888 | tf_op jit(solution)/shard_map/ppermute | solution.py:212
  7.9 0.0 collective-permute-start.3
  7.9 0.0 collective-permute-done._.rest_1_
  7.9 2.1 %shard_map.101 = (f32[64,512]{1,0:T(8,128)S(1)}, bf16[80,1024]{1,0:T(8,128)(2,1)S(1)}, bf16[512,1024]{1,0:T(8,128)(2,1)S(1)}) custom-call(bf16[32,640]{1,0:T(8,128)(2,1)S(1)} %collective-permute-done._.rest_1_, bf16[64,1024]{1,0:T(8,128)(2,1)S(1)} %get-tuple-element.22.x, bf16[2,1024,512]{2,1,0:T(8,128)(2,1)} %weights.3, bf16[512,1024]{1,0:T(8,128)(2,1)} %out_source.1, ...), custom_call_target="tpu_custom_call" | custom-call | tf_op jit(solution)/shard_map/pallas_call | solution.py:269
  10.1 0.9 %collective-permute-done.2.rest_2_ = bf16[32,640]{1,0:T(8,128)(2,1)S(1)} collective-permute-done((bf16[32,640]{1,0:T(8,128)(2,1)S(1)}, bf16[32,640]{1,0:T(8,128)(2,1)S(1)}, u32[]{:S(2)}, u32[]{:S(2)}) %collective-permute-start.2) | collective-permute-done | bytes 40992 | tf_op jit(solution)/shard_map/ppermute | solution.py:212
  11.0 2.7 %collective-permute-done.3.rest_3_ = bf16[32,640]{1,0:T(8,128)(2,1)S(1)} collective-permute-done((bf16[32,640]{1,0:T(8,128)(2,1)S(1)}, bf16[32,640]{1,0:T(8,128)(2,1)S(1)}, u32[]{:S(2)}, u32[]{:S(2)}) %collective-permute-start.3) | collective-permute-done | bytes 40992 | tf_op jit(solution)/shard_map/ppermute | solution.py:212
  13.7 0.0 copy-done.1
  13.7 0.0 copy-done
  13.7 2.7 %shard_map.102 = (bf16[32,640]{1,0:T(8,128)(2,1)S(1)}, bf16[32,640]{1,0:T(8,128)(2,1)S(1)}, bf16[32,640]{1,0:T(8,128)(2,1)S(1)}, bf16[32,640]{1,0:T(8,128)(2,1)S(1)}) custom-call(f32[64,512]{1,0:T(8,128)S(1)} %get-tuple-element.26._.gate, f32[4,512]{1,0:T(4,128)S(1)} %copy-done.1, bf16[8,512,512]{2,1,0:T(8,128)(2,1)S(1)} %copy-done, ...), custom_call_target="tpu_custom_call" | custom-call | tf_op jit(solution)/shard_map/pallas_call | solution.py:285
  16.4 0.1 collective-permute-start.4
  16.5 1.1 %collective-permute-start.5 = (bf16[32,640]{1,0:T(8,128)(2,1)S(1)}, bf16[32,640]{1,0:T(8,128)(2,1)S(1)}, u32[]{:S(2)}, u32[]{:S(2)}) collective-permute-start(bf16[32,640]{1,0:T(8,128)(2,1)S(1)} %get-tuple-element.33), channel_id=1, source_target_pairs={{0,8},{4,12},{8,0},{12,4},{1,9},{5,13},{9,1},{13,5},{2,10},{6,14},... | collective-permute-start | bytes 122888 | tf_op jit(solution)/shard_map/ppermute | solution.py:212
  17.6 3.3 %collective-permute-start.6 = (bf16[32,640]{1,0:T(8,128)(2,1)S(1)}, bf16[32,640]{1,0:T(8,128)(2,1)S(1)}, u32[]{:S(2)}, u32[]{:S(2)}) collective-permute-start(bf16[32,640]{1,0:T(8,128)(2,1)S(1)} %get-tuple-element.34), channel_id=1, source_target_pairs={{0,12},{4,8},{8,4},{12,0},{1,13},{5,9},{9,5},{13,1},{2,14},{6,10},... | collective-permute-start | bytes 122888 | tf_op jit(solution)/shard_map/ppermute | solution.py:212
  20.9 1.5 %collective-permute-start.1 = (bf16[80,1024]{1,0:T(8,128)(2,1)S(1)}, bf16[80,1024]{1,0:T(8,128)(2,1)S(1)}, u32[]{:S(2)}, u32[]{:S(2)}) collective-permute-start(bf16[80,1024]{1,0:T(8,128)(2,1)S(1)} %get-tuple-element.24.rest_0_), channel_id=1, source_target_pairs={{0,2},{2,0},{1,3},{3,1},{4,6},{6,4},{5,7},{7,5},{8,10},{10,8},{9,1... | collective-permute-start | bytes 491528 | tf_op jit(solution)/shard_map/ppermute | solution.py:212
  22.4 0.0 collective-permute-done.4.rest_1_
  22.4 0.0 collective-permute-done.5.rest_2_
  22.4 1.0 %collective-permute-done.6.rest_3_ = bf16[32,640]{1,0:T(8,128)(2,1)S(1)} collective-permute-done((bf16[32,640]{1,0:T(8,128)(2,1)S(1)}, bf16[32,640]{1,0:T(8,128)(2,1)S(1)}, u32[]{:S(2)}, u32[]{:S(2)}) %collective-permute-start.6) | collective-permute-done | bytes 40992 | tf_op jit(solution)/shard_map/ppermute | solution.py:212
  23.4 0.9 %shard_map.103 = (f32[64,1152]{1,0:T(8,128)S(1)}, bf16[64,1152]{1,0:T(8,128)(2,1)S(1)}) custom-call(s32[2]{0:T(128)S(1)} %get-tuple-element.25.place, f32[64,512]{1,0:T(8,128)S(1)} %get-tuple-element.26._.gate, bf16[512,1024]{1,0:T(8,128)(2,1)S(1)} %get-tuple-element.27.out_weight, bf16[32,640]{1,0:T(8,128)(2,1)S(1)} %get-tuple-element.31.rest_0_, ...), custom_call_target="tpu_custom_call" | custom-call | tf_op jit(solution)/shard_map/pallas_call | solution.py:296
  24.3 1.6 %collective-permute-start.7 = (bf16[64,1152]{1,0:T(8,128)(2,1)S(1)}, bf16[64,1152]{1,0:T(8,128)(2,1)S(1)}, u32[]{:S(2)}, u32[]{:S(2)}) collective-permute-start(bf16[64,1152]{1,0:T(8,128)(2,1)S(1)} %get-tuple-element.36), channel_id=1, source_target_pairs={{0,2},{2,0},{1,3},{3,1},{4,6},{6,4},{5,7},{7,5},{8,10},{10,8},{9,1... | collective-permute-start | bytes 442376 | tf_op jit(solution)/shard_map/ppermute | solution.py:212
  25.9 1.6 %collective-permute-done.1.rest_1_ = bf16[80,1024]{1,0:T(8,128)(2,1)S(1)} collective-permute-done((bf16[80,1024]{1,0:T(8,128)(2,1)S(1)}, bf16[80,1024]{1,0:T(8,128)(2,1)S(1)}, u32[]{:S(2)}, u32[]{:S(2)}) %collective-permute-start.1) | collective-permute-done | bytes 163872 | tf_op jit(solution)/shard_map/ppermute | solution.py:212
  27.5 2.0 %collective-permute-done.7.rest_3_ = bf16[64,1152]{1,0:T(8,128)(2,1)S(1)} collective-permute-done((bf16[64,1152]{1,0:T(8,128)(2,1)S(1)}, bf16[64,1152]{1,0:T(8,128)(2,1)S(1)}, u32[]{:S(2)}, u32[]{:S(2)}) %collective-permute-start.7) | collective-permute-done | bytes 147488 | tf_op jit(solution)/shard_map/ppermute | solution.py:212
  29.5 1.5 %shard_map.104 = f32[2,128]{1,0:T(2,128)} custom-call(s32[2]{0:T(128)S(1)} %get-tuple-element.21.block_count, s32[1]{0:T(128)} %bitcast.1.me, bf16[64,1024]{1,0:T(8,128)(2,1)S(1)} %get-tuple-element.22.x, bf16[80,1024]{1,0:T(8,128)(2,1)S(1)} %get-tuple-element.24.rest_0_, bf16[80,1024]{1,0:T(8,128)(2,1)S(1)} %collective-permute-done.1.rest_1_, ...), custom_call_target="tpu_custom_call" | custom-call | tf_op jit(solution)/shard_map/pallas_call | solution.py:303
Async XLA Ops:
  0.0 13.7 %copy-start.1 = (f32[4,512]{1,0:T(4,128)S(1)}, f32[4,512]{1,0:T(4,128)}, u32[]{:S(2)}) copy-start(f32[4,512]{1,0:T(4,128)} %bias.1) | copy-start | bytes 24580
  0.0 13.7 %copy-start = (bf16[8,512,512]{2,1,0:T(8,128)(2,1)S(1)}, bf16[8,512,512]{2,1,0:T(8,128)(2,1)}, u32[]{:S(2)}) copy-start(bf16[8,512,512]{2,1,0:T(8,128)(2,1)} %keys.1) | copy-start | bytes 12582916
  2.2 5.7 %collective-permute-start = (bf16[32,640]{1,0:T(8,128)(2,1)S(1)}, bf16[32,640]{1,0:T(8,128)(2,1)S(1)}, u32[]{:S(2)}, u32[]{:S(2)}) collective-permute-start(bf16[32,640]{1,0:T(8,128)(2,1)S(1)} %get-tuple-element.23), channel_id=1, source_target_pairs={{0,4},{4,0},{8,12},{12,8},{1,5},{5,1},{9,13},{13,9},{2,6},{6,2},{1... | collective-permute-start | bytes 122888 | tf_op jit(solution)/shard_map/ppermute | solution.py:212
  5.3 5.7 %collective-permute-start.2 = (bf16[32,640]{1,0:T(8,128)(2,1)S(1)}, bf16[32,640]{1,0:T(8,128)(2,1)S(1)}, u32[]{:S(2)}, u32[]{:S(2)}) collective-permute-start(bf16[32,640]{1,0:T(8,128)(2,1)S(1)} %get-tuple-element.29), channel_id=1, source_target_pairs={{0,8},{4,12},{8,0},{12,4},{1,9},{5,13},{9,1},{13,5},{2,10},{6,14},... | collective-permute-start | bytes 122888 | tf_op jit(solution)/shard_map/ppermute | solution.py:212
  7.9 5.8 %collective-permute-start.3 = (bf16[32,640]{1,0:T(8,128)(2,1)S(1)}, bf16[32,640]{1,0:T(8,128)(2,1)S(1)}, u32[]{:S(2)}, u32[]{:S(2)}) collective-permute-start(bf16[32,640]{1,0:T(8,128)(2,1)S(1)} %get-tuple-element.30), channel_id=1, source_target_pairs={{0,12},{4,8},{8,4},{12,0},{1,13},{5,9},{9,5},{13,1},{2,14},{6,10},... | collective-permute-start | bytes 122888 | tf_op jit(solution)/shard_map/ppermute | solution.py:212
  16.4 5.9 %collective-permute-start.4 = (bf16[32,640]{1,0:T(8,128)(2,1)S(1)}, bf16[32,640]{1,0:T(8,128)(2,1)S(1)}, u32[]{:S(2)}, u32[]{:S(2)}) collective-permute-start(bf16[32,640]{1,0:T(8,128)(2,1)S(1)} %get-tuple-element.32), channel_id=1, source_target_pairs={{0,4},{4,0},{8,12},{12,8},{1,5},{5,1},{9,13},{13,9},{2,6},{6,2},{1... | collective-permute-start | bytes 122888 | tf_op jit(solution)/shard_map/ppermute | solution.py:212
  16.5 5.9 %collective-permute-start.5 = (bf16[32,640]{1,0:T(8,128)(2,1)S(1)}, bf16[32,640]{1,0:T(8,128)(2,1)S(1)}, u32[]{:S(2)}, u32[]{:S(2)}) collective-permute-start(bf16[32,640]{1,0:T(8,128)(2,1)S(1)} %get-tuple-element.33), channel_id=1, source_target_pairs={{0,8},{4,12},{8,0},{12,4},{1,9},{5,13},{9,1},{13,5},{2,10},{6,14},... | collective-permute-start | bytes 122888 | tf_op jit(solution)/shard_map/ppermute | solution.py:212
  17.6 5.8 %collective-permute-start.6 = (bf16[32,640]{1,0:T(8,128)(2,1)S(1)}, bf16[32,640]{1,0:T(8,128)(2,1)S(1)}, u32[]{:S(2)}, u32[]{:S(2)}) collective-permute-start(bf16[32,640]{1,0:T(8,128)(2,1)S(1)} %get-tuple-element.34), channel_id=1, source_target_pairs={{0,12},{4,8},{8,4},{12,0},{1,13},{5,9},{9,5},{13,1},{2,14},{6,10},... | collective-permute-start | bytes 122888 | tf_op jit(solution)/shard_map/ppermute | solution.py:212
  20.9 6.6 %collective-permute-start.1 = (bf16[80,1024]{1,0:T(8,128)(2,1)S(1)}, bf16[80,1024]{1,0:T(8,128)(2,1)S(1)}, u32[]{:S(2)}, u32[]{:S(2)}) collective-permute-start(bf16[80,1024]{1,0:T(8,128)(2,1)S(1)} %get-tuple-element.24.rest_0_), channel_id=1, source_target_pairs={{0,2},{2,0},{1,3},{3,1},{4,6},{6,4},{5,7},{7,5},{8,10},{10,8},{9,1... | collective-permute-start | bytes 491528 | tf_op jit(solution)/shard_map/ppermute | solution.py:212
  24.3 5.2 %collective-permute-start.7 = (bf16[64,1152]{1,0:T(8,128)(2,1)S(1)}, bf16[64,1152]{1,0:T(8,128)(2,1)S(1)}, u32[]{:S(2)}, u32[]{:S(2)}) collective-permute-start(bf16[64,1152]{1,0:T(8,128)(2,1)S(1)} %get-tuple-element.36), channel_id=1, source_target_pairs={{0,2},{2,0},{1,3},{3,1},{4,6},{6,4},{5,7},{7,5},{8,10},{10,8},{9,1... | collective-permute-start | bytes 442376 | tf_op jit(solution)/shard_map/ppermute | solution.py:212

commit v3 on v2

v3 whole, which is shorter than its diff:
```python
import functools

import jax
import jax.numpy as jnp
from jax import lax
from jax.experimental import pallas as pl
from jax.experimental.pallas import tpu as pltpu
from jax.sharding import PartitionSpec as P

EPSILON = 1e-05
MOST = 32
LANES = 128
TAIL = 16
CHUNKS = 4
F32 = jnp.float32
BF16 = jnp.bfloat16
VMEM = pl.BlockSpec(memory_space=pltpu.VMEM)
HBM = pl.BlockSpec(memory_space=pltpu.HBM)


def silu(v):
    return v / (1.0 + jnp.exp(-v))


def split3(v):
    high = v.astype(BF16).astype(F32)
    rest = v - high
    middle = rest.astype(BF16).astype(F32)
    return high, middle, rest - middle


def in_lanes(columns, rows):
    lane = lax.broadcasted_iota(jnp.int32, (rows, LANES), 1)
    tail = jnp.zeros((rows, LANES), F32)
    for position, column in enumerate(columns):
        tail = jnp.where(lane == position, column, tail)
    return tail


def joined(tail, first):
    return tail[:, first : first + 1] + tail[:, first + 1 : first + 2] + tail[:, first + 2 : first + 3]


def diagonal(width):
    row = lax.broadcasted_iota(jnp.int32, (MOST, width), 0)
    return row == lax.broadcasted_iota(jnp.int32, (MOST, width), 1)


def query_kernel(owners, users_here, heads, user_source, map_source, candidates, weights, *rest):
    slots, (x, notes) = rest[:owners], rest[owners : owners + 2]
    w, block_user, own_map, x_sems, w_sems, sems = rest[owners + 2 :]
    blocks = candidates.shape[0]
    model, width = w.shape
    size = width // heads
    part = model // CHUNKS
    small = [
        pltpu.make_async_copy(user_source, block_user, sems.at[0]),
        pltpu.make_async_copy(map_source, own_map, sems.at[1]),
    ]
    x_copies = [
        pltpu.make_async_copy(
            candidates.at[b, pl.ds(0, MOST)], x.at[pl.ds(b * MOST, MOST)], x_sems.at[b]
        )
        for b in range(blocks)
    ]
    w_copies = [
        pltpu.make_async_copy(
            weights.at[0, pl.ds(i * part, part)], w.at[pl.ds(i * part, part)], w_sems.at[i]
        )
        for i in range(CHUNKS)
    ]
    for copy in small + x_copies + w_copies:
        copy.start()
    for copy in small:
        copy.wait()
    me = lax.axis_index("users")
    homes = []
    for b in range(blocks):
        storage = own_map[block_user[b]]
        homes.append(((storage // users_here) ^ me, storage % users_here))
        notes[b : b + 1, :] = jnp.full((1, LANES), homes[b][0], jnp.int32)
    for copy in x_copies:
        copy.wait()
    query = jnp.zeros((blocks * MOST, width), F32)
    for i, copy in enumerate(w_copies):
        copy.wait()
        cut = slice(i * part, (i + 1) * part)
        query += jnp.dot(x[:, cut], w[cut, :], preferred_element_type=F32)
    query = silu(query).astype(BF16)
    for s in range(owners):
        tag = jnp.zeros((TAIL, size), F32)
        for b, (slot, row) in enumerate(homes):
            tag = jnp.where(slot == s, row.astype(F32), tag)
        for h in range(heads):
            piece = jnp.zeros((MOST, size), BF16)
            for b, (slot, row) in enumerate(homes):
                mine = query[b * MOST : (b + 1) * MOST, h * size : (h + 1) * size]
                piece = jnp.where(slot == s, mine, piece)
            slots[s][h * MOST : (h + 1) * MOST, :] = piece
        slots[s][heads * MOST :, :] = tag.astype(BF16)


def attend_kernel(owners, _, bias, keys, values, *rest):
    slots, outs = rest[:owners][::-1], rest[owners : 2 * owners]
    v, v_sems = rest[2 * owners :]
    users_here, _, width = keys.shape
    heads = bias.shape[0]
    size = width // heads
    scale = size ** (-0.5)
    rows, copies, weights = [], [], []
    for s in range(owners):
        tag = jnp.max(slots[s][heads * MOST :, :].astype(F32))
        row = jnp.clip(tag.astype(jnp.int32), 0, users_here - 1)
        copy = pltpu.make_async_copy(values.at[row], v.at[s], v_sems.at[s])
        copy.start()
        rows.append(row)
        copies.append(copy)
    for s in range(owners):
        for h in range(heads):
            logits = lax.dot_general(
                slots[s][h * MOST : (h + 1) * MOST, :],
                keys[rows[s], :, h * size : (h + 1) * size],
                (((1,), (1,)), ((), ())),
                preferred_element_type=F32,
            )
            weights.append(silu(logits * scale + bias[h : h + 1, :]).astype(BF16))
    mask = diagonal(size)
    for s in range(owners):
        copies[s].wait()
        parts = [
            jnp.dot(
                weights[s * heads + h],
                v[s, :, h * size : (h + 1) * size],
                preferred_element_type=F32,
            )
            for h in range(heads)
        ]
        mean = jnp.sum(sum(parts), axis=1, keepdims=True) / width
        mean = mean.astype(BF16).astype(F32)
        for h, part in enumerate(parts):
            outs[s][h * MOST : (h + 1) * MOST, :] = (part - mean).astype(BF16)
        line = jnp.sum(jnp.where(mask, mean, 0.0), axis=0, keepdims=True)
        outs[s][heads * MOST :, :] = jnp.broadcast_to(line, (TAIL, size)).astype(BF16)


def gate_kernel(
    x, weights, out_source, score_source, count_source, gate_out, base_out, out_w, counts, *rest
):
    w, vector, block_count, sems = rest
    rows = x.shape[0]
    width = w.shape[1]
    model = base_out.shape[1]
    copies = [
        pltpu.make_async_copy(count_source, block_count, sems.at[3]),
        pltpu.make_async_copy(score_source, vector, sems.at[2]),
        pltpu.make_async_copy(weights.at[1], w, sems.at[0]),
        pltpu.make_async_copy(out_source, out_w, sems.at[1]),
    ]
    for copy in copies:
        copy.start()
    copies[0].wait()
    for b in range(block_count.shape[0]):
        counts[b : b + 1, :] = jnp.full((1, LANES), block_count[b], jnp.int32)
    copies[1].wait()
    line = lax.broadcasted_iota(jnp.int32, (TAIL, width), 0)
    block = jnp.zeros((TAIL, width), F32)
    for position, piece in enumerate(split3(vector[...])):
        block = jnp.where(line == position, piece, block)
    block = block.astype(BF16)
    me = lax.axis_index("mp")
    for c in range(model // width):
        base_out[rows:, c * width : (c + 1) * width] = jnp.where(
            me == c, block, jnp.zeros_like(block)
        )
    copies[2].wait()
    gate = silu(jnp.dot(x[...], w[...], preferred_element_type=F32))
    gate_out[...] = gate
    copies[3].wait()
    base = jnp.dot(gate.astype(BF16), out_w[...], preferred_element_type=F32)
    base_out[:rows, :] = base.astype(BF16)


def product_kernel(owners, notes, gate, out_weight, *rest):
    slots = rest[:owners][::-1]
    full, sent = rest[owners:]
    width = gate.shape[1]
    model = out_weight.shape[1]
    blocks = gate.shape[0] // MOST
    size = slots[0].shape[1]
    heads = width // size
    mask = diagonal(size)
    means, squares, gated = [], [], []
    for b in range(blocks):
        place = notes[b : b + 1, :size]
        picked = slots[0][...].astype(F32)
        for s in range(1, owners):
            picked = jnp.where(place == s, slots[s][...].astype(F32), picked)
        parts = [picked[h * MOST : (h + 1) * MOST] for h in range(heads)]
        extra = jnp.sum(sum(parts), axis=1, keepdims=True) / width
        base = jnp.sum(
            jnp.where(mask, picked[heads * MOST : heads * MOST + 1], 0.0), axis=1, keepdims=True
        )
        parts = [part - extra for part in parts]
        means.append(base + extra)
        squares.append(jnp.sum(sum(part * part for part in parts), axis=1, keepdims=True))
        gated.append(
            jnp.concatenate(
                [
                    part * gate[b * MOST : (b + 1) * MOST, h * size : (h + 1) * size]
                    for h, part in enumerate(parts)
                ],
                axis=1,
            )
        )
    mean = jnp.concatenate(means, axis=0)
    square = jnp.concatenate(squares, axis=0)
    product = jnp.dot(
        jnp.concatenate(gated, axis=0).astype(BF16), out_weight[...], preferred_element_type=F32
    )
    tail = in_lanes(split3(mean) + split3(square), mean.shape[0])
    full[:, :model] = product
    full[:, model:] = tail
    sent[:, :model] = product.astype(BF16)
    sent[:, model:] = tail.astype(BF16)


def score_kernel(parts, counts, x, *rest):
    bases, products, out = rest[:parts], rest[parts : 2 * parts], rest[2 * parts]
    blocks, block_rows = out.shape
    rows, model = x.shape
    tails = [p[:, model:].astype(F32) for p in products]
    means = [joined(t, 0) for t in tails]
    squares = sum(joined(t, 3) for t in tails)
    mean = sum(means) / parts
    spread = squares / model + sum((m - mean) * (m - mean) for m in means) / parts
    scale = lax.rsqrt(spread + EPSILON)
    total = sum(p[:, :model].astype(F32) for p in products)
    for m, base in zip(means, bases):
        total = total + (m - mean) * base[:rows, :].astype(F32)
    terms = silu(x[...].astype(F32) + total * scale)
    pieces = sum(base[rows:, :].astype(F32) for base in bases)
    vector = pieces[0:1] + pieces[1:2] + pieces[2:3]
    score = jnp.sum(terms * vector, axis=1, keepdims=True)
    mask = diagonal(block_rows)
    lane = lax.broadcasted_iota(jnp.int32, (1, block_rows), 1)
    for b in range(blocks):
        line = jnp.sum(
            jnp.where(mask, score[b * MOST : (b + 1) * MOST], 0.0), axis=0, keepdims=True
        )
        out[b : b + 1, :] = jnp.where(lane < counts[b : b + 1, :block_rows], line, 0.0)


def swap(arrays, axis, cross=None):
    size = lax.axis_size(axis)
    out = [None] * size
    out[0] = arrays[0]
    for s in range(size - 1, 0, -1):
        if cross is None:
            out[s] = lax.ppermute(arrays[s], axis, [(k, k ^ s) for k in range(size)])
        else:
            cores = lax.axis_size(cross)
            pairs = [
                (k * cores + c, (k ^ s) * cores + cores - 1 - c)
                for k in range(size)
                for c in range(cores)
            ]
            out[s] = lax.ppermute(arrays[s], (axis, cross), pairs)
    return out


def local(
    candidates,
    block_user,
    block_count,
    own_map,
    history_key_cache,
    cache_values,
    w_query_unit,
    time_bias,
    output_weight,
    w_score,
):
    owners = lax.axis_size("users")
    parts = lax.axis_size("mp")
    blocks, block_rows, model = candidates.shape
    users_here, _, width = history_key_cache.shape
    rows = blocks * MOST
    shape = jax.ShapeDtypeStruct

    def call(kernel, out_shape, in_specs, out_specs, scratch=()):
        return pl.pallas_call(
            kernel,
            out_shape=out_shape,
            in_specs=in_specs,
            out_specs=out_specs,
            scratch_shapes=list(scratch),
            compiler_params=pltpu.CompilerParams(vmem_limit_bytes=8 * 1024 * 1024),
        )

    block_user, own_map, block_count, candidates, w_query_unit, output_weight, score_row, value_cache = (
        pltpu.with_memory_space_constraint(a, pltpu.HBM)
        for a in (
            block_user, own_map, block_count, candidates, w_query_unit, output_weight, w_score.reshape(1, width), cache_values,
        )
    )
    heads = time_bias.shape[0]
    slot = shape((heads * MOST + TAIL, width // heads), BF16)
    notes_shape = shape((blocks, LANES), jnp.int32)
    *slots, x, notes = call(
        functools.partial(query_kernel, owners, users_here, heads),
        [slot] * owners + [shape((rows, model), BF16), notes_shape],
        [HBM] * 4,
        [VMEM] * (owners + 2),
        [
            pltpu.VMEM((model, width), BF16),
            pltpu.SMEM(block_user.shape, jnp.int32),
            pltpu.SMEM(own_map.shape, jnp.int32),
            pltpu.SemaphoreType.DMA((blocks,)),
            pltpu.SemaphoreType.DMA((CHUNKS,)),
            pltpu.SemaphoreType.DMA((2,)),
        ],
    )(block_user, own_map, candidates, w_query_unit)
    slots = swap(slots, "users", "helpers")
    gate, base, out_w, counts = call(
        gate_kernel,
        [
            shape((rows, width), F32),
            shape((rows + TAIL, model), BF16),
            shape(output_weight.shape, BF16),
            notes_shape,
        ],
        [VMEM, HBM, HBM, HBM, HBM],
        [VMEM] * 4,
        [
            pltpu.VMEM((model, width), BF16),
            pltpu.VMEM((1, width), F32),
            pltpu.SMEM(block_count.shape, jnp.int32),
            pltpu.SemaphoreType.DMA((4,)),
        ],
    )(x, w_query_unit, output_weight, score_row, block_count)
    bases = swap([base] * parts, "mp")
    mixtures = call(
        functools.partial(attend_kernel, owners),
        [slot] * owners,
        [VMEM, VMEM, VMEM, HBM] + [VMEM] * owners,
        [VMEM] * owners,
        [
            pltpu.VMEM((owners, *history_key_cache.shape[1:]), BF16),
            pltpu.SemaphoreType.DMA((owners,)),
        ],
    )(gate, time_bias, history_key_cache, value_cache, *slots[::-1])
    mixtures = swap(mixtures, "users", "helpers")
    product, sent = call(
        functools.partial(product_kernel, owners),
        [shape((rows, model + LANES), F32), shape((rows, model + LANES), BF16)],
        [VMEM] * (3 + owners),
        [VMEM] * 2,
    )(notes, gate, out_w, *mixtures[::-1])
    products = [product] + swap([sent] * parts, "mp")[1:]
    return call(
        functools.partial(score_kernel, parts),
        shape((blocks, block_rows), F32),
        [VMEM] * (2 + 2 * parts),
        VMEM,
    )(counts, x, *bases, *products)


def solution(mesh):
    return jax.shard_map(
        local,
        mesh=mesh,
        in_specs=(
            P(("groups", "users", "helpers"), None, None),
            P(("groups", "users", "helpers")),
            P(("groups", "users", "helpers")),
            P("groups"),
            P(("groups", "users"), None, "mp"),
            P(("groups", "users"), None, "mp"),
            P(None, None, "mp"),
            P("mp", None),
            P("mp", None),
            P("mp"),
        ),
        out_specs=P(("groups", "users", "helpers"), None),
        check_vma=False,
    )
```

time: 31.2 us -> 28.1 us (0.901)
  Pallas kernels: 9.5 us -> 7.41 us
  waiting for transfers between devices: 8.32 us -> 7.78 us
  starting transfers between devices: 13.2 us -> 12.7 us
    pallas_call x2, Pallas kernels: 4.37 us -> 3.62 us  [the longest x1 1.91 us: local(): call(gate_kernel, [shape((rows, width), F32), shape((rows + TAIL, model),...]
    ppermute x8, waiting for transfers between devices: 8.32 us -> 7.78 us  [the longest x2 4.36 us: swap(): out[s] = lax.ppermute(arrays[s], axis, [(k, k ^ s) for k in range(size)])]
    pallas_call x1, Pallas kernels: 1.53 us -> 1 us  [local(): call(functools.partial(score_kernel, parts), shape((blocks, block_rows),...]
    ppermute x8, starting transfers between devices: 13.2 us -> 12.7 us  [the longest x6 9.59 us: swap(): out[s] = lax.ppermute(arrays[s], (axis, cross), pairs)]
    pallas_call x1, Pallas kernels: 0.88 us -> 0.38 us  [local(): call(functools.partial(product_kernel, owners), [shape((rows, model + LAN...]
  transfers between devices with their start and end apart: 8 -> 8, of which waited for: 5 -> 4; matrix products, arithmetic and copies ran while one was open for 0% -> 0% of each run, Pallas kernels for 10% -> 8%
where the time goes in v3:
time: 28.1 us; the launch traced here: 27.9 us
  starting transfers between devices  12.7 us (45%)
  waiting for transfers between devices  7.78 us (28%)
  Pallas kernels  7.41 us (26%)
    ppermute x6, starting transfers between devices, swap(): out[s] = lax.ppermute(arrays[s], (axis, cross), pairs)  9.59 us
    ppermute x2, waiting for transfers between devices, swap(): out[s] = lax.ppermute(arrays[s], axis, [(k, k ^ s) for k in range(size)])  4.36 us
    ppermute x6, waiting for transfers between devices, swap(): out[s] = lax.ppermute(arrays[s], (axis, cross), pairs)  3.42 us
    ppermute x2, starting transfers between devices, swap(): out[s] = lax.ppermute(arrays[s], axis, [(k, k ^ s) for k in range(size)])  3.06 us
    pallas_call x1, Pallas kernels, local(): call(functools.partial(attend_kernel, owners), [slot] * owners, [VMEM, VM...  2.41 us
    pallas_call x1, Pallas kernels, local(): call(gate_kernel, [shape((rows, width), F32), shape((rows + TAIL, model),...  1.91 us
    pallas_call x1, Pallas kernels, local(): call(functools.partial(query_kernel, owners, users_here, heads), [slot] *...  1.71 us
    pallas_call x1, Pallas kernels, local(): call(functools.partial(score_kernel, parts), shape((blocks, block_rows),...  1 us
  transfers between devices with their start and end apart: 8, of which 4 were waited for; matrix products, arithmetic and copies ran while one was open for 0% of the time, Pallas kernels for 8%

profile of v3, /device:TPU:0, one launch (start us, length us, event | category | flops | bytes accessed | tf_op | source)
XLA Modules:
  0.0 27.9 jit_solution(16040323610746066745)
XLA Ops:
  0.0 0.0 copy-start.1
  0.0 0.0 copy-start
  0.0 1.7 %shard_map.100 = (bf16[144,128]{1,0:T(8,128)(2,1)S(1)}, bf16[144,128]{1,0:T(8,128)(2,1)S(1)}, bf16[144,128]{1,0:T(8,128)(2,1)S(1)}, bf16[144,128]{1,0:T(8,128)(2...) custom-call(s32[2]{0:T(128)} %user_source.1, s32[32]{0:T(128)} %map_source.1, ...), custom_call_target="tpu_custom_call" | custom-call | tf_op jit(solution)/shard_map/pallas_call | solution.py:309
  1.7 4.6 %collective-permute-start.1 = (bf16[144,128]{1,0:T(8,128)(2,1)S(1)}, bf16[144,128]{1,0:T(8,128)(2,1)S(1)}, u32[]{:S(2)}, u32[]{:S(2)}) collective-permute-start(bf16[144,128]{1,0:T(8,128)(2,1)S(1)} %get-tuple-element.27), channel_id=1, source_target_pairs={{0,13},{1,12},{4,9},{5,8},{8,5},{9,4},{12,1},{13,0},{2,15},{3,14},... | collective-permute-start | bytes 110600 | tf_op jit(solution)/shard_map/ppermute | solution.py:267
  6.3 0.0 collective-permute-start.2
  6.3 0.9 %collective-permute-start.3 = (bf16[144,128]{1,0:T(8,128)(2,1)S(1)}, bf16[144,128]{1,0:T(8,128)(2,1)S(1)}, u32[]{:S(2)}, u32[]{:S(2)}) collective-permute-start(bf16[144,128]{1,0:T(8,128)(2,1)S(1)} %get-tuple-element.29), channel_id=1, source_target_pairs={{0,5},{1,4},{4,1},{5,0},{8,13},{9,12},{12,9},{13,8},{2,7},{3,6},{6... | collective-permute-start | bytes 110600 | tf_op jit(solution)/shard_map/ppermute | solution.py:267
  7.2 1.9 %shard_map.101 = (f32[64,512]{1,0:T(8,128)S(1)}, bf16[80,1024]{1,0:T(8,128)(2,1)S(1)}, bf16[512,1024]{1,0:T(8,128)(2,1)S(1)}, s32[2,128]{1,0:T(2,128)S(1)}) custom-call(bf16[64,1024]{1,0:T(8,128)(2,1)S(1)} %get-tuple-element.21.x, bf16[2,1024,512]{2,1,0:T(8,128)(2,1)} %weights.3, bf16[512,1024]{1,0:T(8,128)(2,1)} %out_source.1, f32[1,512]{1,0:T(1,128)} %bitcast.1, ...), custom_call_target="tpu_custom_call" | custom-call | tf_op jit(solution)/shard_map/pallas_call | solution.py:324
  9.1 0.0 collective-permute-done.1.rest_0_
  9.1 1.8 %collective-permute-done.2.rest_1_ = bf16[144,128]{1,0:T(8,128)(2,1)S(1)} collective-permute-done((bf16[144,128]{1,0:T(8,128)(2,1)S(1)}, bf16[144,128]{1,0:T(8,128)(2,1)S(1)}, u32[]{:S(2)}, u32[]{:S(2)}) %collective-permute-start.2) | collective-permute-done | bytes 36896 | tf_op jit(solution)/shard_map/ppermute | solution.py:267
  10.9 0.0 collective-permute-done.3.rest_2_
  10.9 0.0 copy-done.1
  10.9 0.0 copy-done
  10.9 2.4 %shard_map.102 = (bf16[144,128]{1,0:T(8,128)(2,1)S(1)}, bf16[144,128]{1,0:T(8,128)(2,1)S(1)}, bf16[144,128]{1,0:T(8,128)(2,1)S(1)}, bf16[144,128]{1,0:T(8,128)(2,1)S(1)}) custom-call(f32[64,512]{1,0:T(8,128)S(1)} %get-tuple-element.25._.gate, f32[4,512]{1,0:T(4,128)S(1)} %copy-done.1, bf16[8,512,512]{2,1,0:T(8,128)(2,1)S(1)} %copy-done, ...), custom_call_target="tpu_custom_call" | custom-call | tf_op jit(solution)/shard_map/pallas_call | solution.py:342
  13.3 2.0 %collective-permute-start.4 = (bf16[144,128]{1,0:T(8,128)(2,1)S(1)}, bf16[144,128]{1,0:T(8,128)(2,1)S(1)}, u32[]{:S(2)}, u32[]{:S(2)}) collective-permute-start(bf16[144,128]{1,0:T(8,128)(2,1)S(1)} %get-tuple-element.31), channel_id=1, source_target_pairs={{0,13},{1,12},{4,9},{5,8},{8,5},{9,4},{12,1},{13,0},{2,15},{3,14},... | collective-permute-start | bytes 110600 | tf_op jit(solution)/shard_map/ppermute | solution.py:267
  15.3 0.5 %collective-permute-start.5 = (bf16[144,128]{1,0:T(8,128)(2,1)S(1)}, bf16[144,128]{1,0:T(8,128)(2,1)S(1)}, u32[]{:S(2)}, u32[]{:S(2)}) collective-permute-start(bf16[144,128]{1,0:T(8,128)(2,1)S(1)} %get-tuple-element.32), channel_id=1, source_target_pairs={{0,9},{1,8},{4,13},{5,12},{8,1},{9,0},{12,5},{13,4},{2,11},{3,10},... | collective-permute-start | bytes 110600 | tf_op jit(solution)/shard_map/ppermute | solution.py:267
  15.9 1.6 %collective-permute-start.6 = (bf16[144,128]{1,0:T(8,128)(2,1)S(1)}, bf16[144,128]{1,0:T(8,128)(2,1)S(1)}, u32[]{:S(2)}, u32[]{:S(2)}) collective-permute-start(bf16[144,128]{1,0:T(8,128)(2,1)S(1)} %get-tuple-element.33), channel_id=1, source_target_pairs={{0,5},{1,4},{4,1},{5,0},{8,13},{9,12},{12,9},{13,8},{2,7},{3,6},{6... | collective-permute-start | bytes 110600 | tf_op jit(solution)/shard_map/ppermute | solution.py:267
  17.5 1.5 %collective-permute-start = (bf16[80,1024]{1,0:T(8,128)(2,1)S(1)}, bf16[80,1024]{1,0:T(8,128)(2,1)S(1)}, u32[]{:S(2)}, u32[]{:S(2)}) collective-permute-start(bf16[80,1024]{1,0:T(8,128)(2,1)S(1)} %get-tuple-element.23.rest_0_), channel_id=1, source_target_pairs={{0,2},{2,0},{1,3},{3,1},{4,6},{6,4},{5,7},{7,5},{8,10},{10,8},{9,1... | collective-permute-start | bytes 491528 | tf_op jit(solution)/shard_map/ppermute | solution.py:259
  18.9 0.0 collective-permute-done.4.rest_0_
  18.9 1.6 %collective-permute-done.5.rest_1_ = bf16[144,128]{1,0:T(8,128)(2,1)S(1)} collective-permute-done((bf16[144,128]{1,0:T(8,128)(2,1)S(1)}, bf16[144,128]{1,0:T(8,128)(2,1)S(1)}, u32[]{:S(2)}, u32[]{:S(2)}) %collective-permute-start.5) | collective-permute-done | bytes 36896 | tf_op jit(solution)/shard_map/ppermute | solution.py:267
  20.6 0.0 collective-permute-done.6.rest_2_
  20.6 0.4 %shard_map.103 = (f32[64,1152]{1,0:T(8,128)S(1)}, bf16[64,1152]{1,0:T(8,128)(2,1)S(1)}) custom-call(s32[2,128]{1,0:T(2,128)S(1)} %get-tuple-element.24.notes, f32[64,512]{1,0:T(8,128)S(1)} %get-tuple-element.25._.gate, bf16[512,1024]{1,0:T(8,128)(2,1)S(1)} %get-tuple-element.26.out_weight, bf16[144,128]{1,0:T(8,128)(2,1)S(1)} %collective-permute-done.4.rest_0_, ...), custom_call_target="tpu_custom_call" | custom-call | tf_op jit(solution)/shard_map/pallas_call | solution.py:353
  21.0 1.6 %collective-permute-start.7 = (bf16[64,1152]{1,0:T(8,128)(2,1)S(1)}, bf16[64,1152]{1,0:T(8,128)(2,1)S(1)}, u32[]{:S(2)}, u32[]{:S(2)}) collective-permute-start(bf16[64,1152]{1,0:T(8,128)(2,1)S(1)} %get-tuple-element.36), channel_id=1, source_target_pairs={{0,2},{2,0},{1,3},{3,1},{4,6},{6,4},{5,7},{7,5},{8,10},{10,8},{9,1... | collective-permute-start | bytes 442376 | tf_op jit(solution)/shard_map/ppermute | solution.py:259
  22.5 1.2 %collective-permute-done.rest_1_ = bf16[80,1024]{1,0:T(8,128)(2,1)S(1)} collective-permute-done((bf16[80,1024]{1,0:T(8,128)(2,1)S(1)}, bf16[80,1024]{1,0:T(8,128)(2,1)S(1)}, u32[]{:S(2)}, u32[]{:S(2)}) %collective-permute-start) | collective-permute-done | bytes 163872 | tf_op jit(solution)/shard_map/ppermute | solution.py:259
  23.7 3.2 %collective-permute-done.7.rest_3_ = bf16[64,1152]{1,0:T(8,128)(2,1)S(1)} collective-permute-done((bf16[64,1152]{1,0:T(8,128)(2,1)S(1)}, bf16[64,1152]{1,0:T(8,128)(2,1)S(1)}, u32[]{:S(2)}, u32[]{:S(2)}) %collective-permute-start.7) | collective-permute-done | bytes 147488 | tf_op jit(solution)/shard_map/ppermute | solution.py:259
  26.9 1.0 %shard_map.104 = f32[2,128]{1,0:T(2,128)} custom-call(s32[2,128]{1,0:T(2,128)S(1)} %get-tuple-element.22.counts, bf16[64,1024]{1,0:T(8,128)(2,1)S(1)} %get-tuple-element.21.x, bf16[80,1024]{1,0:T(8,128)(2,1)S(1)} %get-tuple-element.23.rest_0_, bf16[80,1024]{1,0:T(8,128)(2,1)S(1)} %collective-permute-done.rest_1_, f32[64,1152]{1,0:T(8,128)S(1)} %get-tuple-element.35.rest_2_, ...), custom_call_target="tpu_custom_call" | custom-call | tf_op jit(solution)/shard_map/pallas_call | solution.py:360
Async XLA Ops:
  0.0 10.9 %copy-start.1 = (f32[4,512]{1,0:T(4,128)S(1)}, f32[4,512]{1,0:T(4,128)}, u32[]{:S(2)}) copy-start(f32[4,512]{1,0:T(4,128)} %bias.1) | copy-start | bytes 24580
  0.0 10.9 %copy-start = (bf16[8,512,512]{2,1,0:T(8,128)(2,1)S(1)}, bf16[8,512,512]{2,1,0:T(8,128)(2,1)}, u32[]{:S(2)}) copy-start(bf16[8,512,512]{2,1,0:T(8,128)(2,1)} %keys.1) | copy-start | bytes 12582916
  1.7 7.4 %collective-permute-start.1 = (bf16[144,128]{1,0:T(8,128)(2,1)S(1)}, bf16[144,128]{1,0:T(8,128)(2,1)S(1)}, u32[]{:S(2)}, u32[]{:S(2)}) collective-permute-start(bf16[144,128]{1,0:T(8,128)(2,1)S(1)} %get-tuple-element.27), channel_id=1, source_target_pairs={{0,13},{1,12},{4,9},{5,8},{8,5},{9,4},{12,1},{13,0},{2,15},{3,14},... | collective-permute-start | bytes 110600 | tf_op jit(solution)/shard_map/ppermute | solution.py:267
  6.3 4.6 %collective-permute-start.2 = (bf16[144,128]{1,0:T(8,128)(2,1)S(1)}, bf16[144,128]{1,0:T(8,128)(2,1)S(1)}, u32[]{:S(2)}, u32[]{:S(2)}) collective-permute-start(bf16[144,128]{1,0:T(8,128)(2,1)S(1)} %get-tuple-element.28), channel_id=1, source_target_pairs={{0,9},{1,8},{4,13},{5,12},{8,1},{9,0},{12,5},{13,4},{2,11},{3,10},... | collective-permute-start | bytes 110600 | tf_op jit(solution)/shard_map/ppermute | solution.py:267
  6.3 4.6 %collective-permute-start.3 = (bf16[144,128]{1,0:T(8,128)(2,1)S(1)}, bf16[144,128]{1,0:T(8,128)(2,1)S(1)}, u32[]{:S(2)}, u32[]{:S(2)}) collective-permute-start(bf16[144,128]{1,0:T(8,128)(2,1)S(1)} %get-tuple-element.29), channel_id=1, source_target_pairs={{0,5},{1,4},{4,1},{5,0},{8,13},{9,12},{12,9},{13,8},{2,7},{3,6},{6... | collective-permute-start | bytes 110600 | tf_op jit(solution)/shard_map/ppermute | solution.py:267
  13.3 5.6 %collective-permute-start.4 = (bf16[144,128]{1,0:T(8,128)(2,1)S(1)}, bf16[144,128]{1,0:T(8,128)(2,1)S(1)}, u32[]{:S(2)}, u32[]{:S(2)}) collective-permute-start(bf16[144,128]{1,0:T(8,128)(2,1)S(1)} %get-tuple-element.31), channel_id=1, source_target_pairs={{0,13},{1,12},{4,9},{5,8},{8,5},{9,4},{12,1},{13,0},{2,15},{3,14},... | collective-permute-start | bytes 110600 | tf_op jit(solution)/shard_map/ppermute | solution.py:267
  15.3 5.2 %collective-permute-start.5 = (bf16[144,128]{1,0:T(8,128)(2,1)S(1)}, bf16[144,128]{1,0:T(8,128)(2,1)S(1)}, u32[]{:S(2)}, u32[]{:S(2)}) collective-permute-start(bf16[144,128]{1,0:T(8,128)(2,1)S(1)} %get-tuple-element.32), channel_id=1, source_target_pairs={{0,9},{1,8},{4,13},{5,12},{8,1},{9,0},{12,5},{13,4},{2,11},{3,10},... | collective-permute-start | bytes 110600 | tf_op jit(solution)/shard_map/ppermute | solution.py:267
  15.9 4.7 %collective-permute-start.6 = (bf16[144,128]{1,0:T(8,128)(2,1)S(1)}, bf16[144,128]{1,0:T(8,128)(2,1)S(1)}, u32[]{:S(2)}, u32[]{:S(2)}) collective-permute-start(bf16[144,128]{1,0:T(8,128)(2,1)S(1)} %get-tuple-element.33), channel_id=1, source_target_pairs={{0,5},{1,4},{4,1},{5,0},{8,13},{9,12},{12,9},{13,8},{2,7},{3,6},{6... | collective-permute-start | bytes 110600 | tf_op jit(solution)/shard_map/ppermute | solution.py:267
  17.5 6.3 %collective-permute-start = (bf16[80,1024]{1,0:T(8,128)(2,1)S(1)}, bf16[80,1024]{1,0:T(8,128)(2,1)S(1)}, u32[]{:S(2)}, u32[]{:S(2)}) collective-permute-start(bf16[80,1024]{1,0:T(8,128)(2,1)S(1)} %get-tuple-element.23.rest_0_), channel_id=1, source_target_pairs={{0,2},{2,0},{1,3},{3,1},{4,6},{6,4},{5,7},{7,5},{8,10},{10,8},{9,1... | collective-permute-start | bytes 491528 | tf_op jit(solution)/shard_map/ppermute | solution.py:259
  21.0 5.9 %collective-permute-start.7 = (bf16[64,1152]{1,0:T(8,128)(2,1)S(1)}, bf16[64,1152]{1,0:T(8,128)(2,1)S(1)}, u32[]{:S(2)}, u32[]{:S(2)}) collective-permute-start(bf16[64,1152]{1,0:T(8,128)(2,1)S(1)} %get-tuple-element.36), channel_id=1, source_target_pairs={{0,2},{2,0},{1,3},{3,1},{4,6},{6,4},{5,7},{7,5},{8,10},{10,8},{9,1... | collective-permute-start | bytes 442376 | tf_op jit(solution)/shard_map/ppermute | solution.py:259

commit v4 on v3

--- a/solution.py
+++ b/solution.py
@@ -29,21 +29,21 @@
     return high, middle, rest - middle
 
 
-def in_lanes(columns, rows):
-    lane = lax.broadcasted_iota(jnp.int32, (rows, LANES), 1)
-    tail = jnp.zeros((rows, LANES), F32)
-    for position, column in enumerate(columns):
-        tail = jnp.where(lane == position, column, tail)
-    return tail
-
-
-def joined(tail, first):
-    return tail[:, first : first + 1] + tail[:, first + 1 : first + 2] + tail[:, first + 2 : first + 3]
-
-
-def diagonal(width):
-    row = lax.broadcasted_iota(jnp.int32, (MOST, width), 0)
-    return row == lax.broadcasted_iota(jnp.int32, (MOST, width), 1)
+def at_lane(shift):
+    row = lax.broadcasted_iota(jnp.int32, (MOST, LANES), 0)
+    return row + shift == lax.broadcasted_iota(jnp.int32, (MOST, LANES), 1)
+
+
+def to_line(column, mask):
+    return jnp.sum(jnp.where(mask, column, 0.0), axis=0, keepdims=True)
+
+
+def to_column(line, mask):
+    return jnp.sum(jnp.where(mask, line, 0.0), axis=1, keepdims=True)
+
+
+def whole_tiles(rows):
+    return -(-rows // TAIL) * TAIL
 
 
 def query_kernel(owners, users_here, heads, user_source, map_source, candidates, weights, *rest):
@@ -100,61 +100,63 @@
         slots[s][heads * MOST :, :] = tag.astype(BF16)
 
 
-def attend_kernel(owners, _, bias, keys, values, *rest):
+def attend_kernel(owners, bias, keys, values, *rest):
     slots, outs = rest[:owners][::-1], rest[owners : 2 * owners]
-    v, v_sems = rest[2 * owners :]
-    users_here, _, width = keys.shape
+    users_here, history, width = keys.shape
     heads = bias.shape[0]
     size = width // heads
     scale = size ** (-0.5)
-    rows, copies, weights = [], [], []
+    rows, weights = [], []
     for s in range(owners):
         tag = jnp.max(slots[s][heads * MOST :, :].astype(F32))
         row = jnp.clip(tag.astype(jnp.int32), 0, users_here - 1)
-        copy = pltpu.make_async_copy(values.at[row], v.at[s], v_sems.at[s])
-        copy.start()
         rows.append(row)
-        copies.append(copy)
+    none = jnp.zeros((MOST, size), BF16)
     for s in range(owners):
-        for h in range(heads):
+        for h in range(0, heads, 2):
+            one = slots[s][h * MOST : (h + 1) * MOST, :]
+            two = slots[s][(h + 1) * MOST : (h + 2) * MOST, :]
+            query = jnp.concatenate(
+                [jnp.concatenate([one, none], axis=1), jnp.concatenate([none, two], axis=1)], axis=0
+            )
             logits = lax.dot_general(
-                slots[s][h * MOST : (h + 1) * MOST, :],
-                keys[rows[s], :, h * size : (h + 1) * size],
+                query,
+                keys[rows[s], :, h * size : (h + 2) * size],
                 (((1,), (1,)), ((), ())),
                 preferred_element_type=F32,
             )
-            weights.append(silu(logits * scale + bias[h : h + 1, :]).astype(BF16))
-    mask = diagonal(size)
+            pair = jnp.concatenate(
+                [jnp.broadcast_to(bias[h + i : h + i + 1, :], (MOST, history)) for i in range(2)]
+            )
+            weights.append(silu(logits * scale + pair).astype(BF16))
+    mask = at_lane(0)
     for s in range(owners):
-        copies[s].wait()
-        parts = [
-            jnp.dot(
-                weights[s * heads + h],
-                v[s, :, h * size : (h + 1) * size],
+        parts = []
+        for h in range(0, heads, 2):
+            mixed = jnp.dot(
+                weights[(s * heads + h) // 2],
+                values[rows[s], :, h * size : (h + 2) * size],
                 preferred_element_type=F32,
             )
-            for h in range(heads)
-        ]
+            parts += [mixed[:MOST, :size], mixed[MOST:, size:]]
         mean = jnp.sum(sum(parts), axis=1, keepdims=True) / width
         mean = mean.astype(BF16).astype(F32)
         for h, part in enumerate(parts):
             outs[s][h * MOST : (h + 1) * MOST, :] = (part - mean).astype(BF16)
-        line = jnp.sum(jnp.where(mask, mean, 0.0), axis=0, keepdims=True)
-        outs[s][heads * MOST :, :] = jnp.broadcast_to(line, (TAIL, size)).astype(BF16)
-
-
-def gate_kernel(
-    x, weights, out_source, score_source, count_source, gate_out, base_out, out_w, counts, *rest
-):
-    w, vector, block_count, sems = rest
+        outs[s][heads * MOST :, :] = jnp.broadcast_to(to_line(mean, mask), (TAIL, size)).astype(BF16)
+
+
+def gate_kernel(x, weights, out_source, score_source, count_source, value_source, *rest):
+    gate_out, base_out, out_w, counts, values, w, vector, block_count, sems = rest
     rows = x.shape[0]
     width = w.shape[1]
-    model = base_out.shape[1]
+    model = out_w.shape[1]
     copies = [
         pltpu.make_async_copy(count_source, block_count, sems.at[3]),
         pltpu.make_async_copy(score_source, vector, sems.at[2]),
         pltpu.make_async_copy(weights.at[1], w, sems.at[0]),
         pltpu.make_async_copy(out_source, out_w, sems.at[1]),
+        pltpu.make_async_copy(value_source, values, sems.at[4]),
     ]
     for copy in copies:
         copy.start()
@@ -162,34 +164,31 @@
     for b in range(block_count.shape[0]):
         counts[b : b + 1, :] = jnp.full((1, LANES), block_count[b], jnp.int32)
     copies[1].wait()
-    line = lax.broadcasted_iota(jnp.int32, (TAIL, width), 0)
-    block = jnp.zeros((TAIL, width), F32)
-    for position, piece in enumerate(split3(vector[...])):
-        block = jnp.where(line == position, piece, block)
-    block = block.astype(BF16)
-    me = lax.axis_index("mp")
-    for c in range(model // width):
-        base_out[rows:, c * width : (c + 1) * width] = jnp.where(
-            me == c, block, jnp.zeros_like(block)
-        )
+    chunks = model // LANES
+    pieces = jnp.concatenate(split3(vector[...]), axis=0).astype(BF16)
+    base_out[chunks * rows :, :] = jnp.zeros((base_out.shape[0] - chunks * rows, LANES), BF16)
+    base_out[chunks * rows : chunks * rows + pieces.shape[0], :] = pieces
     copies[2].wait()
     gate = silu(jnp.dot(x[...], w[...], preferred_element_type=F32))
     gate_out[...] = gate
     copies[3].wait()
     base = jnp.dot(gate.astype(BF16), out_w[...], preferred_element_type=F32)
-    base_out[:rows, :] = base.astype(BF16)
+    for c in range(chunks):
+        base_out[c * rows : (c + 1) * rows, :] = base[:, c * LANES : (c + 1) * LANES].astype(BF16)
+    copies[4].wait()
 
 
 def product_kernel(owners, notes, gate, out_weight, *rest):
     slots = rest[:owners][::-1]
     full, sent = rest[owners:]
-    width = gate.shape[1]
-    model = out_weight.shape[1]
-    blocks = gate.shape[0] // MOST
+    rows, width = gate.shape
+    chunks = out_weight.shape[1] // LANES
+    blocks = rows // MOST
     size = slots[0].shape[1]
     heads = width // size
-    mask = diagonal(size)
-    means, squares, gated = [], [], []
+    group = LANES // MOST
+    lines = [[jnp.zeros((1, LANES), F32)] * 6 for _ in range(-(-blocks // group))]
+    gated = []
     for b in range(blocks):
         place = notes[b : b + 1, :size]
         picked = slots[0][...].astype(F32)
@@ -197,12 +196,12 @@
             picked = jnp.where(place == s, slots[s][...].astype(F32), picked)
         parts = [picked[h * MOST : (h + 1) * MOST] for h in range(heads)]
         extra = jnp.sum(sum(parts), axis=1, keepdims=True) / width
-        base = jnp.sum(
-            jnp.where(mask, picked[heads * MOST : heads * MOST + 1], 0.0), axis=1, keepdims=True
-        )
+        mean = to_column(picked[heads * MOST : heads * MOST + 1], at_lane(0)) + extra
         parts = [part - extra for part in parts]
-        means.append(base + extra)
-        squares.append(jnp.sum(sum(part * part for part in parts), axis=1, keepdims=True))
+        square = jnp.sum(sum(part * part for part in parts), axis=1, keepdims=True)
+        mask = at_lane(b % group * MOST)
+        values = (*split3(to_line(mean, mask)), *split3(to_line(square, mask)))
+        lines[b // group] = [one + two for one, two in zip(lines[b // group], values)]
         gated.append(
             jnp.concatenate(
                 [
@@ -212,42 +211,65 @@
                 axis=1,
             )
         )
-    mean = jnp.concatenate(means, axis=0)
-    square = jnp.concatenate(squares, axis=0)
     product = jnp.dot(
         jnp.concatenate(gated, axis=0).astype(BF16), out_weight[...], preferred_element_type=F32
     )
-    tail = in_lanes(split3(mean) + split3(square), mean.shape[0])
-    full[:, :model] = product
-    full[:, model:] = tail
-    sent[:, :model] = product.astype(BF16)
-    sent[:, model:] = tail.astype(BF16)
+    tail = jnp.concatenate([line for part in lines for line in part], axis=0)
+    for ref, kind in ((full, F32), (sent, BF16)):
+        for c in range(chunks):
+            ref[c * rows : (c + 1) * rows, :] = product[:, c * LANES : (c + 1) * LANES].astype(kind)
+        ref[chunks * rows :, :] = jnp.zeros((ref.shape[0] - chunks * rows, LANES), kind)
+        ref[chunks * rows : chunks * rows + tail.shape[0], :] = tail.astype(kind)
 
 
 def score_kernel(parts, counts, x, *rest):
     bases, products, out = rest[:parts], rest[parts : 2 * parts], rest[2 * parts]
     blocks, block_rows = out.shape
     rows, model = x.shape
-    tails = [p[:, model:].astype(F32) for p in products]
-    means = [joined(t, 0) for t in tails]
-    squares = sum(joined(t, 3) for t in tails)
+    chunks = model // LANES
+    own = chunks // parts
+    group = LANES // MOST
+    means, squares = [], []
+    for p in products:
+        tail = p[chunks * rows :, :].astype(F32)
+        mean, square = [], []
+        for b in range(blocks):
+            mask = at_lane(b % group * MOST)
+            first = b // group * 6
+            line = tail[first : first + 1] + tail[first + 1 : first + 2] + tail[first + 2 : first + 3]
+            mean.append(to_column(line, mask))
+            first += 3
+            line = tail[first : first + 1] + tail[first + 1 : first + 2] + tail[first + 2 : first + 3]
+            square.append(to_column(line, mask))
+        means.append(jnp.concatenate(mean, axis=0))
+        squares.append(jnp.concatenate(square, axis=0))
     mean = sum(means) / parts
-    spread = squares / model + sum((m - mean) * (m - mean) for m in means) / parts
+    offsets = [m - mean for m in means]
+    spread = sum(squares) / model + sum(d * d for d in offsets) / parts
     scale = lax.rsqrt(spread + EPSILON)
-    total = sum(p[:, :model].astype(F32) for p in products)
-    for m, base in zip(means, bases):
-        total = total + (m - mean) * base[:rows, :].astype(F32)
-    terms = silu(x[...].astype(F32) + total * scale)
-    pieces = sum(base[rows:, :].astype(F32) for base in bases)
-    vector = pieces[0:1] + pieces[1:2] + pieces[2:3]
-    score = jnp.sum(terms * vector, axis=1, keepdims=True)
-    mask = diagonal(block_rows)
-    lane = lax.broadcasted_iota(jnp.int32, (1, block_rows), 1)
+    me = lax.axis_index("mp")
+    vectors = [base[chunks * rows : chunks * rows + 3 * own, :].astype(F32) for base in bases]
+    vectors = [v[:own] + v[own : 2 * own] + v[2 * own :] for v in vectors]
+    score = jnp.zeros((rows, LANES), F32)
+    for c in range(chunks):
+        cut = slice(c * rows, (c + 1) * rows)
+        total = sum(p[cut, :].astype(F32) for p in products)
+        for d, base in zip(offsets, bases):
+            total = total + d * base[cut, :].astype(F32)
+        vector = vectors[0][c % own : c % own + 1]
+        for s in range(1, parts):
+            vector = jnp.where((me ^ s) == c // own, vectors[s][c % own : c % own + 1], vector)
+        feature = x[:, c * LANES : (c + 1) * LANES].astype(F32)
+        score = score + silu(feature + total * scale) * vector
+    score = jnp.sum(score, axis=1, keepdims=True)
+    mask = at_lane(0)
+    lane = lax.broadcasted_iota(jnp.int32, (1, LANES), 1)
     for b in range(blocks):
-        line = jnp.sum(
-            jnp.where(mask, score[b * MOST : (b + 1) * MOST], 0.0), axis=0, keepdims=True
-        )
-        out[b : b + 1, :] = jnp.where(lane < counts[b : b + 1, :block_rows], line, 0.0)
+        line = to_line(score[b * MOST : (b + 1) * MOST], mask)
+        line = jnp.where(lane < counts[b : b + 1, :], line, 0.0)
+        out[b : b + 1, :LANES] = line
+        if block_rows > LANES:
+            out[b : b + 1, LANES:] = jnp.zeros((1, block_rows - LANES), F32)
 
 
 def swap(arrays, axis, cross=None):
@@ -300,10 +322,12 @@
     block_user, own_map, block_count, candidates, w_query_unit, output_weight, score_row, value_cache = (
         pltpu.with_memory_space_constraint(a, pltpu.HBM)
         for a in (
-            block_user, own_map, block_count, candidates, w_query_unit, output_weight, w_score.reshape(1, width), cache_values,
+            block_user, own_map, block_count, candidates, w_query_unit, output_weight, w_score.reshape(width // LANES, LANES), cache_values,
         )
     )
     heads = time_bias.shape[0]
+    chunks = model // LANES
+    sums = (chunks * rows + whole_tiles(6 * -(-rows // LANES)), LANES)
     slot = shape((heads * MOST + TAIL, width // heads), BF16)
     notes_shape = shape((blocks, LANES), jnp.int32)
     *slots, x, notes = call(
@@ -321,38 +345,35 @@
         ],
     )(block_user, own_map, candidates, w_query_unit)
     slots = swap(slots, "users", "helpers")
-    gate, base, out_w, counts = call(
+    gate, base, out_w, counts, values = call(
         gate_kernel,
         [
             shape((rows, width), F32),
-            shape((rows + TAIL, model), BF16),
+            shape((chunks * rows + whole_tiles(3 * width // LANES), LANES), BF16),
             shape(output_weight.shape, BF16),
             notes_shape,
+            shape(cache_values.shape, BF16),
         ],
-        [VMEM, HBM, HBM, HBM, HBM],
-        [VMEM] * 4,
+        [VMEM, HBM, HBM, HBM, HBM, HBM],
+        [VMEM] * 5,
         [
             pltpu.VMEM((model, width), BF16),
-            pltpu.VMEM((1, width), F32),
+            pltpu.VMEM((width // LANES, LANES), F32),
             pltpu.SMEM(block_count.shape, jnp.int32),
-            pltpu.SemaphoreType.DMA((4,)),
+            pltpu.SemaphoreType.DMA((5,)),
         ],
-    )(x, w_query_unit, output_weight, score_row, block_count)
+    )(x, w_query_unit, output_weight, score_row, block_count, value_cache)
     bases = swap([base] * parts, "mp")
     mixtures = call(
         functools.partial(attend_kernel, owners),
         [slot] * owners,
-        [VMEM, VMEM, VMEM, HBM] + [VMEM] * owners,
+        [VMEM] * (3 + owners),
         [VMEM] * owners,
-        [
-            pltpu.VMEM((owners, *history_key_cache.shape[1:]), BF16),
-            pltpu.SemaphoreType.DMA((owners,)),
-        ],
-    )(gate, time_bias, history_key_cache, value_cache, *slots[::-1])
+    )(time_bias, history_key_cache, values, *slots[::-1])
     mixtures = swap(mixtures, "users", "helpers")
     product, sent = call(
         functools.partial(product_kernel, owners),
-        [shape((rows, model + LANES), F32), shape((rows, model + LANES), BF16)],
+        [shape(sums, F32), shape(sums, BF16)],
         [VMEM] * (3 + owners),
         [VMEM] * 2,
     )(notes, gate, out_w, *mixtures[::-1])

time: 28.1 us -> 27.1 us (0.964)
  waiting for transfers between devices: 7.78 us -> 7.04 us
    ppermute x6, waiting for transfers between devices: 3.42 us -> 2.96 us  [swap(): out[s] = lax.ppermute(arrays[s], (axis, cross), pairs)]
    ppermute x2, waiting for transfers between devices: 4.36 us -> 4.08 us  [swap(): out[s] = lax.ppermute(arrays[s], axis, [(k, k ^ s) for k in range(size)])]
  transfers between devices with their start and end apart: 8 -> 8, of which waited for: 4 -> 3; matrix products, arithmetic and copies ran while one was open for 0% -> 0% of each run, Pallas kernels for 8% -> 12%
where the time goes in v4:
time: 27.1 us; the launch traced here: 27 us
  starting transfers between devices  12.7 us (47%)
  Pallas kernels  7.2 us (27%)
  waiting for transfers between devices  7.04 us (26%)
    ppermute x6, starting transfers between devices, swap(): out[s] = lax.ppermute(arrays[s], (axis, cross), pairs)  9.58 us
    ppermute x2, waiting for transfers between devices, swap(): out[s] = lax.ppermute(arrays[s], axis, [(k, k ^ s) for k in range(size)])  4.08 us
    ppermute x2, starting transfers between devices, swap(): out[s] = lax.ppermute(arrays[s], axis, [(k, k ^ s) for k in range(size)])  3.08 us
    ppermute x6, waiting for transfers between devices, swap(): out[s] = lax.ppermute(arrays[s], (axis, cross), pairs)  2.96 us
    pallas_call x1, Pallas kernels, local(): call(gate_kernel, [shape((rows, width), F32), shape((chunks * rows + whol...  2.89 us
    pallas_call x1, Pallas kernels, local(): call(functools.partial(query_kernel, owners, users_here, heads), [slot] *...  1.57 us
    pallas_call x1, Pallas kernels, local(): call(functools.partial(attend_kernel, owners), [slot] * owners, [VMEM] *...  1.37 us
    pallas_call x1, Pallas kernels, local(): call(functools.partial(score_kernel, parts), shape((blocks, block_rows),...  0.98 us
  transfers between devices with their start and end apart: 8, of which 3 were waited for; matrix products, arithmetic and copies ran while one was open for 0% of the time, Pallas kernels for 12%

profile of v4, /device:TPU:0, one launch (start us, length us, event | category | flops | bytes accessed | tf_op | source)
XLA Modules:
  0.0 27.0 jit_solution(7882517327899281298)
XLA Ops:
  0.0 1.6 %shard_map.100 = (bf16[144,128]{1,0:T(8,128)(2,1)S(1)}, bf16[144,128]{1,0:T(8,128)(2,1)S(1)}, bf16[144,128]{1,0:T(8,128)(2,1)S(1)}, bf16[144,128]{1,0:T(8,128)(2...) custom-call(s32[2]{0:T(128)} %user_source.1, s32[32]{0:T(128)} %map_source.1, ...), custom_call_target="tpu_custom_call" | custom-call | tf_op jit(solution)/shard_map/pallas_call | solution.py:333
  1.6 0.0 copy-start
  1.6 0.0 copy-start.1
  1.6 4.6 %collective-permute-start.1 = (bf16[144,128]{1,0:T(8,128)(2,1)S(1)}, bf16[144,128]{1,0:T(8,128)(2,1)S(1)}, u32[]{:S(2)}, u32[]{:S(2)}) collective-permute-start(bf16[144,128]{1,0:T(8,128)(2,1)S(1)} %get-tuple-element.29), channel_id=1, source_target_pairs={{0,13},{1,12},{4,9},{5,8},{8,5},{9,4},{12,1},{13,0},{2,15},{3,14},... | collective-permute-start | bytes 110600 | tf_op jit(solution)/shard_map/ppermute | solution.py:289
  6.2 0.0 collective-permute-start.2
  6.2 0.9 %collective-permute-start.3 = (bf16[144,128]{1,0:T(8,128)(2,1)S(1)}, bf16[144,128]{1,0:T(8,128)(2,1)S(1)}, u32[]{:S(2)}, u32[]{:S(2)}) collective-permute-start(bf16[144,128]{1,0:T(8,128)(2,1)S(1)} %get-tuple-element.31), channel_id=1, source_target_pairs={{0,5},{1,4},{4,1},{5,0},{8,13},{9,12},{12,9},{13,8},{2,7},{3,6},{6... | collective-permute-start | bytes 110600 | tf_op jit(solution)/shard_map/ppermute | solution.py:289
  7.1 2.9 %shard_map.101 = (f32[64,512]{1,0:T(8,128)S(1)}, bf16[528,128]{1,0:T(8,128)(2,1)S(1)}, bf16[512,1024]{1,0:T(8,128)(2,1)S(1)}, s32[2,128]{1,0:T(2,128)S(1)}, bf16[8,512,512]{2,1,0:T(8,128)(2,1)S(1)}) custom-call(bf16[64,1024]{1,0:T(8,128)(2,1)S(1)} %get-tuple-element.22.x, bf16[2,1024,512]{2,1,0:T(8,128)(2,1)} %weights.3, bf16[512,1024]{1,0:T(8,128)(2,1)} %out_source.1, ...), custom_call_target="tpu_custom_call" | custom-call | tf_op jit(solution)/shard_map/pallas_call | solution.py:348
  10.0 0.0 collective-permute-done.1.rest_0_
  10.0 0.8 %collective-permute-done.2.rest_1_ = bf16[144,128]{1,0:T(8,128)(2,1)S(1)} collective-permute-done((bf16[144,128]{1,0:T(8,128)(2,1)S(1)}, bf16[144,128]{1,0:T(8,128)(2,1)S(1)}, u32[]{:S(2)}, u32[]{:S(2)}) %collective-permute-start.2) | collective-permute-done | bytes 36896 | tf_op jit(solution)/shard_map/ppermute | solution.py:289
  10.8 0.0 collective-permute-done.3.rest_2_
  10.8 0.0 copy-done
  10.8 0.0 copy-done.1
  10.8 1.4 %shard_map.102 = (bf16[144,128]{1,0:T(8,128)(2,1)S(1)}, bf16[144,128]{1,0:T(8,128)(2,1)S(1)}, bf16[144,128]{1,0:T(8,128)(2,1)S(1)}, bf16[144,128]{1,0:T(8,128)(2,1)S(1)}) custom-call(f32[4,512]{1,0:T(4,128)S(1)} %copy-done.1, bf16[8,512,512]{2,1,0:T(8,128)(2,1)S(1)} %copy-done, bf16[8,512,512]{2,1,0:T(8,128)(2,1)S(1)} %get-tuple-element.28.values, ...), custom_call_target="tpu_custom_call" | custom-call | tf_op jit(solution)/shard_map/pallas_call | solution.py:367
  12.2 2.8 %collective-permute-start.4 = (bf16[144,128]{1,0:T(8,128)(2,1)S(1)}, bf16[144,128]{1,0:T(8,128)(2,1)S(1)}, u32[]{:S(2)}, u32[]{:S(2)}) collective-permute-start(bf16[144,128]{1,0:T(8,128)(2,1)S(1)} %get-tuple-element.33), channel_id=1, source_target_pairs={{0,13},{1,12},{4,9},{5,8},{8,5},{9,4},{12,1},{13,0},{2,15},{3,14},... | collective-permute-start | bytes 110600 | tf_op jit(solution)/shard_map/ppermute | solution.py:289
  14.9 0.0 collective-permute-start.5
  14.9 1.3 %collective-permute-start.6 = (bf16[144,128]{1,0:T(8,128)(2,1)S(1)}, bf16[144,128]{1,0:T(8,128)(2,1)S(1)}, u32[]{:S(2)}, u32[]{:S(2)}) collective-permute-start(bf16[144,128]{1,0:T(8,128)(2,1)S(1)} %get-tuple-element.35), channel_id=1, source_target_pairs={{0,5},{1,4},{4,1},{5,0},{8,13},{9,12},{12,9},{13,8},{2,7},{3,6},{6... | collective-permute-start | bytes 110600 | tf_op jit(solution)/shard_map/ppermute | solution.py:289
  16.3 1.5 %collective-permute-start = (bf16[528,128]{1,0:T(8,128)(2,1)S(1)}, bf16[528,128]{1,0:T(8,128)(2,1)S(1)}, u32[]{:S(2)}, u32[]{:S(2)}) collective-permute-start(bf16[528,128]{1,0:T(8,128)(2,1)S(1)} %get-tuple-element.24.rest_0_), channel_id=1, source_target_pairs={{0,2},{2,0},{1,3},{3,1},{4,6},{6,4},{5,7},{7,5},{8,10},{10,8},{9,1... | collective-permute-start | bytes 405512 | tf_op jit(solution)/shard_map/ppermute | solution.py:281
  17.8 0.0 collective-permute-done.4.rest_0_
  17.8 2.2 %collective-permute-done.5.rest_1_ = bf16[144,128]{1,0:T(8,128)(2,1)S(1)} collective-permute-done((bf16[144,128]{1,0:T(8,128)(2,1)S(1)}, bf16[144,128]{1,0:T(8,128)(2,1)S(1)}, u32[]{:S(2)}, u32[]{:S(2)}) %collective-permute-start.5) | collective-permute-done | bytes 36896 | tf_op jit(solution)/shard_map/ppermute | solution.py:289
  19.9 0.0 collective-permute-done.6.rest_2_
  19.9 0.4 %shard_map.103 = (f32[528,128]{1,0:T(8,128)S(1)}, bf16[528,128]{1,0:T(8,128)(2,1)S(1)}) custom-call(s32[2,128]{1,0:T(2,128)S(1)} %get-tuple-element.25.notes, f32[64,512]{1,0:T(8,128)S(1)} %get-tuple-element.26.gate, bf16[512,1024]{1,0:T(8,128)(2,1)S(1)} %get-tuple-element.27.out_weight, bf16[144,128]{1,0:T(8,128)(2,1)S(1)} %collective-permute-done.4.rest_0_, ...), custom_call_target="tpu_custom_call" | custom-call | tf_op jit(solution)/shard_map/pallas_call | solution.py:374
  20.3 1.6 %collective-permute-start.7 = (bf16[528,128]{1,0:T(8,128)(2,1)S(1)}, bf16[528,128]{1,0:T(8,128)(2,1)S(1)}, u32[]{:S(2)}, u32[]{:S(2)}) collective-permute-start(bf16[528,128]{1,0:T(8,128)(2,1)S(1)} %get-tuple-element.38), channel_id=1, source_target_pairs={{0,2},{2,0},{1,3},{3,1},{4,6},{6,4},{5,7},{7,5},{8,10},{10,8},{9,1... | collective-permute-start | bytes 405512 | tf_op jit(solution)/shard_map/ppermute | solution.py:281
  21.9 0.0 collective-permute-done.rest_1_
  21.9 4.0 %collective-permute-done.7.rest_3_ = bf16[528,128]{1,0:T(8,128)(2,1)S(1)} collective-permute-done((bf16[528,128]{1,0:T(8,128)(2,1)S(1)}, bf16[528,128]{1,0:T(8,128)(2,1)S(1)}, u32[]{:S(2)}, u32[]{:S(2)}) %collective-permute-start.7) | collective-permute-done | bytes 135200 | tf_op jit(solution)/shard_map/ppermute | solution.py:281
  26.0 1.0 %shard_map.104 = f32[2,128]{1,0:T(2,128)} custom-call(s32[2,128]{1,0:T(2,128)S(1)} %get-tuple-element.23.counts, bf16[64,1024]{1,0:T(8,128)(2,1)S(1)} %get-tuple-element.22.x, bf16[528,128]{1,0:T(8,128)(2,1)S(1)} %get-tuple-element.24.rest_0_, bf16[528,128]{1,0:T(8,128)(2,1)S(1)} %collective-permute-done.rest_1_, f32[528,128]{1,0:T(8,128)S(1)} %get-tuple-element.37.rest_2_, ...), custom_call_target="tpu_custom_call" | custom-call | tf_op jit(solution)/shard_map/pallas_call | solution.py:381
Async XLA Ops:
  1.6 9.2 %copy-start = (bf16[8,512,512]{2,1,0:T(8,128)(2,1)S(1)}, bf16[8,512,512]{2,1,0:T(8,128)(2,1)}, u32[]{:S(2)}) copy-start(bf16[8,512,512]{2,1,0:T(8,128)(2,1)} %keys.1) | copy-start | bytes 12582916
  1.6 9.2 %copy-start.1 = (f32[4,512]{1,0:T(4,128)S(1)}, f32[4,512]{1,0:T(4,128)}, u32[]{:S(2)}) copy-start(f32[4,512]{1,0:T(4,128)} %bias.1) | copy-start | bytes 24580
  1.6 8.4 %collective-permute-start.1 = (bf16[144,128]{1,0:T(8,128)(2,1)S(1)}, bf16[144,128]{1,0:T(8,128)(2,1)S(1)}, u32[]{:S(2)}, u32[]{:S(2)}) collective-permute-start(bf16[144,128]{1,0:T(8,128)(2,1)S(1)} %get-tuple-element.29), channel_id=1, source_target_pairs={{0,13},{1,12},{4,9},{5,8},{8,5},{9,4},{12,1},{13,0},{2,15},{3,14},... | collective-permute-start | bytes 110600 | tf_op jit(solution)/shard_map/ppermute | solution.py:289
  6.2 4.6 %collective-permute-start.2 = (bf16[144,128]{1,0:T(8,128)(2,1)S(1)}, bf16[144,128]{1,0:T(8,128)(2,1)S(1)}, u32[]{:S(2)}, u32[]{:S(2)}) collective-permute-start(bf16[144,128]{1,0:T(8,128)(2,1)S(1)} %get-tuple-element.30), channel_id=1, source_target_pairs={{0,9},{1,8},{4,13},{5,12},{8,1},{9,0},{12,5},{13,4},{2,11},{3,10},... | collective-permute-start | bytes 110600 | tf_op jit(solution)/shard_map/ppermute | solution.py:289
  6.2 4.6 %collective-permute-start.3 = (bf16[144,128]{1,0:T(8,128)(2,1)S(1)}, bf16[144,128]{1,0:T(8,128)(2,1)S(1)}, u32[]{:S(2)}, u32[]{:S(2)}) collective-permute-start(bf16[144,128]{1,0:T(8,128)(2,1)S(1)} %get-tuple-element.31), channel_id=1, source_target_pairs={{0,5},{1,4},{4,1},{5,0},{8,13},{9,12},{12,9},{13,8},{2,7},{3,6},{6... | collective-permute-start | bytes 110600 | tf_op jit(solution)/shard_map/ppermute | solution.py:289
  12.2 5.6 %collective-permute-start.4 = (bf16[144,128]{1,0:T(8,128)(2,1)S(1)}, bf16[144,128]{1,0:T(8,128)(2,1)S(1)}, u32[]{:S(2)}, u32[]{:S(2)}) collective-permute-start(bf16[144,128]{1,0:T(8,128)(2,1)S(1)} %get-tuple-element.33), channel_id=1, source_target_pairs={{0,13},{1,12},{4,9},{5,8},{8,5},{9,4},{12,1},{13,0},{2,15},{3,14},... | collective-permute-start | bytes 110600 | tf_op jit(solution)/shard_map/ppermute | solution.py:289
  14.9 5.0 %collective-permute-start.5 = (bf16[144,128]{1,0:T(8,128)(2,1)S(1)}, bf16[144,128]{1,0:T(8,128)(2,1)S(1)}, u32[]{:S(2)}, u32[]{:S(2)}) collective-permute-start(bf16[144,128]{1,0:T(8,128)(2,1)S(1)} %get-tuple-element.34), channel_id=1, source_target_pairs={{0,9},{1,8},{4,13},{5,12},{8,1},{9,0},{12,5},{13,4},{2,11},{3,10},... | collective-permute-start | bytes 110600 | tf_op jit(solution)/shard_map/ppermute | solution.py:289
  14.9 5.0 %collective-permute-start.6 = (bf16[144,128]{1,0:T(8,128)(2,1)S(1)}, bf16[144,128]{1,0:T(8,128)(2,1)S(1)}, u32[]{:S(2)}, u32[]{:S(2)}) collective-permute-start(bf16[144,128]{1,0:T(8,128)(2,1)S(1)} %get-tuple-element.35), channel_id=1, source_target_pairs={{0,5},{1,4},{4,1},{5,0},{8,13},{9,12},{12,9},{13,8},{2,7},{3,6},{6... | collective-permute-start | bytes 110600 | tf_op jit(solution)/shard_map/ppermute | solution.py:289
  16.3 5.7 %collective-permute-start = (bf16[528,128]{1,0:T(8,128)(2,1)S(1)}, bf16[528,128]{1,0:T(8,128)(2,1)S(1)}, u32[]{:S(2)}, u32[]{:S(2)}) collective-permute-start(bf16[528,128]{1,0:T(8,128)(2,1)S(1)} %get-tuple-element.24.rest_0_), channel_id=1, source_target_pairs={{0,2},{2,0},{1,3},{3,1},{4,6},{6,4},{5,7},{7,5},{8,10},{10,8},{9,1... | collective-permute-start | bytes 405512 | tf_op jit(solution)/shard_map/ppermute | solution.py:281
  20.3 5.7 %collective-permute-start.7 = (bf16[528,128]{1,0:T(8,128)(2,1)S(1)}, bf16[528,128]{1,0:T(8,128)(2,1)S(1)}, u32[]{:S(2)}, u32[]{:S(2)}) collective-permute-start(bf16[528,128]{1,0:T(8,128)(2,1)S(1)} %get-tuple-element.38), channel_id=1, source_target_pairs={{0,2},{2,0},{1,3},{3,1},{4,6},{6,4},{5,7},{7,5},{8,10},{10,8},{9,1... | collective-permute-start | bytes 405512 | tf_op jit(solution)/shard_map/ppermute | solution.py:281

commit v5 on v4

--- a/solution.py
+++ b/solution.py
@@ -100,19 +100,19 @@
         slots[s][heads * MOST :, :] = tag.astype(BF16)
 
 
-def attend_kernel(owners, bias, keys, values, *rest):
-    slots, outs = rest[:owners][::-1], rest[owners : 2 * owners]
+def attend_kernel(count, bias, keys, values, *rest):
+    slots, outs = rest[:count], rest[count:]
     users_here, history, width = keys.shape
     heads = bias.shape[0]
     size = width // heads
     scale = size ** (-0.5)
     rows, weights = [], []
-    for s in range(owners):
+    for s in range(count):
         tag = jnp.max(slots[s][heads * MOST :, :].astype(F32))
         row = jnp.clip(tag.astype(jnp.int32), 0, users_here - 1)
         rows.append(row)
     none = jnp.zeros((MOST, size), BF16)
-    for s in range(owners):
+    for s in range(count):
         for h in range(0, heads, 2):
             one = slots[s][h * MOST : (h + 1) * MOST, :]
             two = slots[s][(h + 1) * MOST : (h + 2) * MOST, :]
@@ -130,7 +130,7 @@
             )
             weights.append(silu(logits * scale + pair).astype(BF16))
     mask = at_lane(0)
-    for s in range(owners):
+    for s in range(count):
         parts = []
         for h in range(0, heads, 2):
             mixed = jnp.dot(
@@ -178,8 +178,9 @@
     copies[4].wait()
 
 
-def product_kernel(owners, notes, gate, out_weight, *rest):
-    slots = rest[:owners][::-1]
+def product_kernel(order, notes, gate, out_weight, *rest):
+    owners = len(order)
+    slots = {s: ref for s, ref in zip(order, rest)}
     full, sent = rest[owners:]
     rows, width = gate.shape
     chunks = out_weight.shape[1] // LANES
@@ -364,19 +365,26 @@
         ],
     )(x, w_query_unit, output_weight, score_row, block_count, value_cache)
     bases = swap([base] * parts, "mp")
-    mixtures = call(
-        functools.partial(attend_kernel, owners),
-        [slot] * owners,
-        [VMEM] * (3 + owners),
-        [VMEM] * owners,
-    )(time_bias, history_key_cache, values, *slots[::-1])
+    def attend(order):
+        return call(
+            functools.partial(attend_kernel, len(order)),
+            [slot] * len(order),
+            [VMEM] * (3 + len(order)),
+            [VMEM] * len(order),
+        )(time_bias, history_key_cache, values, *[slots[s] for s in order])
+
+    far_first = list(range(owners - 1, 0, -1))
+    half_first = sorted(far_first, key=lambda s: s != owners // 2)
+    mixtures = dict(zip([0], attend([0])))
+    mixtures.update(zip(half_first, attend(half_first)))
     mixtures = swap(mixtures, "users", "helpers")
+    order = [*far_first, 0]
     product, sent = call(
-        functools.partial(product_kernel, owners),
+        functools.partial(product_kernel, order),
         [shape(sums, F32), shape(sums, BF16)],
         [VMEM] * (3 + owners),
         [VMEM] * 2,
-    )(notes, gate, out_w, *mixtures[::-1])
+    )(notes, gate, out_w, *[mixtures[s] for s in order])
     products = [product] + swap([sent] * parts, "mp")[1:]
     return call(
         functools.partial(score_kernel, parts),

time: 27.1 us -> 26.3 us (0.970)
  waiting for transfers between devices: 7.04 us -> 5.63 us
  Pallas kernels: 7.2 us -> 7.59 us
    ppermute x6, waiting for transfers between devices: 2.96 us -> 1.42 us  [swap(): out[s] = lax.ppermute(arrays[s], (axis, cross), pairs)]
    pallas_call x2 -> x3, Pallas kernels: 1.76 us -> 2.16 us  [the longest x2 1.76 us: attend(): call(functools.partial(attend_kernel, len(order)), [slot] * len(order), [...]
  transfers between devices with their start and end apart: 8 -> 8, of which waited for: 3 -> 5; matrix products, arithmetic and copies ran while one was open for 0% -> 0% of each run, Pallas kernels for 12% -> 15%
where the time goes in v5:
time: 26.3 us; the launch traced here: 26.2 us
  starting transfers between devices  12.9 us (49%)
  Pallas kernels  7.59 us (29%)
  waiting for transfers between devices  5.63 us (21%)
    ppermute x6, starting transfers between devices, swap(): out[s] = lax.ppermute(arrays[s], (axis, cross), pairs)  9.79 us
    ppermute x2, waiting for transfers between devices, swap(): out[s] = lax.ppermute(arrays[s], axis, [(k, k ^ s) for k in range(size)])  4.22 us
    ppermute x2, starting transfers between devices, swap(): out[s] = lax.ppermute(arrays[s], axis, [(k, k ^ s) for k in range(size)])  3.08 us
    pallas_call x1, Pallas kernels, local(): call(gate_kernel, [shape((rows, width), F32), shape((chunks * rows + whol...  2.89 us
    pallas_call x2, Pallas kernels, attend(): call(functools.partial(attend_kernel, len(order)), [slot] * len(order), [...  1.76 us
    pallas_call x1, Pallas kernels, local(): call(functools.partial(query_kernel, owners, users_here, heads), [slot] *...  1.57 us
    ppermute x6, waiting for transfers between devices, swap(): out[s] = lax.ppermute(arrays[s], (axis, cross), pairs)  1.42 us
    pallas_call x1, Pallas kernels, local(): call(functools.partial(score_kernel, parts), shape((blocks, block_rows),...  0.98 us
  transfers between devices with their start and end apart: 8, of which 5 were waited for; matrix products, arithmetic and copies ran while one was open for 0% of the time, Pallas kernels for 15%

profile of v5, /device:TPU:0, one launch (start us, length us, event | category | flops | bytes accessed | tf_op | source)
XLA Modules:
  0.0 26.2 jit_solution(7155785453706854966)
XLA Ops:
  0.0 1.6 %shard_map.100 = (bf16[144,128]{1,0:T(8,128)(2,1)S(1)}, bf16[144,128]{1,0:T(8,128)(2,1)S(1)}, bf16[144,128]{1,0:T(8,128)(2,1)S(1)}, bf16[144,128]{1,0:T(8,128)(2...) custom-call(s32[2]{0:T(128)} %user_source.1, s32[32]{0:T(128)} %map_source.1, ...), custom_call_target="tpu_custom_call" | custom-call | tf_op jit(solution)/shard_map/pallas_call | solution.py:334
  1.6 0.0 copy-start
  1.6 0.0 copy-start.1
  1.6 3.5 %collective-permute-start.1 = (bf16[144,128]{1,0:T(8,128)(2,1)S(1)}, bf16[144,128]{1,0:T(8,128)(2,1)S(1)}, u32[]{:S(2)}, u32[]{:S(2)}) collective-permute-start(bf16[144,128]{1,0:T(8,128)(2,1)S(1)} %get-tuple-element.28), channel_id=1, source_target_pairs={{0,9},{1,8},{4,13},{5,12},{8,1},{9,0},{12,5},{13,4},{2,11},{3,10},... | collective-permute-start | bytes 110600 | tf_op jit(solution)/shard_map/ppermute | solution.py:290
  5.1 1.6 %collective-permute-start.2 = (bf16[144,128]{1,0:T(8,128)(2,1)S(1)}, bf16[144,128]{1,0:T(8,128)(2,1)S(1)}, u32[]{:S(2)}, u32[]{:S(2)}) collective-permute-start(bf16[144,128]{1,0:T(8,128)(2,1)S(1)} %get-tuple-element.29), channel_id=1, source_target_pairs={{0,13},{1,12},{4,9},{5,8},{8,5},{9,4},{12,1},{13,0},{2,15},{3,14},... | collective-permute-start | bytes 110600 | tf_op jit(solution)/shard_map/ppermute | solution.py:290
  6.8 0.2 collective-permute-start.3
  7.0 2.9 %shard_map.101 = (f32[64,512]{1,0:T(8,128)S(1)}, bf16[528,128]{1,0:T(8,128)(2,1)S(1)}, bf16[512,1024]{1,0:T(8,128)(2,1)S(1)}, s32[2,128]{1,0:T(2,128)S(1)}, bf16[8,512,512]{2,1,0:T(8,128)(2,1)S(1)}) custom-call(bf16[64,1024]{1,0:T(8,128)(2,1)S(1)} %get-tuple-element.21.x, bf16[2,1024,512]{2,1,0:T(8,128)(2,1)} %weights.3, bf16[512,1024]{1,0:T(8,128)(2,1)} %out_source.1, ...), custom_call_target="tpu_custom_call" | custom-call | tf_op jit(solution)/shard_map/pallas_call | solution.py:349
  9.9 0.0 collective-permute-done.1.rest_0_
  9.9 0.5 %collective-permute-done.2.rest_1_ = bf16[144,128]{1,0:T(8,128)(2,1)S(1)} collective-permute-done((bf16[144,128]{1,0:T(8,128)(2,1)S(1)}, bf16[144,128]{1,0:T(8,128)(2,1)S(1)}, u32[]{:S(2)}, u32[]{:S(2)}) %collective-permute-start.2) | collective-permute-done | bytes 36896 | tf_op jit(solution)/shard_map/ppermute | solution.py:290
  10.4 0.2 collective-permute-done.3.rest_2_
  10.7 0.0 copy-done
  10.7 0.0 copy-done.1
  10.7 1.1 %shard_map.102 = (bf16[144,128]{1,0:T(8,128)(2,1)S(1)}, bf16[144,128]{1,0:T(8,128)(2,1)S(1)}, bf16[144,128]{1,0:T(8,128)(2,1)S(1)}) custom-call(f32[4,512]{1,0:T(4,128)S(1)} %copy-done.1, bf16[8,512,512]{2,1,0:T(8,128)(2,1)S(1)} %copy-done, bf16[8,512,512]{2,1,0:T(8,128)(2,1)S(1)} %get-tuple-element.27.values, ...), custom_call_target="tpu_custom_call" | custom-call | tf_op jit(solution)/shard_map/pallas_call | solution.py:369
  11.8 2.8 %collective-permute-start.4 = (bf16[144,128]{1,0:T(8,128)(2,1)S(1)}, bf16[144,128]{1,0:T(8,128)(2,1)S(1)}, u32[]{:S(2)}, u32[]{:S(2)}) collective-permute-start(bf16[144,128]{1,0:T(8,128)(2,1)S(1)} %get-tuple-element.31), channel_id=1, source_target_pairs={{0,13},{1,12},{4,9},{5,8},{8,5},{9,4},{12,1},{13,0},{2,15},{3,14},... | collective-permute-start | bytes 110600 | tf_op jit(solution)/shard_map/ppermute | solution.py:290
  14.5 0.0 collective-permute-start.5
  14.5 1.6 %collective-permute-start.6 = (bf16[144,128]{1,0:T(8,128)(2,1)S(1)}, bf16[144,128]{1,0:T(8,128)(2,1)S(1)}, u32[]{:S(2)}, u32[]{:S(2)}) collective-permute-start(bf16[144,128]{1,0:T(8,128)(2,1)S(1)} %get-tuple-element.33), channel_id=1, source_target_pairs={{0,5},{1,4},{4,1},{5,0},{8,13},{9,12},{12,9},{13,8},{2,7},{3,6},{6... | collective-permute-start | bytes 110600 | tf_op jit(solution)/shard_map/ppermute | solution.py:290
  16.2 1.5 %collective-permute-start = (bf16[528,128]{1,0:T(8,128)(2,1)S(1)}, bf16[528,128]{1,0:T(8,128)(2,1)S(1)}, u32[]{:S(2)}, u32[]{:S(2)}) collective-permute-start(bf16[528,128]{1,0:T(8,128)(2,1)S(1)} %get-tuple-element.23.rest_0_), channel_id=1, source_target_pairs={{0,2},{2,0},{1,3},{3,1},{4,6},{6,4},{5,7},{7,5},{8,10},{10,8},{9,1... | collective-permute-start | bytes 405512 | tf_op jit(solution)/shard_map/ppermute | solution.py:282
  17.7 0.7 %shard_map.103.rest_3_ = bf16[144,128]{1,0:T(8,128)(2,1)S(1)} custom-call(f32[4,512]{1,0:T(4,128)S(1)} %copy-done.1, bf16[8,512,512]{2,1,0:T(8,128)(2,1)S(1)} %copy-done, bf16[8,512,512]{2,1,0:T(8,128)(2,1)S(1)} %get-tuple-element.27.values, bf16[144,128]{1,0:T(8,128)(2,1)S(1)} %get-tuple-element.34.rest_0_), custom_call_target="tpu_custom_call" | custom-call | tf_op jit(solution)/shard_map/pallas_call | solution.py:369
  18.4 0.0 collective-permute-done.4.rest_0_
  18.4 0.6 %collective-permute-done.5.rest_1_ = bf16[144,128]{1,0:T(8,128)(2,1)S(1)} collective-permute-done((bf16[144,128]{1,0:T(8,128)(2,1)S(1)}, bf16[144,128]{1,0:T(8,128)(2,1)S(1)}, u32[]{:S(2)}, u32[]{:S(2)}) %collective-permute-start.5) | collective-permute-done | bytes 36896 | tf_op jit(solution)/shard_map/ppermute | solution.py:290
  19.0 0.0 collective-permute-done.6.rest_2_
  19.0 0.4 %shard_map.104 = (f32[528,128]{1,0:T(8,128)S(1)}, bf16[528,128]{1,0:T(8,128)(2,1)S(1)}) custom-call(s32[2,128]{1,0:T(2,128)S(1)} %get-tuple-element.24.notes, f32[64,512]{1,0:T(8,128)S(1)} %get-tuple-element.25.gate, bf16[512,1024]{1,0:T(8,128)(2,1)S(1)} %get-tuple-element.26.out_weight, bf16[144,128]{1,0:T(8,128)(2,1)S(1)} %collective-permute-done.4.rest_0_, ...), custom_call_target="tpu_custom_call" | custom-call | tf_op jit(solution)/shard_map/pallas_call | solution.py:382
  19.4 1.6 %collective-permute-start.7 = (bf16[528,128]{1,0:T(8,128)(2,1)S(1)}, bf16[528,128]{1,0:T(8,128)(2,1)S(1)}, u32[]{:S(2)}, u32[]{:S(2)}) collective-permute-start(bf16[528,128]{1,0:T(8,128)(2,1)S(1)} %get-tuple-element.36), channel_id=1, source_target_pairs={{0,2},{2,0},{1,3},{3,1},{4,6},{6,4},{5,7},{7,5},{8,10},{10,8},{9,1... | collective-permute-start | bytes 405512 | tf_op jit(solution)/shard_map/ppermute | solution.py:282
  21.0 0.6 %collective-permute-done.rest_1_ = bf16[528,128]{1,0:T(8,128)(2,1)S(1)} collective-permute-done((bf16[528,128]{1,0:T(8,128)(2,1)S(1)}, bf16[528,128]{1,0:T(8,128)(2,1)S(1)}, u32[]{:S(2)}, u32[]{:S(2)}) %collective-permute-start) | collective-permute-done | bytes 135200 | tf_op jit(solution)/shard_map/ppermute | solution.py:282
  21.6 3.6 %collective-permute-done.7.rest_3_ = bf16[528,128]{1,0:T(8,128)(2,1)S(1)} collective-permute-done((bf16[528,128]{1,0:T(8,128)(2,1)S(1)}, bf16[528,128]{1,0:T(8,128)(2,1)S(1)}, u32[]{:S(2)}, u32[]{:S(2)}) %collective-permute-start.7) | collective-permute-done | bytes 135200 | tf_op jit(solution)/shard_map/ppermute | solution.py:282
  25.2 1.0 %shard_map.105 = f32[2,128]{1,0:T(2,128)} custom-call(s32[2,128]{1,0:T(2,128)S(1)} %get-tuple-element.22.counts, bf16[64,1024]{1,0:T(8,128)(2,1)S(1)} %get-tuple-element.21.x, bf16[528,128]{1,0:T(8,128)(2,1)S(1)} %get-tuple-element.23.rest_0_, bf16[528,128]{1,0:T(8,128)(2,1)S(1)} %collective-permute-done.rest_1_, f32[528,128]{1,0:T(8,128)S(1)} %get-tuple-element.35.rest_2_, ...), custom_call_target="tpu_custom_call" | custom-call | tf_op jit(solution)/shard_map/pallas_call | solution.py:389
Async XLA Ops:
  1.6 9.1 %copy-start = (bf16[8,512,512]{2,1,0:T(8,128)(2,1)S(1)}, bf16[8,512,512]{2,1,0:T(8,128)(2,1)}, u32[]{:S(2)}) copy-start(bf16[8,512,512]{2,1,0:T(8,128)(2,1)} %keys.3) | copy-start | bytes 12582916
  1.6 9.1 %copy-start.1 = (f32[4,512]{1,0:T(4,128)S(1)}, f32[4,512]{1,0:T(4,128)}, u32[]{:S(2)}) copy-start(f32[4,512]{1,0:T(4,128)} %bias.3) | copy-start | bytes 24580
  1.6 8.3 %collective-permute-start.1 = (bf16[144,128]{1,0:T(8,128)(2,1)S(1)}, bf16[144,128]{1,0:T(8,128)(2,1)S(1)}, u32[]{:S(2)}, u32[]{:S(2)}) collective-permute-start(bf16[144,128]{1,0:T(8,128)(2,1)S(1)} %get-tuple-element.28), channel_id=1, source_target_pairs={{0,9},{1,8},{4,13},{5,12},{8,1},{9,0},{12,5},{13,4},{2,11},{3,10},... | collective-permute-start | bytes 110600 | tf_op jit(solution)/shard_map/ppermute | solution.py:290
  5.1 5.3 %collective-permute-start.2 = (bf16[144,128]{1,0:T(8,128)(2,1)S(1)}, bf16[144,128]{1,0:T(8,128)(2,1)S(1)}, u32[]{:S(2)}, u32[]{:S(2)}) collective-permute-start(bf16[144,128]{1,0:T(8,128)(2,1)S(1)} %get-tuple-element.29), channel_id=1, source_target_pairs={{0,13},{1,12},{4,9},{5,8},{8,5},{9,4},{12,1},{13,0},{2,15},{3,14},... | collective-permute-start | bytes 110600 | tf_op jit(solution)/shard_map/ppermute | solution.py:290
  6.8 3.9 %collective-permute-start.3 = (bf16[144,128]{1,0:T(8,128)(2,1)S(1)}, bf16[144,128]{1,0:T(8,128)(2,1)S(1)}, u32[]{:S(2)}, u32[]{:S(2)}) collective-permute-start(bf16[144,128]{1,0:T(8,128)(2,1)S(1)} %get-tuple-element.30), channel_id=1, source_target_pairs={{0,5},{1,4},{4,1},{5,0},{8,13},{9,12},{12,9},{13,8},{2,7},{3,6},{6... | collective-permute-start | bytes 110600 | tf_op jit(solution)/shard_map/ppermute | solution.py:290
  11.8 6.6 %collective-permute-start.4 = (bf16[144,128]{1,0:T(8,128)(2,1)S(1)}, bf16[144,128]{1,0:T(8,128)(2,1)S(1)}, u32[]{:S(2)}, u32[]{:S(2)}) collective-permute-start(bf16[144,128]{1,0:T(8,128)(2,1)S(1)} %get-tuple-element.31), channel_id=1, source_target_pairs={{0,13},{1,12},{4,9},{5,8},{8,5},{9,4},{12,1},{13,0},{2,15},{3,14},... | collective-permute-start | bytes 110600 | tf_op jit(solution)/shard_map/ppermute | solution.py:290
  14.5 4.5 %collective-permute-start.5 = (bf16[144,128]{1,0:T(8,128)(2,1)S(1)}, bf16[144,128]{1,0:T(8,128)(2,1)S(1)}, u32[]{:S(2)}, u32[]{:S(2)}) collective-permute-start(bf16[144,128]{1,0:T(8,128)(2,1)S(1)} %get-tuple-element.32), channel_id=1, source_target_pairs={{0,9},{1,8},{4,13},{5,12},{8,1},{9,0},{12,5},{13,4},{2,11},{3,10},... | collective-permute-start | bytes 110600 | tf_op jit(solution)/shard_map/ppermute | solution.py:290
  14.5 4.5 %collective-permute-start.6 = (bf16[144,128]{1,0:T(8,128)(2,1)S(1)}, bf16[144,128]{1,0:T(8,128)(2,1)S(1)}, u32[]{:S(2)}, u32[]{:S(2)}) collective-permute-start(bf16[144,128]{1,0:T(8,128)(2,1)S(1)} %get-tuple-element.33), channel_id=1, source_target_pairs={{0,5},{1,4},{4,1},{5,0},{8,13},{9,12},{12,9},{13,8},{2,7},{3,6},{6... | collective-permute-start | bytes 110600 | tf_op jit(solution)/shard_map/ppermute | solution.py:290
  16.2 5.4 %collective-permute-start = (bf16[528,128]{1,0:T(8,128)(2,1)S(1)}, bf16[528,128]{1,0:T(8,128)(2,1)S(1)}, u32[]{:S(2)}, u32[]{:S(2)}) collective-permute-start(bf16[528,128]{1,0:T(8,128)(2,1)S(1)} %get-tuple-element.23.rest_0_), channel_id=1, source_target_pairs={{0,2},{2,0},{1,3},{3,1},{4,6},{6,4},{5,7},{7,5},{8,10},{10,8},{9,1... | collective-permute-start | bytes 405512 | tf_op jit(solution)/shard_map/ppermute | solution.py:282
  19.4 5.8 %collective-permute-start.7 = (bf16[528,128]{1,0:T(8,128)(2,1)S(1)}, bf16[528,128]{1,0:T(8,128)(2,1)S(1)}, u32[]{:S(2)}, u32[]{:S(2)}) collective-permute-start(bf16[528,128]{1,0:T(8,128)(2,1)S(1)} %get-tuple-element.36), channel_id=1, source_target_pairs={{0,2},{2,0},{1,3},{3,1},{4,6},{6,4},{5,7},{7,5},{8,10},{10,8},{9,1... | collective-permute-start | bytes 405512 | tf_op jit(solution)/shard_map/ppermute | solution.py:282

commit v6 on v5

--- a/solution.py
+++ b/solution.py
@@ -40,6 +40,12 @@
 
 def to_column(line, mask):
     return jnp.sum(jnp.where(mask, line, 0.0), axis=1, keepdims=True)
+
+
+def filled(pieces, rows):
+    spare = rows - sum(piece.shape[0] for piece in pieces)
+    none = [jnp.zeros((spare, LANES), F32)] if spare > 0 else []
+    return jnp.concatenate([*pieces, *none], axis=0)
 
 
 def whole_tiles(rows):
@@ -165,9 +171,8 @@
         counts[b : b + 1, :] = jnp.full((1, LANES), block_count[b], jnp.int32)
     copies[1].wait()
     chunks = model // LANES
-    pieces = jnp.concatenate(split3(vector[...]), axis=0).astype(BF16)
-    base_out[chunks * rows :, :] = jnp.zeros((base_out.shape[0] - chunks * rows, LANES), BF16)
-    base_out[chunks * rows : chunks * rows + pieces.shape[0], :] = pieces
+    pieces = filled(split3(vector[...]), base_out.shape[0] - chunks * rows)
+    base_out[chunks * rows :, :] = pieces.astype(BF16)
     copies[2].wait()
     gate = silu(jnp.dot(x[...], w[...], preferred_element_type=F32))
     gate_out[...] = gate
@@ -215,12 +220,11 @@
     product = jnp.dot(
         jnp.concatenate(gated, axis=0).astype(BF16), out_weight[...], preferred_element_type=F32
     )
-    tail = jnp.concatenate([line for part in lines for line in part], axis=0)
+    tail = filled([line for part in lines for line in part], sent.shape[0] - chunks * rows)
     for ref, kind in ((full, F32), (sent, BF16)):
         for c in range(chunks):
             ref[c * rows : (c + 1) * rows, :] = product[:, c * LANES : (c + 1) * LANES].astype(kind)
-        ref[chunks * rows :, :] = jnp.zeros((ref.shape[0] - chunks * rows, LANES), kind)
-        ref[chunks * rows : chunks * rows + tail.shape[0], :] = tail.astype(kind)
+        ref[chunks * rows :, :] = tail.astype(kind)
 
 
 def score_kernel(parts, counts, x, *rest):
@@ -249,8 +253,8 @@
     spread = sum(squares) / model + sum(d * d for d in offsets) / parts
     scale = lax.rsqrt(spread + EPSILON)
     me = lax.axis_index("mp")
-    vectors = [base[chunks * rows : chunks * rows + 3 * own, :].astype(F32) for base in bases]
-    vectors = [v[:own] + v[own : 2 * own] + v[2 * own :] for v in vectors]
+    vectors = [base[chunks * rows :, :].astype(F32) for base in bases]
+    vectors = [v[:own] + v[own : 2 * own] + v[2 * own : 3 * own] for v in vectors]
     score = jnp.zeros((rows, LANES), F32)
     for c in range(chunks):
         cut = slice(c * rows, (c + 1) * rows)
@@ -320,12 +324,13 @@
             compiler_params=pltpu.CompilerParams(vmem_limit_bytes=8 * 1024 * 1024),
         )
 
-    block_user, own_map, block_count, candidates, w_query_unit, output_weight, score_row, value_cache = (
-        pltpu.with_memory_space_constraint(a, pltpu.HBM)
-        for a in (
-            block_user, own_map, block_count, candidates, w_query_unit, output_weight, w_score.reshape(width // LANES, LANES), cache_values,
-        )
-    )
+    def fetched(array):
+        return pltpu.with_memory_space_constraint(array, pltpu.HBM)
+
+    block_user, own_map, block_count = fetched(block_user), fetched(own_map), fetched(block_count)
+    candidates, w_query_unit = fetched(candidates), fetched(w_query_unit)
+    output_weight, value_cache = fetched(output_weight), fetched(cache_values)
+    score_row = fetched(w_score.reshape(width // LANES, LANES))
     heads = time_bias.shape[0]
     chunks = model // LANES
     sums = (chunks * rows + whole_tiles(6 * -(-rows // LANES)), LANES)
@@ -365,6 +370,7 @@
         ],
     )(x, w_query_unit, output_weight, score_row, block_count, value_cache)
     bases = swap([base] * parts, "mp")
+
     def attend(order):
         return call(
             functools.partial(attend_kernel, len(order)),

time: 26.3 us -> 26.3 us (level)
  no operation moved by 1% of the time
where the time goes in v6:
time: 26.3 us; the launch traced here: 26.2 us
  starting transfers between devices  12.9 us (49%)
  Pallas kernels  7.59 us (29%)
  waiting for transfers between devices  5.64 us (21%)
    ppermute x6, starting transfers between devices, swap(): out[s] = lax.ppermute(arrays[s], (axis, cross), pairs)  9.79 us
    ppermute x2, waiting for transfers between devices, swap(): out[s] = lax.ppermute(arrays[s], axis, [(k, k ^ s) for k in range(size)])  4.22 us
    ppermute x2, starting transfers between devices, swap(): out[s] = lax.ppermute(arrays[s], axis, [(k, k ^ s) for k in range(size)])  3.08 us
    pallas_call x1, Pallas kernels, local(): call(gate_kernel, [shape((rows, width), F32), shape((chunks * rows + whol...  2.89 us
    pallas_call x2, Pallas kernels, attend(): call(functools.partial(attend_kernel, len(order)), [slot] * len(order), [...  1.76 us
    pallas_call x1, Pallas kernels, local(): call(functools.partial(query_kernel, owners, users_here, heads), [slot] *...  1.57 us
    ppermute x6, waiting for transfers between devices, swap(): out[s] = lax.ppermute(arrays[s], (axis, cross), pairs)  1.42 us
    pallas_call x1, Pallas kernels, local(): call(functools.partial(score_kernel, parts), shape((blocks, block_rows),...  0.98 us
  transfers between devices with their start and end apart: 8, of which 5 were waited for; matrix products, arithmetic and copies ran while one was open for 0% of the time, Pallas kernels for 15%

profile of v6, /device:TPU:0, one launch (start us, length us, event | category | flops | bytes accessed | tf_op | source)
XLA Modules:
  0.0 26.2 jit_solution(4443462126296749262)
XLA Ops:
  0.0 1.6 %shard_map.100 = (bf16[144,128]{1,0:T(8,128)(2,1)S(1)}, bf16[144,128]{1,0:T(8,128)(2,1)S(1)}, bf16[144,128]{1,0:T(8,128)(2,1)S(1)}, bf16[144,128]{1,0:T(8,128)(2...) custom-call(s32[2]{0:T(128)} %user_source.1, s32[32]{0:T(128)} %map_source.1, ...), custom_call_target="tpu_custom_call" | custom-call | tf_op jit(solution)/shard_map/pallas_call | solution.py:339
  1.6 0.0 copy-start
  1.6 0.0 copy-start.1
  1.6 3.5 %collective-permute-start.1 = (bf16[144,128]{1,0:T(8,128)(2,1)S(1)}, bf16[144,128]{1,0:T(8,128)(2,1)S(1)}, u32[]{:S(2)}, u32[]{:S(2)}) collective-permute-start(bf16[144,128]{1,0:T(8,128)(2,1)S(1)} %get-tuple-element.28), channel_id=1, source_target_pairs={{0,9},{1,8},{4,13},{5,12},{8,1},{9,0},{12,5},{13,4},{2,11},{3,10},... | collective-permute-start | bytes 110600 | tf_op jit(solution)/shard_map/ppermute | solution.py:294
  5.1 1.6 %collective-permute-start.2 = (bf16[144,128]{1,0:T(8,128)(2,1)S(1)}, bf16[144,128]{1,0:T(8,128)(2,1)S(1)}, u32[]{:S(2)}, u32[]{:S(2)}) collective-permute-start(bf16[144,128]{1,0:T(8,128)(2,1)S(1)} %get-tuple-element.29), channel_id=1, source_target_pairs={{0,13},{1,12},{4,9},{5,8},{8,5},{9,4},{12,1},{13,0},{2,15},{3,14},... | collective-permute-start | bytes 110600 | tf_op jit(solution)/shard_map/ppermute | solution.py:294
  6.8 0.2 collective-permute-start.3
  7.0 2.9 %shard_map.101 = (f32[64,512]{1,0:T(8,128)S(1)}, bf16[528,128]{1,0:T(8,128)(2,1)S(1)}, bf16[512,1024]{1,0:T(8,128)(2,1)S(1)}, s32[2,128]{1,0:T(2,128)S(1)}, bf16[8,512,512]{2,1,0:T(8,128)(2,1)S(1)}) custom-call(bf16[64,1024]{1,0:T(8,128)(2,1)S(1)} %get-tuple-element.21.x, bf16[2,1024,512]{2,1,0:T(8,128)(2,1)} %weights.3, bf16[512,1024]{1,0:T(8,128)(2,1)} %out_source.1, ...), custom_call_target="tpu_custom_call" | custom-call | tf_op jit(solution)/shard_map/pallas_call | solution.py:354
  9.9 0.0 collective-permute-done.1.rest_0_
  9.9 0.5 %collective-permute-done.2.rest_1_ = bf16[144,128]{1,0:T(8,128)(2,1)S(1)} collective-permute-done((bf16[144,128]{1,0:T(8,128)(2,1)S(1)}, bf16[144,128]{1,0:T(8,128)(2,1)S(1)}, u32[]{:S(2)}, u32[]{:S(2)}) %collective-permute-start.2) | collective-permute-done | bytes 36896 | tf_op jit(solution)/shard_map/ppermute | solution.py:294
  10.4 0.2 collective-permute-done.3.rest_2_
  10.7 0.0 copy-done
  10.7 0.0 copy-done.1
  10.7 1.1 %shard_map.102 = (bf16[144,128]{1,0:T(8,128)(2,1)S(1)}, bf16[144,128]{1,0:T(8,128)(2,1)S(1)}, bf16[144,128]{1,0:T(8,128)(2,1)S(1)}) custom-call(f32[4,512]{1,0:T(4,128)S(1)} %copy-done.1, bf16[8,512,512]{2,1,0:T(8,128)(2,1)S(1)} %copy-done, bf16[8,512,512]{2,1,0:T(8,128)(2,1)S(1)} %get-tuple-element.27.values, ...), custom_call_target="tpu_custom_call" | custom-call | tf_op jit(solution)/shard_map/pallas_call | solution.py:375
  11.8 2.8 %collective-permute-start.4 = (bf16[144,128]{1,0:T(8,128)(2,1)S(1)}, bf16[144,128]{1,0:T(8,128)(2,1)S(1)}, u32[]{:S(2)}, u32[]{:S(2)}) collective-permute-start(bf16[144,128]{1,0:T(8,128)(2,1)S(1)} %get-tuple-element.31), channel_id=1, source_target_pairs={{0,13},{1,12},{4,9},{5,8},{8,5},{9,4},{12,1},{13,0},{2,15},{3,14},... | collective-permute-start | bytes 110600 | tf_op jit(solution)/shard_map/ppermute | solution.py:294
  14.5 0.0 collective-permute-start.5
  14.5 1.6 %collective-permute-start.6 = (bf16[144,128]{1,0:T(8,128)(2,1)S(1)}, bf16[144,128]{1,0:T(8,128)(2,1)S(1)}, u32[]{:S(2)}, u32[]{:S(2)}) collective-permute-start(bf16[144,128]{1,0:T(8,128)(2,1)S(1)} %get-tuple-element.33), channel_id=1, source_target_pairs={{0,5},{1,4},{4,1},{5,0},{8,13},{9,12},{12,9},{13,8},{2,7},{3,6},{6... | collective-permute-start | bytes 110600 | tf_op jit(solution)/shard_map/ppermute | solution.py:294
  16.2 1.5 %collective-permute-start = (bf16[528,128]{1,0:T(8,128)(2,1)S(1)}, bf16[528,128]{1,0:T(8,128)(2,1)S(1)}, u32[]{:S(2)}, u32[]{:S(2)}) collective-permute-start(bf16[528,128]{1,0:T(8,128)(2,1)S(1)} %get-tuple-element.23.rest_0_), channel_id=1, source_target_pairs={{0,2},{2,0},{1,3},{3,1},{4,6},{6,4},{5,7},{7,5},{8,10},{10,8},{9,1... | collective-permute-start | bytes 405512 | tf_op jit(solution)/shard_map/ppermute | solution.py:286
  17.7 0.7 %shard_map.103.rest_3_ = bf16[144,128]{1,0:T(8,128)(2,1)S(1)} custom-call(f32[4,512]{1,0:T(4,128)S(1)} %copy-done.1, bf16[8,512,512]{2,1,0:T(8,128)(2,1)S(1)} %copy-done, bf16[8,512,512]{2,1,0:T(8,128)(2,1)S(1)} %get-tuple-element.27.values, bf16[144,128]{1,0:T(8,128)(2,1)S(1)} %get-tuple-element.34.rest_0_), custom_call_target="tpu_custom_call" | custom-call | tf_op jit(solution)/shard_map/pallas_call | solution.py:375
  18.4 0.0 collective-permute-done.4.rest_0_
  18.4 0.6 %collective-permute-done.5.rest_1_ = bf16[144,128]{1,0:T(8,128)(2,1)S(1)} collective-permute-done((bf16[144,128]{1,0:T(8,128)(2,1)S(1)}, bf16[144,128]{1,0:T(8,128)(2,1)S(1)}, u32[]{:S(2)}, u32[]{:S(2)}) %collective-permute-start.5) | collective-permute-done | bytes 36896 | tf_op jit(solution)/shard_map/ppermute | solution.py:294
  19.0 0.0 collective-permute-done.6.rest_2_
  19.0 0.4 %shard_map.104 = (f32[528,128]{1,0:T(8,128)S(1)}, bf16[528,128]{1,0:T(8,128)(2,1)S(1)}) custom-call(s32[2,128]{1,0:T(2,128)S(1)} %get-tuple-element.24.notes, f32[64,512]{1,0:T(8,128)S(1)} %get-tuple-element.25.gate, bf16[512,1024]{1,0:T(8,128)(2,1)S(1)} %get-tuple-element.26.out_weight, bf16[144,128]{1,0:T(8,128)(2,1)S(1)} %collective-permute-done.4.rest_0_, ...), custom_call_target="tpu_custom_call" | custom-call | tf_op jit(solution)/shard_map/pallas_call | solution.py:388
  19.4 1.6 %collective-permute-start.7 = (bf16[528,128]{1,0:T(8,128)(2,1)S(1)}, bf16[528,128]{1,0:T(8,128)(2,1)S(1)}, u32[]{:S(2)}, u32[]{:S(2)}) collective-permute-start(bf16[528,128]{1,0:T(8,128)(2,1)S(1)} %get-tuple-element.36), channel_id=1, source_target_pairs={{0,2},{2,0},{1,3},{3,1},{4,6},{6,4},{5,7},{7,5},{8,10},{10,8},{9,1... | collective-permute-start | bytes 405512 | tf_op jit(solution)/shard_map/ppermute | solution.py:286
  21.0 0.6 %collective-permute-done.rest_1_ = bf16[528,128]{1,0:T(8,128)(2,1)S(1)} collective-permute-done((bf16[528,128]{1,0:T(8,128)(2,1)S(1)}, bf16[528,128]{1,0:T(8,128)(2,1)S(1)}, u32[]{:S(2)}, u32[]{:S(2)}) %collective-permute-start) | collective-permute-done | bytes 135200 | tf_op jit(solution)/shard_map/ppermute | solution.py:286
  21.6 3.6 %collective-permute-done.7.rest_3_ = bf16[528,128]{1,0:T(8,128)(2,1)S(1)} collective-permute-done((bf16[528,128]{1,0:T(8,128)(2,1)S(1)}, bf16[528,128]{1,0:T(8,128)(2,1)S(1)}, u32[]{:S(2)}, u32[]{:S(2)}) %collective-permute-start.7) | collective-permute-done | bytes 135200 | tf_op jit(solution)/shard_map/ppermute | solution.py:286
  25.2 1.0 %shard_map.105 = f32[2,128]{1,0:T(2,128)} custom-call(s32[2,128]{1,0:T(2,128)S(1)} %get-tuple-element.22.counts, bf16[64,1024]{1,0:T(8,128)(2,1)S(1)} %get-tuple-element.21.x, bf16[528,128]{1,0:T(8,128)(2,1)S(1)} %get-tuple-element.23.rest_0_, bf16[528,128]{1,0:T(8,128)(2,1)S(1)} %collective-permute-done.rest_1_, f32[528,128]{1,0:T(8,128)S(1)} %get-tuple-element.35.rest_2_, ...), custom_call_target="tpu_custom_call" | custom-call | tf_op jit(solution)/shard_map/pallas_call | solution.py:395
Async XLA Ops:
  1.6 9.1 %copy-start = (bf16[8,512,512]{2,1,0:T(8,128)(2,1)S(1)}, bf16[8,512,512]{2,1,0:T(8,128)(2,1)}, u32[]{:S(2)}) copy-start(bf16[8,512,512]{2,1,0:T(8,128)(2,1)} %keys.3) | copy-start | bytes 12582916
  1.6 9.1 %copy-start.1 = (f32[4,512]{1,0:T(4,128)S(1)}, f32[4,512]{1,0:T(4,128)}, u32[]{:S(2)}) copy-start(f32[4,512]{1,0:T(4,128)} %bias.3) | copy-start | bytes 24580
  1.6 8.3 %collective-permute-start.1 = (bf16[144,128]{1,0:T(8,128)(2,1)S(1)}, bf16[144,128]{1,0:T(8,128)(2,1)S(1)}, u32[]{:S(2)}, u32[]{:S(2)}) collective-permute-start(bf16[144,128]{1,0:T(8,128)(2,1)S(1)} %get-tuple-element.28), channel_id=1, source_target_pairs={{0,9},{1,8},{4,13},{5,12},{8,1},{9,0},{12,5},{13,4},{2,11},{3,10},... | collective-permute-start | bytes 110600 | tf_op jit(solution)/shard_map/ppermute | solution.py:294
  5.1 5.3 %collective-permute-start.2 = (bf16[144,128]{1,0:T(8,128)(2,1)S(1)}, bf16[144,128]{1,0:T(8,128)(2,1)S(1)}, u32[]{:S(2)}, u32[]{:S(2)}) collective-permute-start(bf16[144,128]{1,0:T(8,128)(2,1)S(1)} %get-tuple-element.29), channel_id=1, source_target_pairs={{0,13},{1,12},{4,9},{5,8},{8,5},{9,4},{12,1},{13,0},{2,15},{3,14},... | collective-permute-start | bytes 110600 | tf_op jit(solution)/shard_map/ppermute | solution.py:294
  6.8 3.9 %collective-permute-start.3 = (bf16[144,128]{1,0:T(8,128)(2,1)S(1)}, bf16[144,128]{1,0:T(8,128)(2,1)S(1)}, u32[]{:S(2)}, u32[]{:S(2)}) collective-permute-start(bf16[144,128]{1,0:T(8,128)(2,1)S(1)} %get-tuple-element.30), channel_id=1, source_target_pairs={{0,5},{1,4},{4,1},{5,0},{8,13},{9,12},{12,9},{13,8},{2,7},{3,6},{6... | collective-permute-start | bytes 110600 | tf_op jit(solution)/shard_map/ppermute | solution.py:294
  11.8 6.6 %collective-permute-start.4 = (bf16[144,128]{1,0:T(8,128)(2,1)S(1)}, bf16[144,128]{1,0:T(8,128)(2,1)S(1)}, u32[]{:S(2)}, u32[]{:S(2)}) collective-permute-start(bf16[144,128]{1,0:T(8,128)(2,1)S(1)} %get-tuple-element.31), channel_id=1, source_target_pairs={{0,13},{1,12},{4,9},{5,8},{8,5},{9,4},{12,1},{13,0},{2,15},{3,14},... | collective-permute-start | bytes 110600 | tf_op jit(solution)/shard_map/ppermute | solution.py:294
  14.5 4.5 %collective-permute-start.5 = (bf16[144,128]{1,0:T(8,128)(2,1)S(1)}, bf16[144,128]{1,0:T(8,128)(2,1)S(1)}, u32[]{:S(2)}, u32[]{:S(2)}) collective-permute-start(bf16[144,128]{1,0:T(8,128)(2,1)S(1)} %get-tuple-element.32), channel_id=1, source_target_pairs={{0,9},{1,8},{4,13},{5,12},{8,1},{9,0},{12,5},{13,4},{2,11},{3,10},... | collective-permute-start | bytes 110600 | tf_op jit(solution)/shard_map/ppermute | solution.py:294
  14.5 4.5 %collective-permute-start.6 = (bf16[144,128]{1,0:T(8,128)(2,1)S(1)}, bf16[144,128]{1,0:T(8,128)(2,1)S(1)}, u32[]{:S(2)}, u32[]{:S(2)}) collective-permute-start(bf16[144,128]{1,0:T(8,128)(2,1)S(1)} %get-tuple-element.33), channel_id=1, source_target_pairs={{0,5},{1,4},{4,1},{5,0},{8,13},{9,12},{12,9},{13,8},{2,7},{3,6},{6... | collective-permute-start | bytes 110600 | tf_op jit(solution)/shard_map/ppermute | solution.py:294
  16.2 5.4 %collective-permute-start = (bf16[528,128]{1,0:T(8,128)(2,1)S(1)}, bf16[528,128]{1,0:T(8,128)(2,1)S(1)}, u32[]{:S(2)}, u32[]{:S(2)}) collective-permute-start(bf16[528,128]{1,0:T(8,128)(2,1)S(1)} %get-tuple-element.23.rest_0_), channel_id=1, source_target_pairs={{0,2},{2,0},{1,3},{3,1},{4,6},{6,4},{5,7},{7,5},{8,10},{10,8},{9,1... | collective-permute-start | bytes 405512 | tf_op jit(solution)/shard_map/ppermute | solution.py:286
  19.4 5.8 %collective-permute-start.7 = (bf16[528,128]{1,0:T(8,128)(2,1)S(1)}, bf16[528,128]{1,0:T(8,128)(2,1)S(1)}, u32[]{:S(2)}, u32[]{:S(2)}) collective-permute-start(bf16[528,128]{1,0:T(8,128)(2,1)S(1)} %get-tuple-element.36), channel_id=1, source_target_pairs={{0,2},{2,0},{1,3},{3,1},{4,6},{6,4},{5,7},{7,5},{8,10},{10,8},{9,1... | collective-permute-start | bytes 405512 | tf_op jit(solution)/shard_map/ppermute | solution.py:286

commit v7 on v6

--- a/solution.py
+++ b/solution.py
@@ -193,7 +193,7 @@
     size = slots[0].shape[1]
     heads = width // size
     group = LANES // MOST
-    lines = [[jnp.zeros((1, LANES), F32)] * 6 for _ in range(-(-blocks // group))]
+    lines = [[jnp.zeros((1, LANES), F32)] * 7 for _ in range(-(-blocks // group))]
     gated = []
     for b in range(blocks):
         place = notes[b : b + 1, :size]
@@ -201,12 +201,15 @@
         for s in range(1, owners):
             picked = jnp.where(place == s, slots[s][...].astype(F32), picked)
         parts = [picked[h * MOST : (h + 1) * MOST] for h in range(heads)]
-        extra = jnp.sum(sum(parts), axis=1, keepdims=True) / width
-        mean = to_column(picked[heads * MOST : heads * MOST + 1], at_lane(0)) + extra
-        parts = [part - extra for part in parts]
+        extra = jnp.sum(sum(parts), axis=1, keepdims=True)
+        centre = to_column(picked[heads * MOST : heads * MOST + 1], at_lane(0))
         square = jnp.sum(sum(part * part for part in parts), axis=1, keepdims=True)
         mask = at_lane(b % group * MOST)
-        values = (*split3(to_line(mean, mask)), *split3(to_line(square, mask)))
+        values = (
+            to_line(centre, mask),
+            *split3(to_line(extra, mask)),
+            *split3(to_line(square, mask)),
+        )
         lines[b // group] = [one + two for one, two in zip(lines[b // group], values)]
         gated.append(
             jnp.concatenate(
@@ -234,24 +237,27 @@
     chunks = model // LANES
     own = chunks // parts
     group = LANES // MOST
-    means, squares = [], []
-    for p in products:
-        tail = p[chunks * rows :, :].astype(F32)
-        mean, square = [], []
-        for b in range(blocks):
-            mask = at_lane(b % group * MOST)
-            first = b // group * 6
-            line = tail[first : first + 1] + tail[first + 1 : first + 2] + tail[first + 2 : first + 3]
-            mean.append(to_column(line, mask))
-            first += 3
-            line = tail[first : first + 1] + tail[first + 1 : first + 2] + tail[first + 2 : first + 3]
-            square.append(to_column(line, mask))
-        means.append(jnp.concatenate(mean, axis=0))
-        squares.append(jnp.concatenate(square, axis=0))
-    mean = sum(means) / parts
-    offsets = [m - mean for m in means]
-    spread = sum(squares) / model + sum(d * d for d in offsets) / parts
-    scale = lax.rsqrt(spread + EPSILON)
+    masks = [at_lane(b % group * MOST) for b in range(blocks)]
+    tails = [p[chunks * rows :, :].astype(F32) for p in products]
+    shifts, scales = [[] for _ in products], []
+    for first in range(0, blocks, group):
+        top = first // group * 7
+        lines = [[tail[top + i : top + i + 1] for i in range(7)] for tail in tails]
+        centres = [line[0] for line in lines]
+        extras = [line[1] + line[2] + line[3] for line in lines]
+        squares = [line[4] + line[5] + line[6] for line in lines]
+        mean = sum(c * (model // parts) + e for c, e in zip(centres, extras)) / model
+        deltas = [c - mean for c in centres]
+        spread = sum(
+            q + d * (2.0 * e + d * (model // parts)) for q, e, d in zip(squares, extras, deltas)
+        )
+        scale = lax.rsqrt(spread / model + EPSILON)
+        for b in range(first, min(first + group, blocks)):
+            scales.append(to_column(scale, masks[b]))
+            for shift, delta in zip(shifts, deltas):
+                shift.append(to_column(delta, masks[b]))
+    offsets = [jnp.concatenate(shift, axis=0) for shift in shifts]
+    scale = jnp.concatenate(scales, axis=0)
     me = lax.axis_index("mp")
     vectors = [base[chunks * rows :, :].astype(F32) for base in bases]
     vectors = [v[:own] + v[own : 2 * own] + v[2 * own : 3 * own] for v in vectors]
@@ -277,22 +283,11 @@
             out[b : b + 1, LANES:] = jnp.zeros((1, block_rows - LANES), F32)
 
 
-def swap(arrays, axis, cross=None):
+def swap(arrays, axis):
     size = lax.axis_size(axis)
-    out = [None] * size
-    out[0] = arrays[0]
-    for s in range(size - 1, 0, -1):
-        if cross is None:
-            out[s] = lax.ppermute(arrays[s], axis, [(k, k ^ s) for k in range(size)])
-        else:
-            cores = lax.axis_size(cross)
-            pairs = [
-                (k * cores + c, (k ^ s) * cores + cores - 1 - c)
-                for k in range(size)
-                for c in range(cores)
-            ]
-            out[s] = lax.ppermute(arrays[s], (axis, cross), pairs)
-    return out
+    return [arrays[0]] + [
+        lax.ppermute(arrays[s], axis, [(k, k ^ s) for k in range(size)]) for s in range(1, size)
+    ]
 
 
 def local(
@@ -333,7 +328,7 @@
     score_row = fetched(w_score.reshape(width // LANES, LANES))
     heads = time_bias.shape[0]
     chunks = model // LANES
-    sums = (chunks * rows + whole_tiles(6 * -(-rows // LANES)), LANES)
+    sums = (chunks * rows + whole_tiles(7 * -(-rows // LANES)), LANES)
     slot = shape((heads * MOST + TAIL, width // heads), BF16)
     notes_shape = shape((blocks, LANES), jnp.int32)
     *slots, x, notes = call(
@@ -350,7 +345,7 @@
             pltpu.SemaphoreType.DMA((2,)),
         ],
     )(block_user, own_map, candidates, w_query_unit)
-    slots = swap(slots, "users", "helpers")
+    slots = swap(slots, "users")
     gate, base, out_w, counts, values = call(
         gate_kernel,
         [
@@ -383,7 +378,7 @@
     half_first = sorted(far_first, key=lambda s: s != owners // 2)
     mixtures = dict(zip([0], attend([0])))
     mixtures.update(zip(half_first, attend(half_first)))
-    mixtures = swap(mixtures, "users", "helpers")
+    mixtures = swap(mixtures, "users")
     order = [*far_first, 0]
     product, sent = call(
         functools.partial(product_kernel, order),

time: 26.3 us -> 26.1 us (level)
  waiting for transfers between devices: 5.64 us -> 5.16 us
  starting transfers between devices: 12.9 us -> 13.2 us
    ppermute x8, waiting for transfers between devices: 5.64 us -> 5.16 us  [swap(): lax.ppermute(arrays[s], axis, [(k, k ^ s) for k in range(size)])]
    ppermute x8, starting transfers between devices: 12.9 us -> 13.2 us  [swap(): lax.ppermute(arrays[s], axis, [(k, k ^ s) for k in range(size)])]
  transfers between devices with their start and end apart: 8 -> 8, of which waited for: 5 -> 4; matrix products, arithmetic and copies ran while one was open for 0% -> 0% of each run, Pallas kernels for 15% -> 15%
where the time goes in v7:
time: 26.1 us; the launch traced here: 25.9 us
  starting transfers between devices  13.2 us (51%)
  Pallas kernels  7.52 us (29%)
  waiting for transfers between devices  5.16 us (20%)
    ppermute x8, starting transfers between devices, swap(): lax.ppermute(arrays[s], axis, [(k, k ^ s) for k in range(size)])  13.2 us
    ppermute x8, waiting for transfers between devices, swap(): lax.ppermute(arrays[s], axis, [(k, k ^ s) for k in range(size)])  5.16 us
    pallas_call x1, Pallas kernels, local(): call(gate_kernel, [shape((rows, width), F32), shape((chunks * rows + whol...  2.89 us
    pallas_call x2, Pallas kernels, attend(): call(functools.partial(attend_kernel, len(order)), [slot] * len(order), [...  1.77 us
    pallas_call x1, Pallas kernels, local(): call(functools.partial(query_kernel, owners, users_here, heads), [slot] *...  1.57 us
    pallas_call x1, Pallas kernels, local(): call(functools.partial(score_kernel, parts), shape((blocks, block_rows),...  0.97 us
  transfers between devices with their start and end apart: 8, of which 4 were waited for; matrix products, arithmetic and copies ran while one was open for 0% of the time, Pallas kernels for 15%

profile of v7, /device:TPU:0, one launch (start us, length us, event | category | flops | bytes accessed | tf_op | source)
XLA Modules:
  0.0 25.9 jit_solution(16326401722290079440)
XLA Ops:
  0.0 1.6 %shard_map.100 = (bf16[144,128]{1,0:T(8,128)(2,1)S(1)}, bf16[144,128]{1,0:T(8,128)(2,1)S(1)}, bf16[144,128]{1,0:T(8,128)(2,1)S(1)}, bf16[144,128]{1,0:T(8,128)(2...) custom-call(s32[2]{0:T(128)} %user_source.1, s32[32]{0:T(128)} %map_source.1, ...), custom_call_target="tpu_custom_call" | custom-call | tf_op jit(solution)/shard_map/pallas_call | solution.py:334
  1.6 0.0 copy-start
  1.6 0.0 copy-start.1
  1.6 4.1 %collective-permute-start.1 = (bf16[144,128]{1,0:T(8,128)(2,1)S(1)}, bf16[144,128]{1,0:T(8,128)(2,1)S(1)}, u32[]{:S(2)}, u32[]{:S(2)}) collective-permute-start(bf16[144,128]{1,0:T(8,128)(2,1)S(1)} %get-tuple-element.28), channel_id=1, source_target_pairs={{0,8},{4,12},{8,0},{12,4},{1,9},{5,13},{9,1},{13,5},{2,10},{6,14},... | collective-permute-start | bytes 110600 | tf_op jit(solution)/shard_map/ppermute | solution.py:289
  5.7 1.3 %collective-permute-start.2 = (bf16[144,128]{1,0:T(8,128)(2,1)S(1)}, bf16[144,128]{1,0:T(8,128)(2,1)S(1)}, u32[]{:S(2)}, u32[]{:S(2)}) collective-permute-start(bf16[144,128]{1,0:T(8,128)(2,1)S(1)} %get-tuple-element.29), channel_id=1, source_target_pairs={{0,12},{4,8},{8,4},{12,0},{1,13},{5,9},{9,5},{13,1},{2,14},{6,10},... | collective-permute-start | bytes 110600 | tf_op jit(solution)/shard_map/ppermute | solution.py:289
  7.0 0.2 collective-permute-start.3
  7.3 2.9 %shard_map.101 = (f32[64,512]{1,0:T(8,128)S(1)}, bf16[528,128]{1,0:T(8,128)(2,1)S(1)}, bf16[512,1024]{1,0:T(8,128)(2,1)S(1)}, s32[2,128]{1,0:T(2,128)S(1)}, bf16[8,512,512]{2,1,0:T(8,128)(2,1)S(1)}) custom-call(bf16[64,1024]{1,0:T(8,128)(2,1)S(1)} %get-tuple-element.21.x, bf16[2,1024,512]{2,1,0:T(8,128)(2,1)} %weights.3, bf16[512,1024]{1,0:T(8,128)(2,1)} %out_source.1, ...), custom_call_target="tpu_custom_call" | custom-call | tf_op jit(solution)/shard_map/pallas_call | solution.py:349
  10.2 0.0 collective-permute-done.1.rest_0_
  10.2 1.3 %collective-permute-done.2.rest_1_ = bf16[144,128]{1,0:T(8,128)(2,1)S(1)} collective-permute-done((bf16[144,128]{1,0:T(8,128)(2,1)S(1)}, bf16[144,128]{1,0:T(8,128)(2,1)S(1)}, u32[]{:S(2)}, u32[]{:S(2)}) %collective-permute-start.2) | collective-permute-done | bytes 36896 | tf_op jit(solution)/shard_map/ppermute | solution.py:289
  11.5 0.0 collective-permute-done.3.rest_2_
  11.5 0.0 copy-done
  11.5 0.0 copy-done.1
  11.5 1.1 %shard_map.102 = (bf16[144,128]{1,0:T(8,128)(2,1)S(1)}, bf16[144,128]{1,0:T(8,128)(2,1)S(1)}, bf16[144,128]{1,0:T(8,128)(2,1)S(1)}) custom-call(f32[4,512]{1,0:T(4,128)S(1)} %copy-done.1, bf16[8,512,512]{2,1,0:T(8,128)(2,1)S(1)} %copy-done, bf16[8,512,512]{2,1,0:T(8,128)(2,1)S(1)} %get-tuple-element.27.values, ...), custom_call_target="tpu_custom_call" | custom-call | tf_op jit(solution)/shard_map/pallas_call | solution.py:370
  12.6 2.1 %collective-permute-start.4 = (bf16[144,128]{1,0:T(8,128)(2,1)S(1)}, bf16[144,128]{1,0:T(8,128)(2,1)S(1)}, u32[]{:S(2)}, u32[]{:S(2)}) collective-permute-start(bf16[144,128]{1,0:T(8,128)(2,1)S(1)} %get-tuple-element.31), channel_id=1, source_target_pairs={{0,12},{4,8},{8,4},{12,0},{1,13},{5,9},{9,5},{13,1},{2,14},{6,10},... | collective-permute-start | bytes 110600 | tf_op jit(solution)/shard_map/ppermute | solution.py:289
  14.7 0.0 collective-permute-start.5
  14.7 2.4 %collective-permute-start.6 = (bf16[144,128]{1,0:T(8,128)(2,1)S(1)}, bf16[144,128]{1,0:T(8,128)(2,1)S(1)}, u32[]{:S(2)}, u32[]{:S(2)}) collective-permute-start(bf16[144,128]{1,0:T(8,128)(2,1)S(1)} %get-tuple-element.33), channel_id=1, source_target_pairs={{0,4},{4,0},{8,12},{12,8},{1,5},{5,1},{9,13},{13,9},{2,6},{6,2},{1... | collective-permute-start | bytes 110600 | tf_op jit(solution)/shard_map/ppermute | solution.py:289
  17.0 1.5 %collective-permute-start = (bf16[528,128]{1,0:T(8,128)(2,1)S(1)}, bf16[528,128]{1,0:T(8,128)(2,1)S(1)}, u32[]{:S(2)}, u32[]{:S(2)}) collective-permute-start(bf16[528,128]{1,0:T(8,128)(2,1)S(1)} %get-tuple-element.23.rest_0_), channel_id=1, source_target_pairs={{0,2},{2,0},{1,3},{3,1},{4,6},{6,4},{5,7},{7,5},{8,10},{10,8},{9,1... | collective-permute-start | bytes 405512 | tf_op jit(solution)/shard_map/ppermute | solution.py:289
  18.5 0.7 %shard_map.103.rest_3_ = bf16[144,128]{1,0:T(8,128)(2,1)S(1)} custom-call(f32[4,512]{1,0:T(4,128)S(1)} %copy-done.1, bf16[8,512,512]{2,1,0:T(8,128)(2,1)S(1)} %copy-done, bf16[8,512,512]{2,1,0:T(8,128)(2,1)S(1)} %get-tuple-element.27.values, bf16[144,128]{1,0:T(8,128)(2,1)S(1)} %get-tuple-element.34.rest_0_), custom_call_target="tpu_custom_call" | custom-call | tf_op jit(solution)/shard_map/pallas_call | solution.py:370
  19.2 0.0 collective-permute-done.4.rest_0_
  19.2 0.4 %collective-permute-done.5.rest_1_ = bf16[144,128]{1,0:T(8,128)(2,1)S(1)} collective-permute-done((bf16[144,128]{1,0:T(8,128)(2,1)S(1)}, bf16[144,128]{1,0:T(8,128)(2,1)S(1)}, u32[]{:S(2)}, u32[]{:S(2)}) %collective-permute-start.5) | collective-permute-done | bytes 36896 | tf_op jit(solution)/shard_map/ppermute | solution.py:289
  19.6 0.0 collective-permute-done.6.rest_2_
  19.6 0.3 %shard_map.104 = (f32[528,128]{1,0:T(8,128)S(1)}, bf16[528,128]{1,0:T(8,128)(2,1)S(1)}) custom-call(s32[2,128]{1,0:T(2,128)S(1)} %get-tuple-element.24.notes, f32[64,512]{1,0:T(8,128)S(1)} %get-tuple-element.25.gate, bf16[512,1024]{1,0:T(8,128)(2,1)S(1)} %get-tuple-element.26.out_weight, bf16[144,128]{1,0:T(8,128)(2,1)S(1)} %collective-permute-done.4.rest_0_, ...), custom_call_target="tpu_custom_call" | custom-call | tf_op jit(solution)/shard_map/pallas_call | solution.py:383
  19.9 1.6 %collective-permute-start.7 = (bf16[528,128]{1,0:T(8,128)(2,1)S(1)}, bf16[528,128]{1,0:T(8,128)(2,1)S(1)}, u32[]{:S(2)}, u32[]{:S(2)}) collective-permute-start(bf16[528,128]{1,0:T(8,128)(2,1)S(1)} %get-tuple-element.36), channel_id=1, source_target_pairs={{0,2},{2,0},{1,3},{3,1},{4,6},{6,4},{5,7},{7,5},{8,10},{10,8},{9,1... | collective-permute-start | bytes 405512 | tf_op jit(solution)/shard_map/ppermute | solution.py:289
  21.5 1.6 %collective-permute-done.rest_1_ = bf16[528,128]{1,0:T(8,128)(2,1)S(1)} collective-permute-done((bf16[528,128]{1,0:T(8,128)(2,1)S(1)}, bf16[528,128]{1,0:T(8,128)(2,1)S(1)}, u32[]{:S(2)}, u32[]{:S(2)}) %collective-permute-start) | collective-permute-done | bytes 135200 | tf_op jit(solution)/shard_map/ppermute | solution.py:289
  23.1 1.9 %collective-permute-done.7.rest_3_ = bf16[528,128]{1,0:T(8,128)(2,1)S(1)} collective-permute-done((bf16[528,128]{1,0:T(8,128)(2,1)S(1)}, bf16[528,128]{1,0:T(8,128)(2,1)S(1)}, u32[]{:S(2)}, u32[]{:S(2)}) %collective-permute-start.7) | collective-permute-done | bytes 135200 | tf_op jit(solution)/shard_map/ppermute | solution.py:289
  25.0 1.0 %shard_map.105 = f32[2,128]{1,0:T(2,128)} custom-call(s32[2,128]{1,0:T(2,128)S(1)} %get-tuple-element.22.counts, bf16[64,1024]{1,0:T(8,128)(2,1)S(1)} %get-tuple-element.21.x, bf16[528,128]{1,0:T(8,128)(2,1)S(1)} %get-tuple-element.23.rest_0_, bf16[528,128]{1,0:T(8,128)(2,1)S(1)} %collective-permute-done.rest_1_, f32[528,128]{1,0:T(8,128)S(1)} %get-tuple-element.35.rest_2_, ...), custom_call_target="tpu_custom_call" | custom-call | tf_op jit(solution)/shard_map/pallas_call | solution.py:390
Async XLA Ops:
  1.6 9.9 %copy-start = (bf16[8,512,512]{2,1,0:T(8,128)(2,1)S(1)}, bf16[8,512,512]{2,1,0:T(8,128)(2,1)}, u32[]{:S(2)}) copy-start(bf16[8,512,512]{2,1,0:T(8,128)(2,1)} %keys.3) | copy-start | bytes 12582916
  1.6 9.9 %copy-start.1 = (f32[4,512]{1,0:T(4,128)S(1)}, f32[4,512]{1,0:T(4,128)}, u32[]{:S(2)}) copy-start(f32[4,512]{1,0:T(4,128)} %bias.3) | copy-start | bytes 24580
  1.6 8.6 %collective-permute-start.1 = (bf16[144,128]{1,0:T(8,128)(2,1)S(1)}, bf16[144,128]{1,0:T(8,128)(2,1)S(1)}, u32[]{:S(2)}, u32[]{:S(2)}) collective-permute-start(bf16[144,128]{1,0:T(8,128)(2,1)S(1)} %get-tuple-element.28), channel_id=1, source_target_pairs={{0,8},{4,12},{8,0},{12,4},{1,9},{5,13},{9,1},{13,5},{2,10},{6,14},... | collective-permute-start | bytes 110600 | tf_op jit(solution)/shard_map/ppermute | solution.py:289
  5.7 5.8 %collective-permute-start.2 = (bf16[144,128]{1,0:T(8,128)(2,1)S(1)}, bf16[144,128]{1,0:T(8,128)(2,1)S(1)}, u32[]{:S(2)}, u32[]{:S(2)}) collective-permute-start(bf16[144,128]{1,0:T(8,128)(2,1)S(1)} %get-tuple-element.29), channel_id=1, source_target_pairs={{0,12},{4,8},{8,4},{12,0},{1,13},{5,9},{9,5},{13,1},{2,14},{6,10},... | collective-permute-start | bytes 110600 | tf_op jit(solution)/shard_map/ppermute | solution.py:289
  7.0 4.4 %collective-permute-start.3 = (bf16[144,128]{1,0:T(8,128)(2,1)S(1)}, bf16[144,128]{1,0:T(8,128)(2,1)S(1)}, u32[]{:S(2)}, u32[]{:S(2)}) collective-permute-start(bf16[144,128]{1,0:T(8,128)(2,1)S(1)} %get-tuple-element.30), channel_id=1, source_target_pairs={{0,4},{4,0},{8,12},{12,8},{1,5},{5,1},{9,13},{13,9},{2,6},{6,2},{1... | collective-permute-start | bytes 110600 | tf_op jit(solution)/shard_map/ppermute | solution.py:289
  12.6 6.6 %collective-permute-start.4 = (bf16[144,128]{1,0:T(8,128)(2,1)S(1)}, bf16[144,128]{1,0:T(8,128)(2,1)S(1)}, u32[]{:S(2)}, u32[]{:S(2)}) collective-permute-start(bf16[144,128]{1,0:T(8,128)(2,1)S(1)} %get-tuple-element.31), channel_id=1, source_target_pairs={{0,12},{4,8},{8,4},{12,0},{1,13},{5,9},{9,5},{13,1},{2,14},{6,10},... | collective-permute-start | bytes 110600 | tf_op jit(solution)/shard_map/ppermute | solution.py:289
  14.7 4.9 %collective-permute-start.5 = (bf16[144,128]{1,0:T(8,128)(2,1)S(1)}, bf16[144,128]{1,0:T(8,128)(2,1)S(1)}, u32[]{:S(2)}, u32[]{:S(2)}) collective-permute-start(bf16[144,128]{1,0:T(8,128)(2,1)S(1)} %get-tuple-element.32), channel_id=1, source_target_pairs={{0,8},{4,12},{8,0},{12,4},{1,9},{5,13},{9,1},{13,5},{2,10},{6,14},... | collective-permute-start | bytes 110600 | tf_op jit(solution)/shard_map/ppermute | solution.py:289
  14.7 4.9 %collective-permute-start.6 = (bf16[144,128]{1,0:T(8,128)(2,1)S(1)}, bf16[144,128]{1,0:T(8,128)(2,1)S(1)}, u32[]{:S(2)}, u32[]{:S(2)}) collective-permute-start(bf16[144,128]{1,0:T(8,128)(2,1)S(1)} %get-tuple-element.33), channel_id=1, source_target_pairs={{0,4},{4,0},{8,12},{12,8},{1,5},{5,1},{9,13},{13,9},{2,6},{6,2},{1... | collective-permute-start | bytes 110600 | tf_op jit(solution)/shard_map/ppermute | solution.py:289
  17.0 6.1 %collective-permute-start = (bf16[528,128]{1,0:T(8,128)(2,1)S(1)}, bf16[528,128]{1,0:T(8,128)(2,1)S(1)}, u32[]{:S(2)}, u32[]{:S(2)}) collective-permute-start(bf16[528,128]{1,0:T(8,128)(2,1)S(1)} %get-tuple-element.23.rest_0_), channel_id=1, source_target_pairs={{0,2},{2,0},{1,3},{3,1},{4,6},{6,4},{5,7},{7,5},{8,10},{10,8},{9,1... | collective-permute-start | bytes 405512 | tf_op jit(solution)/shard_map/ppermute | solution.py:289
  19.9 5.1 %collective-permute-start.7 = (bf16[528,128]{1,0:T(8,128)(2,1)S(1)}, bf16[528,128]{1,0:T(8,128)(2,1)S(1)}, u32[]{:S(2)}, u32[]{:S(2)}) collective-permute-start(bf16[528,128]{1,0:T(8,128)(2,1)S(1)} %get-tuple-element.36), channel_id=1, source_target_pairs={{0,2},{2,0},{1,3},{3,1},{4,6},{6,4},{5,7},{7,5},{8,10},{10,8},{9,1... | collective-permute-start | bytes 405512 | tf_op jit(solution)/shard_map/ppermute | solution.py:289

commit v8 on v7

--- a/solution.py
+++ b/solution.py
@@ -379,7 +379,7 @@
     mixtures = dict(zip([0], attend([0])))
     mixtures.update(zip(half_first, attend(half_first)))
     mixtures = swap(mixtures, "users")
-    order = [*far_first, 0]
+    order = [*sorted(far_first, key=lambda s: s == owners // 2), 0]
     product, sent = call(
         functools.partial(product_kernel, order),
         [shape(sums, F32), shape(sums, BF16)],

time: 26.1 us -> 26.1 us (level)
  no operation moved by 1% of the time
where the time goes in v8:
time: 26.1 us; the launch traced here: 26 us
  starting transfers between devices  13.2 us (51%)
  Pallas kernels  7.52 us (29%)
  waiting for transfers between devices  5.21 us (20%)
    ppermute x8, starting transfers between devices, swap(): lax.ppermute(arrays[s], axis, [(k, k ^ s) for k in range(size)])  13.2 us
    ppermute x8, waiting for transfers between devices, swap(): lax.ppermute(arrays[s], axis, [(k, k ^ s) for k in range(size)])  5.21 us
    pallas_call x1, Pallas kernels, local(): call(gate_kernel, [shape((rows, width), F32), shape((chunks * rows + whol...  2.89 us
    pallas_call x2, Pallas kernels, attend(): call(functools.partial(attend_kernel, len(order)), [slot] * len(order), [...  1.77 us
    pallas_call x1, Pallas kernels, local(): call(functools.partial(query_kernel, owners, users_here, heads), [slot] *...  1.57 us
    pallas_call x1, Pallas kernels, local(): call(functools.partial(score_kernel, parts), shape((blocks, block_rows),...  0.97 us
  transfers between devices with their start and end apart: 8, of which 4 were waited for; matrix products, arithmetic and copies ran while one was open for 0% of the time, Pallas kernels for 15%

profile of v8, /device:TPU:0, one launch (start us, length us, event | category | flops | bytes accessed | tf_op | source)
XLA Modules:
  0.0 26.0 jit_solution(10585710336007337314)
XLA Ops:
  0.0 1.6 %shard_map.100 = (bf16[144,128]{1,0:T(8,128)(2,1)S(1)}, bf16[144,128]{1,0:T(8,128)(2,1)S(1)}, bf16[144,128]{1,0:T(8,128)(2,1)S(1)}, bf16[144,128]{1,0:T(8,128)(2...) custom-call(s32[2]{0:T(128)} %user_source.1, s32[32]{0:T(128)} %map_source.1, ...), custom_call_target="tpu_custom_call" | custom-call | tf_op jit(solution)/shard_map/pallas_call | solution.py:334
  1.6 0.0 copy-start
  1.6 0.0 copy-start.1
  1.6 4.1 %collective-permute-start.1 = (bf16[144,128]{1,0:T(8,128)(2,1)S(1)}, bf16[144,128]{1,0:T(8,128)(2,1)S(1)}, u32[]{:S(2)}, u32[]{:S(2)}) collective-permute-start(bf16[144,128]{1,0:T(8,128)(2,1)S(1)} %get-tuple-element.28), channel_id=1, source_target_pairs={{0,8},{4,12},{8,0},{12,4},{1,9},{5,13},{9,1},{13,5},{2,10},{6,14},... | collective-permute-start | bytes 110600 | tf_op jit(solution)/shard_map/ppermute | solution.py:289
  5.7 1.3 %collective-permute-start.2 = (bf16[144,128]{1,0:T(8,128)(2,1)S(1)}, bf16[144,128]{1,0:T(8,128)(2,1)S(1)}, u32[]{:S(2)}, u32[]{:S(2)}) collective-permute-start(bf16[144,128]{1,0:T(8,128)(2,1)S(1)} %get-tuple-element.29), channel_id=1, source_target_pairs={{0,12},{4,8},{8,4},{12,0},{1,13},{5,9},{9,5},{13,1},{2,14},{6,10},... | collective-permute-start | bytes 110600 | tf_op jit(solution)/shard_map/ppermute | solution.py:289
  7.0 0.2 collective-permute-start.3
  7.3 2.9 %shard_map.101 = (f32[64,512]{1,0:T(8,128)S(1)}, bf16[528,128]{1,0:T(8,128)(2,1)S(1)}, bf16[512,1024]{1,0:T(8,128)(2,1)S(1)}, s32[2,128]{1,0:T(2,128)S(1)}, bf16[8,512,512]{2,1,0:T(8,128)(2,1)S(1)}) custom-call(bf16[64,1024]{1,0:T(8,128)(2,1)S(1)} %get-tuple-element.21.x, bf16[2,1024,512]{2,1,0:T(8,128)(2,1)} %weights.3, bf16[512,1024]{1,0:T(8,128)(2,1)} %out_source.1, ...), custom_call_target="tpu_custom_call" | custom-call | tf_op jit(solution)/shard_map/pallas_call | solution.py:349
  10.2 0.0 collective-permute-done.1.rest_0_
  10.2 1.3 %collective-permute-done.2.rest_1_ = bf16[144,128]{1,0:T(8,128)(2,1)S(1)} collective-permute-done((bf16[144,128]{1,0:T(8,128)(2,1)S(1)}, bf16[144,128]{1,0:T(8,128)(2,1)S(1)}, u32[]{:S(2)}, u32[]{:S(2)}) %collective-permute-start.2) | collective-permute-done | bytes 36896 | tf_op jit(solution)/shard_map/ppermute | solution.py:289
  11.5 0.0 collective-permute-done.3.rest_2_
  11.5 0.0 copy-done
  11.5 0.0 copy-done.1
  11.5 1.1 %shard_map.102 = (bf16[144,128]{1,0:T(8,128)(2,1)S(1)}, bf16[144,128]{1,0:T(8,128)(2,1)S(1)}, bf16[144,128]{1,0:T(8,128)(2,1)S(1)}) custom-call(f32[4,512]{1,0:T(4,128)S(1)} %copy-done.1, bf16[8,512,512]{2,1,0:T(8,128)(2,1)S(1)} %copy-done, bf16[8,512,512]{2,1,0:T(8,128)(2,1)S(1)} %get-tuple-element.27.values, ...), custom_call_target="tpu_custom_call" | custom-call | tf_op jit(solution)/shard_map/pallas_call | solution.py:370
  12.6 2.1 %collective-permute-start.4 = (bf16[144,128]{1,0:T(8,128)(2,1)S(1)}, bf16[144,128]{1,0:T(8,128)(2,1)S(1)}, u32[]{:S(2)}, u32[]{:S(2)}) collective-permute-start(bf16[144,128]{1,0:T(8,128)(2,1)S(1)} %get-tuple-element.31), channel_id=1, source_target_pairs={{0,12},{4,8},{8,4},{12,0},{1,13},{5,9},{9,5},{13,1},{2,14},{6,10},... | collective-permute-start | bytes 110600 | tf_op jit(solution)/shard_map/ppermute | solution.py:289
  14.7 0.1 collective-permute-start.5
  14.8 2.3 %collective-permute-start.6 = (bf16[144,128]{1,0:T(8,128)(2,1)S(1)}, bf16[144,128]{1,0:T(8,128)(2,1)S(1)}, u32[]{:S(2)}, u32[]{:S(2)}) collective-permute-start(bf16[144,128]{1,0:T(8,128)(2,1)S(1)} %get-tuple-element.33), channel_id=1, source_target_pairs={{0,8},{4,12},{8,0},{12,4},{1,9},{5,13},{9,1},{13,5},{2,10},{6,14},... | collective-permute-start | bytes 110600 | tf_op jit(solution)/shard_map/ppermute | solution.py:289
  17.0 1.5 %collective-permute-start = (bf16[528,128]{1,0:T(8,128)(2,1)S(1)}, bf16[528,128]{1,0:T(8,128)(2,1)S(1)}, u32[]{:S(2)}, u32[]{:S(2)}) collective-permute-start(bf16[528,128]{1,0:T(8,128)(2,1)S(1)} %get-tuple-element.23.rest_0_), channel_id=1, source_target_pairs={{0,2},{2,0},{1,3},{3,1},{4,6},{6,4},{5,7},{7,5},{8,10},{10,8},{9,1... | collective-permute-start | bytes 405512 | tf_op jit(solution)/shard_map/ppermute | solution.py:289
  18.5 0.7 %shard_map.103.rest_3_ = bf16[144,128]{1,0:T(8,128)(2,1)S(1)} custom-call(f32[4,512]{1,0:T(4,128)S(1)} %copy-done.1, bf16[8,512,512]{2,1,0:T(8,128)(2,1)S(1)} %copy-done, bf16[8,512,512]{2,1,0:T(8,128)(2,1)S(1)} %get-tuple-element.27.values, bf16[144,128]{1,0:T(8,128)(2,1)S(1)} %get-tuple-element.34.rest_0_), custom_call_target="tpu_custom_call" | custom-call | tf_op jit(solution)/shard_map/pallas_call | solution.py:370
  19.2 0.0 collective-permute-done.4.rest_0_
  19.2 0.0 collective-permute-done.5.rest_1_
  19.2 0.4 %collective-permute-done.6.rest_2_ = bf16[144,128]{1,0:T(8,128)(2,1)S(1)} collective-permute-done((bf16[144,128]{1,0:T(8,128)(2,1)S(1)}, bf16[144,128]{1,0:T(8,128)(2,1)S(1)}, u32[]{:S(2)}, u32[]{:S(2)}) %collective-permute-start.6) | collective-permute-done | bytes 36896 | tf_op jit(solution)/shard_map/ppermute | solution.py:289
  19.6 0.3 %shard_map.104 = (f32[528,128]{1,0:T(8,128)S(1)}, bf16[528,128]{1,0:T(8,128)(2,1)S(1)}) custom-call(s32[2,128]{1,0:T(2,128)S(1)} %get-tuple-element.24.notes, f32[64,512]{1,0:T(8,128)S(1)} %get-tuple-element.25.gate, bf16[512,1024]{1,0:T(8,128)(2,1)S(1)} %get-tuple-element.26.out_weight, bf16[144,128]{1,0:T(8,128)(2,1)S(1)} %collective-permute-done.4.rest_0_, ...), custom_call_target="tpu_custom_call" | custom-call | tf_op jit(solution)/shard_map/pallas_call | solution.py:383
  19.9 1.6 %collective-permute-start.7 = (bf16[528,128]{1,0:T(8,128)(2,1)S(1)}, bf16[528,128]{1,0:T(8,128)(2,1)S(1)}, u32[]{:S(2)}, u32[]{:S(2)}) collective-permute-start(bf16[528,128]{1,0:T(8,128)(2,1)S(1)} %get-tuple-element.36), channel_id=1, source_target_pairs={{0,2},{2,0},{1,3},{3,1},{4,6},{6,4},{5,7},{7,5},{8,10},{10,8},{9,1... | collective-permute-start | bytes 405512 | tf_op jit(solution)/shard_map/ppermute | solution.py:289
  21.5 1.5 %collective-permute-done.rest_1_ = bf16[528,128]{1,0:T(8,128)(2,1)S(1)} collective-permute-done((bf16[528,128]{1,0:T(8,128)(2,1)S(1)}, bf16[528,128]{1,0:T(8,128)(2,1)S(1)}, u32[]{:S(2)}, u32[]{:S(2)}) %collective-permute-start) | collective-permute-done | bytes 135200 | tf_op jit(solution)/shard_map/ppermute | solution.py:289
  23.0 2.0 %collective-permute-done.7.rest_3_ = bf16[528,128]{1,0:T(8,128)(2,1)S(1)} collective-permute-done((bf16[528,128]{1,0:T(8,128)(2,1)S(1)}, bf16[528,128]{1,0:T(8,128)(2,1)S(1)}, u32[]{:S(2)}, u32[]{:S(2)}) %collective-permute-start.7) | collective-permute-done | bytes 135200 | tf_op jit(solution)/shard_map/ppermute | solution.py:289
  25.0 1.0 %shard_map.105 = f32[2,128]{1,0:T(2,128)} custom-call(s32[2,128]{1,0:T(2,128)S(1)} %get-tuple-element.22.counts, bf16[64,1024]{1,0:T(8,128)(2,1)S(1)} %get-tuple-element.21.x, bf16[528,128]{1,0:T(8,128)(2,1)S(1)} %get-tuple-element.23.rest_0_, bf16[528,128]{1,0:T(8,128)(2,1)S(1)} %collective-permute-done.rest_1_, f32[528,128]{1,0:T(8,128)S(1)} %get-tuple-element.35.rest_2_, ...), custom_call_target="tpu_custom_call" | custom-call | tf_op jit(solution)/shard_map/pallas_call | solution.py:390
Async XLA Ops:
  1.6 9.9 %copy-start = (bf16[8,512,512]{2,1,0:T(8,128)(2,1)S(1)}, bf16[8,512,512]{2,1,0:T(8,128)(2,1)}, u32[]{:S(2)}) copy-start(bf16[8,512,512]{2,1,0:T(8,128)(2,1)} %keys.3) | copy-start | bytes 12582916
  1.6 9.9 %copy-start.1 = (f32[4,512]{1,0:T(4,128)S(1)}, f32[4,512]{1,0:T(4,128)}, u32[]{:S(2)}) copy-start(f32[4,512]{1,0:T(4,128)} %bias.3) | copy-start | bytes 24580
  1.6 8.6 %collective-permute-start.1 = (bf16[144,128]{1,0:T(8,128)(2,1)S(1)}, bf16[144,128]{1,0:T(8,128)(2,1)S(1)}, u32[]{:S(2)}, u32[]{:S(2)}) collective-permute-start(bf16[144,128]{1,0:T(8,128)(2,1)S(1)} %get-tuple-element.28), channel_id=1, source_target_pairs={{0,8},{4,12},{8,0},{12,4},{1,9},{5,13},{9,1},{13,5},{2,10},{6,14},... | collective-permute-start | bytes 110600 | tf_op jit(solution)/shard_map/ppermute | solution.py:289
  5.7 5.8 %collective-permute-start.2 = (bf16[144,128]{1,0:T(8,128)(2,1)S(1)}, bf16[144,128]{1,0:T(8,128)(2,1)S(1)}, u32[]{:S(2)}, u32[]{:S(2)}) collective-permute-start(bf16[144,128]{1,0:T(8,128)(2,1)S(1)} %get-tuple-element.29), channel_id=1, source_target_pairs={{0,12},{4,8},{8,4},{12,0},{1,13},{5,9},{9,5},{13,1},{2,14},{6,10},... | collective-permute-start | bytes 110600 | tf_op jit(solution)/shard_map/ppermute | solution.py:289
  7.0 4.4 %collective-permute-start.3 = (bf16[144,128]{1,0:T(8,128)(2,1)S(1)}, bf16[144,128]{1,0:T(8,128)(2,1)S(1)}, u32[]{:S(2)}, u32[]{:S(2)}) collective-permute-start(bf16[144,128]{1,0:T(8,128)(2,1)S(1)} %get-tuple-element.30), channel_id=1, source_target_pairs={{0,4},{4,0},{8,12},{12,8},{1,5},{5,1},{9,13},{13,9},{2,6},{6,2},{1... | collective-permute-start | bytes 110600 | tf_op jit(solution)/shard_map/ppermute | solution.py:289
  12.6 6.6 %collective-permute-start.4 = (bf16[144,128]{1,0:T(8,128)(2,1)S(1)}, bf16[144,128]{1,0:T(8,128)(2,1)S(1)}, u32[]{:S(2)}, u32[]{:S(2)}) collective-permute-start(bf16[144,128]{1,0:T(8,128)(2,1)S(1)} %get-tuple-element.31), channel_id=1, source_target_pairs={{0,12},{4,8},{8,4},{12,0},{1,13},{5,9},{9,5},{13,1},{2,14},{6,10},... | collective-permute-start | bytes 110600 | tf_op jit(solution)/shard_map/ppermute | solution.py:289
  14.7 4.5 %collective-permute-start.5 = (bf16[144,128]{1,0:T(8,128)(2,1)S(1)}, bf16[144,128]{1,0:T(8,128)(2,1)S(1)}, u32[]{:S(2)}, u32[]{:S(2)}) collective-permute-start(bf16[144,128]{1,0:T(8,128)(2,1)S(1)} %get-tuple-element.32), channel_id=1, source_target_pairs={{0,4},{4,0},{8,12},{12,8},{1,5},{5,1},{9,13},{13,9},{2,6},{6,2},{1... | collective-permute-start | bytes 110600 | tf_op jit(solution)/shard_map/ppermute | solution.py:289
  14.8 4.9 %collective-permute-start.6 = (bf16[144,128]{1,0:T(8,128)(2,1)S(1)}, bf16[144,128]{1,0:T(8,128)(2,1)S(1)}, u32[]{:S(2)}, u32[]{:S(2)}) collective-permute-start(bf16[144,128]{1,0:T(8,128)(2,1)S(1)} %get-tuple-element.33), channel_id=1, source_target_pairs={{0,8},{4,12},{8,0},{12,4},{1,9},{5,13},{9,1},{13,5},{2,10},{6,14},... | collective-permute-start | bytes 110600 | tf_op jit(solution)/shard_map/ppermute | solution.py:289
  17.0 6.0 %collective-permute-start = (bf16[528,128]{1,0:T(8,128)(2,1)S(1)}, bf16[528,128]{1,0:T(8,128)(2,1)S(1)}, u32[]{:S(2)}, u32[]{:S(2)}) collective-permute-start(bf16[528,128]{1,0:T(8,128)(2,1)S(1)} %get-tuple-element.23.rest_0_), channel_id=1, source_target_pairs={{0,2},{2,0},{1,3},{3,1},{4,6},{6,4},{5,7},{7,5},{8,10},{10,8},{9,1... | collective-permute-start | bytes 405512 | tf_op jit(solution)/shard_map/ppermute | solution.py:289
  19.9 5.1 %collective-permute-start.7 = (bf16[528,128]{1,0:T(8,128)(2,1)S(1)}, bf16[528,128]{1,0:T(8,128)(2,1)S(1)}, u32[]{:S(2)}, u32[]{:S(2)}) collective-permute-start(bf16[528,128]{1,0:T(8,128)(2,1)S(1)} %get-tuple-element.36), channel_id=1, source_target_pairs={{0,2},{2,0},{1,3},{3,1},{4,6},{6,4},{5,7},{7,5},{8,10},{10,8},{9,1... | collective-permute-start | bytes 405512 | tf_op jit(solution)/shard_map/ppermute | solution.py:289

commit v9 on v7

--- a/solution.py
+++ b/solution.py
@@ -186,7 +186,7 @@
 def product_kernel(order, notes, gate, out_weight, *rest):
     owners = len(order)
     slots = {s: ref for s, ref in zip(order, rest)}
-    full, sent = rest[owners:]
+    (sent,) = rest[owners:]
     rows, width = gate.shape
     chunks = out_weight.shape[1] // LANES
     blocks = rows // MOST
@@ -224,10 +224,10 @@
         jnp.concatenate(gated, axis=0).astype(BF16), out_weight[...], preferred_element_type=F32
     )
     tail = filled([line for part in lines for line in part], sent.shape[0] - chunks * rows)
-    for ref, kind in ((full, F32), (sent, BF16)):
-        for c in range(chunks):
-            ref[c * rows : (c + 1) * rows, :] = product[:, c * LANES : (c + 1) * LANES].astype(kind)
-        ref[chunks * rows :, :] = tail.astype(kind)
+    kind = sent.dtype
+    for c in range(chunks):
+        sent[c * rows : (c + 1) * rows, :] = product[:, c * LANES : (c + 1) * LANES].astype(kind)
+    sent[chunks * rows :, :] = tail.astype(kind)
 
 
 def score_kernel(parts, counts, x, *rest):
@@ -380,12 +380,15 @@
     mixtures.update(zip(half_first, attend(half_first)))
     mixtures = swap(mixtures, "users")
     order = [*far_first, 0]
-    product, sent = call(
-        functools.partial(product_kernel, order),
-        [shape(sums, F32), shape(sums, BF16)],
-        [VMEM] * (3 + owners),
-        [VMEM] * 2,
-    )(notes, gate, out_w, *[mixtures[s] for s in order])
+    sent, product = (
+        call(
+            functools.partial(product_kernel, order),
+            [shape(sums, kind)],
+            [VMEM] * (3 + owners),
+            [VMEM],
+        )(notes, gate, out_w, *[mixtures[s] for s in order])[0]
+        for kind in (BF16, F32)
+    )
     products = [product] + swap([sent] * parts, "mp")[1:]
     return call(
         functools.partial(score_kernel, parts),

time: 26.1 us -> 26.1 us (level)
  Pallas kernels: 7.52 us -> 7.84 us
  waiting for transfers between devices: 5.16 us -> 4.84 us
    ppermute x8, waiting for transfers between devices: 5.16 us -> 4.84 us  [swap(): lax.ppermute(arrays[s], axis, [(k, k ^ s) for k in range(size)])]
    pallas_call x1 -> x2, Pallas kernels: 0.32 us -> 0.64 us  [local(): call(functools.partial(product_kernel, order), [shape(sums, kind)], [VMEM...]
  transfers between devices with their start and end apart: 8 -> 8, of which waited for: 4 -> 4; matrix products, arithmetic and copies ran while one was open for 0% -> 0% of each run, Pallas kernels for 15% -> 16%
where the time goes in v9:
time: 26.1 us; the launch traced here: 26 us
  starting transfers between devices  13.2 us (51%)
  Pallas kernels  7.84 us (30%)
  waiting for transfers between devices  4.84 us (19%)
    ppermute x8, starting transfers between devices, swap(): lax.ppermute(arrays[s], axis, [(k, k ^ s) for k in range(size)])  13.2 us
    ppermute x8, waiting for transfers between devices, swap(): lax.ppermute(arrays[s], axis, [(k, k ^ s) for k in range(size)])  4.84 us
    pallas_call x1, Pallas kernels, local(): call(gate_kernel, [shape((rows, width), F32), shape((chunks * rows + whol...  2.89 us
    pallas_call x2, Pallas kernels, attend(): call(functools.partial(attend_kernel, len(order)), [slot] * len(order), [...  1.77 us
    pallas_call x1, Pallas kernels, local(): call(functools.partial(query_kernel, owners, users_here, heads), [slot] *...  1.57 us
    pallas_call x1, Pallas kernels, local(): call(functools.partial(score_kernel, parts), shape((blocks, block_rows),...  0.97 us
    pallas_call x2, Pallas kernels, local(): call(functools.partial(product_kernel, order), [shape(sums, kind)], [VMEM...  0.64 us
  transfers between devices with their start and end apart: 8, of which 4 were waited for; matrix products, arithmetic and copies ran while one was open for 0% of the time, Pallas kernels for 16%

profile of v9, /device:TPU:0, one launch (start us, length us, event | category | flops | bytes accessed | tf_op | source)
XLA Modules:
  0.0 26.0 jit_solution(3346877169664159130)
XLA Ops:
  0.0 1.6 %shard_map.100 = (bf16[144,128]{1,0:T(8,128)(2,1)S(1)}, bf16[144,128]{1,0:T(8,128)(2,1)S(1)}, bf16[144,128]{1,0:T(8,128)(2,1)S(1)}, bf16[144,128]{1,0:T(8,128)(2...) custom-call(s32[2]{0:T(128)} %user_source.1, s32[32]{0:T(128)} %map_source.1, ...), custom_call_target="tpu_custom_call" | custom-call | tf_op jit(solution)/shard_map/pallas_call | solution.py:334
  1.6 0.0 copy-start
  1.6 0.0 copy-start.1
  1.6 4.1 %collective-permute-start.1 = (bf16[144,128]{1,0:T(8,128)(2,1)S(1)}, bf16[144,128]{1,0:T(8,128)(2,1)S(1)}, u32[]{:S(2)}, u32[]{:S(2)}) collective-permute-start(bf16[144,128]{1,0:T(8,128)(2,1)S(1)} %get-tuple-element.26), channel_id=1, source_target_pairs={{0,8},{4,12},{8,0},{12,4},{1,9},{5,13},{9,1},{13,5},{2,10},{6,14},... | collective-permute-start | bytes 110600 | tf_op jit(solution)/shard_map/ppermute | solution.py:289
  5.7 1.3 %collective-permute-start.2 = (bf16[144,128]{1,0:T(8,128)(2,1)S(1)}, bf16[144,128]{1,0:T(8,128)(2,1)S(1)}, u32[]{:S(2)}, u32[]{:S(2)}) collective-permute-start(bf16[144,128]{1,0:T(8,128)(2,1)S(1)} %get-tuple-element.27), channel_id=1, source_target_pairs={{0,12},{4,8},{8,4},{12,0},{1,13},{5,9},{9,5},{13,1},{2,14},{6,10},... | collective-permute-start | bytes 110600 | tf_op jit(solution)/shard_map/ppermute | solution.py:289
  7.0 0.2 collective-permute-start.3
  7.3 2.9 %shard_map.101 = (f32[64,512]{1,0:T(8,128)S(1)}, bf16[528,128]{1,0:T(8,128)(2,1)S(1)}, bf16[512,1024]{1,0:T(8,128)(2,1)S(1)}, s32[2,128]{1,0:T(2,128)S(1)}, bf16[8,512,512]{2,1,0:T(8,128)(2,1)S(1)}) custom-call(bf16[64,1024]{1,0:T(8,128)(2,1)S(1)} %get-tuple-element.19.x, bf16[2,1024,512]{2,1,0:T(8,128)(2,1)} %weights.3, bf16[512,1024]{1,0:T(8,128)(2,1)} %out_source.1, ...), custom_call_target="tpu_custom_call" | custom-call | tf_op jit(solution)/shard_map/pallas_call | solution.py:349
  10.2 0.0 collective-permute-done.1.rest_0_
  10.2 1.3 %collective-permute-done.2.rest_1_ = bf16[144,128]{1,0:T(8,128)(2,1)S(1)} collective-permute-done((bf16[144,128]{1,0:T(8,128)(2,1)S(1)}, bf16[144,128]{1,0:T(8,128)(2,1)S(1)}, u32[]{:S(2)}, u32[]{:S(2)}) %collective-permute-start.2) | collective-permute-done | bytes 36896 | tf_op jit(solution)/shard_map/ppermute | solution.py:289
  11.5 0.0 collective-permute-done.3.rest_2_
  11.5 0.0 copy-done
  11.5 0.0 copy-done.1
  11.5 1.1 %shard_map.102 = (bf16[144,128]{1,0:T(8,128)(2,1)S(1)}, bf16[144,128]{1,0:T(8,128)(2,1)S(1)}, bf16[144,128]{1,0:T(8,128)(2,1)S(1)}) custom-call(f32[4,512]{1,0:T(4,128)S(1)} %copy-done.1, bf16[8,512,512]{2,1,0:T(8,128)(2,1)S(1)} %copy-done, bf16[8,512,512]{2,1,0:T(8,128)(2,1)S(1)} %get-tuple-element.25.values, ...), custom_call_target="tpu_custom_call" | custom-call | tf_op jit(solution)/shard_map/pallas_call | solution.py:370
  12.6 2.1 %collective-permute-start.4 = (bf16[144,128]{1,0:T(8,128)(2,1)S(1)}, bf16[144,128]{1,0:T(8,128)(2,1)S(1)}, u32[]{:S(2)}, u32[]{:S(2)}) collective-permute-start(bf16[144,128]{1,0:T(8,128)(2,1)S(1)} %get-tuple-element.29), channel_id=1, source_target_pairs={{0,12},{4,8},{8,4},{12,0},{1,13},{5,9},{9,5},{13,1},{2,14},{6,10},... | collective-permute-start | bytes 110600 | tf_op jit(solution)/shard_map/ppermute | solution.py:289
  14.7 0.0 collective-permute-start.5
  14.7 2.4 %collective-permute-start.6 = (bf16[144,128]{1,0:T(8,128)(2,1)S(1)}, bf16[144,128]{1,0:T(8,128)(2,1)S(1)}, u32[]{:S(2)}, u32[]{:S(2)}) collective-permute-start(bf16[144,128]{1,0:T(8,128)(2,1)S(1)} %get-tuple-element.31), channel_id=1, source_target_pairs={{0,4},{4,0},{8,12},{12,8},{1,5},{5,1},{9,13},{13,9},{2,6},{6,2},{1... | collective-permute-start | bytes 110600 | tf_op jit(solution)/shard_map/ppermute | solution.py:289
  17.0 1.5 %collective-permute-start = (bf16[528,128]{1,0:T(8,128)(2,1)S(1)}, bf16[528,128]{1,0:T(8,128)(2,1)S(1)}, u32[]{:S(2)}, u32[]{:S(2)}) collective-permute-start(bf16[528,128]{1,0:T(8,128)(2,1)S(1)} %get-tuple-element.21.rest_0_), channel_id=1, source_target_pairs={{0,2},{2,0},{1,3},{3,1},{4,6},{6,4},{5,7},{7,5},{8,10},{10,8},{9,1... | collective-permute-start | bytes 405512 | tf_op jit(solution)/shard_map/ppermute | solution.py:289
  18.5 0.7 %shard_map.103.rest_3_ = bf16[144,128]{1,0:T(8,128)(2,1)S(1)} custom-call(f32[4,512]{1,0:T(4,128)S(1)} %copy-done.1, bf16[8,512,512]{2,1,0:T(8,128)(2,1)S(1)} %copy-done, bf16[8,512,512]{2,1,0:T(8,128)(2,1)S(1)} %get-tuple-element.25.values, bf16[144,128]{1,0:T(8,128)(2,1)S(1)} %get-tuple-element.32.rest_0_), custom_call_target="tpu_custom_call" | custom-call | tf_op jit(solution)/shard_map/pallas_call | solution.py:370
  19.2 0.0 collective-permute-done.4.rest_0_
  19.2 0.4 %collective-permute-done.5.rest_1_ = bf16[144,128]{1,0:T(8,128)(2,1)S(1)} collective-permute-done((bf16[144,128]{1,0:T(8,128)(2,1)S(1)}, bf16[144,128]{1,0:T(8,128)(2,1)S(1)}, u32[]{:S(2)}, u32[]{:S(2)}) %collective-permute-start.5) | collective-permute-done | bytes 36896 | tf_op jit(solution)/shard_map/ppermute | solution.py:289
  19.6 0.0 collective-permute-done.6.rest_2_
  19.6 0.3 %shard_map.105 = bf16[528,128]{1,0:T(8,128)(2,1)S(1)} custom-call(s32[2,128]{1,0:T(2,128)S(1)} %get-tuple-element.22.notes, f32[64,512]{1,0:T(8,128)S(1)} %get-tuple-element.23.gate, bf16[512,1024]{1,0:T(8,128)(2,1)S(1)} %get-tuple-element.24.out_weight, bf16[144,128]{1,0:T(8,128)(2,1)S(1)} %collective-permute-done.4.rest_0_, ...), custom_call_target="tpu_custom_call" | custom-call | tf_op jit(solution)/shard_map/pallas_call | solution.py:384
  19.9 1.6 %collective-permute-start.7 = (bf16[528,128]{1,0:T(8,128)(2,1)S(1)}, bf16[528,128]{1,0:T(8,128)(2,1)S(1)}, u32[]{:S(2)}, u32[]{:S(2)}) collective-permute-start(bf16[528,128]{1,0:T(8,128)(2,1)S(1)} %shard_map.105), channel_id=1, source_target_pairs={{0,2},{2,0},{1,3},{3,1},{4,6},{6,4},{5,7},{7,5},{8,10},{10,8},{9,1... | collective-permute-start | bytes 405512 | tf_op jit(solution)/shard_map/ppermute | solution.py:289
  21.5 0.3 %shard_map.104.rest_2_ = f32[528,128]{1,0:T(8,128)S(1)} custom-call(s32[2,128]{1,0:T(2,128)S(1)} %get-tuple-element.22.notes, f32[64,512]{1,0:T(8,128)S(1)} %get-tuple-element.23.gate, bf16[512,1024]{1,0:T(8,128)(2,1)S(1)} %get-tuple-element.24.out_weight, bf16[144,128]{1,0:T(8,128)(2,1)S(1)} %collective-permute-done.4.rest_0_, ...), custom_call_target="tpu_custom_call" | custom-call | tf_op jit(solution)/shard_map/pallas_call | solution.py:384
  21.8 1.3 %collective-permute-done.rest_1_ = bf16[528,128]{1,0:T(8,128)(2,1)S(1)} collective-permute-done((bf16[528,128]{1,0:T(8,128)(2,1)S(1)}, bf16[528,128]{1,0:T(8,128)(2,1)S(1)}, u32[]{:S(2)}, u32[]{:S(2)}) %collective-permute-start) | collective-permute-done | bytes 135200 | tf_op jit(solution)/shard_map/ppermute | solution.py:289
  23.1 1.9 %collective-permute-done.7.rest_3_ = bf16[528,128]{1,0:T(8,128)(2,1)S(1)} collective-permute-done((bf16[528,128]{1,0:T(8,128)(2,1)S(1)}, bf16[528,128]{1,0:T(8,128)(2,1)S(1)}, u32[]{:S(2)}, u32[]{:S(2)}) %collective-permute-start.7) | collective-permute-done | bytes 135200 | tf_op jit(solution)/shard_map/ppermute | solution.py:289
  25.0 1.0 %shard_map.106 = f32[2,128]{1,0:T(2,128)} custom-call(s32[2,128]{1,0:T(2,128)S(1)} %get-tuple-element.20.counts, bf16[64,1024]{1,0:T(8,128)(2,1)S(1)} %get-tuple-element.19.x, bf16[528,128]{1,0:T(8,128)(2,1)S(1)} %get-tuple-element.21.rest_0_, bf16[528,128]{1,0:T(8,128)(2,1)S(1)} %collective-permute-done.rest_1_, f32[528,128]{1,0:T(8,128)S(1)} %shard_map.104.rest_2_, ...), custom_call_target="tpu_custom_call" | custom-call | tf_op jit(solution)/shard_map/pallas_call | solution.py:393
Async XLA Ops:
  1.6 9.9 %copy-start = (bf16[8,512,512]{2,1,0:T(8,128)(2,1)S(1)}, bf16[8,512,512]{2,1,0:T(8,128)(2,1)}, u32[]{:S(2)}) copy-start(bf16[8,512,512]{2,1,0:T(8,128)(2,1)} %keys.3) | copy-start | bytes 12582916
  1.6 9.9 %copy-start.1 = (f32[4,512]{1,0:T(4,128)S(1)}, f32[4,512]{1,0:T(4,128)}, u32[]{:S(2)}) copy-start(f32[4,512]{1,0:T(4,128)} %bias.3) | copy-start | bytes 24580
  1.6 8.6 %collective-permute-start.1 = (bf16[144,128]{1,0:T(8,128)(2,1)S(1)}, bf16[144,128]{1,0:T(8,128)(2,1)S(1)}, u32[]{:S(2)}, u32[]{:S(2)}) collective-permute-start(bf16[144,128]{1,0:T(8,128)(2,1)S(1)} %get-tuple-element.26), channel_id=1, source_target_pairs={{0,8},{4,12},{8,0},{12,4},{1,9},{5,13},{9,1},{13,5},{2,10},{6,14},... | collective-permute-start | bytes 110600 | tf_op jit(solution)/shard_map/ppermute | solution.py:289
  5.7 5.8 %collective-permute-start.2 = (bf16[144,128]{1,0:T(8,128)(2,1)S(1)}, bf16[144,128]{1,0:T(8,128)(2,1)S(1)}, u32[]{:S(2)}, u32[]{:S(2)}) collective-permute-start(bf16[144,128]{1,0:T(8,128)(2,1)S(1)} %get-tuple-element.27), channel_id=1, source_target_pairs={{0,12},{4,8},{8,4},{12,0},{1,13},{5,9},{9,5},{13,1},{2,14},{6,10},... | collective-permute-start | bytes 110600 | tf_op jit(solution)/shard_map/ppermute | solution.py:289
  7.0 4.4 %collective-permute-start.3 = (bf16[144,128]{1,0:T(8,128)(2,1)S(1)}, bf16[144,128]{1,0:T(8,128)(2,1)S(1)}, u32[]{:S(2)}, u32[]{:S(2)}) collective-permute-start(bf16[144,128]{1,0:T(8,128)(2,1)S(1)} %get-tuple-element.28), channel_id=1, source_target_pairs={{0,4},{4,0},{8,12},{12,8},{1,5},{5,1},{9,13},{13,9},{2,6},{6,2},{1... | collective-permute-start | bytes 110600 | tf_op jit(solution)/shard_map/ppermute | solution.py:289
  12.6 6.6 %collective-permute-start.4 = (bf16[144,128]{1,0:T(8,128)(2,1)S(1)}, bf16[144,128]{1,0:T(8,128)(2,1)S(1)}, u32[]{:S(2)}, u32[]{:S(2)}) collective-permute-start(bf16[144,128]{1,0:T(8,128)(2,1)S(1)} %get-tuple-element.29), channel_id=1, source_target_pairs={{0,12},{4,8},{8,4},{12,0},{1,13},{5,9},{9,5},{13,1},{2,14},{6,10},... | collective-permute-start | bytes 110600 | tf_op jit(solution)/shard_map/ppermute | solution.py:289
  14.7 4.9 %collective-permute-start.5 = (bf16[144,128]{1,0:T(8,128)(2,1)S(1)}, bf16[144,128]{1,0:T(8,128)(2,1)S(1)}, u32[]{:S(2)}, u32[]{:S(2)}) collective-permute-start(bf16[144,128]{1,0:T(8,128)(2,1)S(1)} %get-tuple-element.30), channel_id=1, source_target_pairs={{0,8},{4,12},{8,0},{12,4},{1,9},{5,13},{9,1},{13,5},{2,10},{6,14},... | collective-permute-start | bytes 110600 | tf_op jit(solution)/shard_map/ppermute | solution.py:289
  14.7 4.9 %collective-permute-start.6 = (bf16[144,128]{1,0:T(8,128)(2,1)S(1)}, bf16[144,128]{1,0:T(8,128)(2,1)S(1)}, u32[]{:S(2)}, u32[]{:S(2)}) collective-permute-start(bf16[144,128]{1,0:T(8,128)(2,1)S(1)} %get-tuple-element.31), channel_id=1, source_target_pairs={{0,4},{4,0},{8,12},{12,8},{1,5},{5,1},{9,13},{13,9},{2,6},{6,2},{1... | collective-permute-start | bytes 110600 | tf_op jit(solution)/shard_map/ppermute | solution.py:289
  17.0 6.1 %collective-permute-start = (bf16[528,128]{1,0:T(8,128)(2,1)S(1)}, bf16[528,128]{1,0:T(8,128)(2,1)S(1)}, u32[]{:S(2)}, u32[]{:S(2)}) collective-permute-start(bf16[528,128]{1,0:T(8,128)(2,1)S(1)} %get-tuple-element.21.rest_0_), channel_id=1, source_target_pairs={{0,2},{2,0},{1,3},{3,1},{4,6},{6,4},{5,7},{7,5},{8,10},{10,8},{9,1... | collective-permute-start | bytes 405512 | tf_op jit(solution)/shard_map/ppermute | solution.py:289
  19.9 5.1 %collective-permute-start.7 = (bf16[528,128]{1,0:T(8,128)(2,1)S(1)}, bf16[528,128]{1,0:T(8,128)(2,1)S(1)}, u32[]{:S(2)}, u32[]{:S(2)}) collective-permute-start(bf16[528,128]{1,0:T(8,128)(2,1)S(1)} %shard_map.105), channel_id=1, source_target_pairs={{0,2},{2,0},{1,3},{3,1},{4,6},{6,4},{5,7},{7,5},{8,10},{10,8},{9,1... | collective-permute-start | bytes 405512 | tf_op jit(solution)/shard_map/ppermute | solution.py:289
